TPU v7x, 32 devices: a whole 2x2x4 slice. The times are simulated.
32 devices in a mesh: rep: 4 (over x, core), shard: 4 (over z), tp: 2 (over y).
Axes of the slice: x: 2, y: 2, z: 4, core: 2. Of those that a mesh axis runs over, the one named last changes fastest.
Arguments:
- expert_change: float32 [4, 4, 768, 3072], P('rep', None, 'shard', 'tp'), may hold values from -6 to 6
- table_change: float32 [4, 768, 16384], P('rep', 'shard', 'tp'), may hold values from -6 to 6
- expert_master: float32 [4, 3072, 768], P(None, 'shard'), may hold values from -6 to 6
- expert_moment: float32 [4, 3072, 768], P(None, 'shard'), may hold values from -6 to 6
- table_master: float32 [16384, 768], P('shard'), may hold values from -6 to 6
- table_moment: float32 [16384, 768], P('shard'), may hold values from -6 to 6
Outputs:
- expert_weights: float32 [4, 3072, 768], P(None, 'shard')
- expert_velocity: float32 [4, 3072, 768], P(None, 'shard')
- expert_copies: bfloat16 [4, 768, 3072], P(None, 'shard', 'tp')
- table_weights: float32 [16384, 768], P('shard')
- table_velocity: float32 [16384, 768], P('shard')
- table_copies: bfloat16 [768, 16384], P('shard', 'tp')
All inputs are finite; a program needn't handle non-finite values.
Results may differ from a plain program's by a relative error of at most 0.001.
Values may be sent and summed in bfloat16 or wider, within the bound.
No kernel may reach another device: no remote copies, remote signals or barrier semaphores. Data moves between devices by JAX's collectives and lax.ppermute only.
A program may use at most 256 MiB of HBM per device.

v0:
```python
import jax
import jax.numpy as jnp
from jax import lax
from jax.sharding import PartitionSpec as P

momentum_coef = 0.9
outer_rate = 0.7


def local(expert_change, table_change, expert_master, expert_moment, table_master, table_moment):
    groups = lax.axis_size("rep")
    tensor = lax.axis_size("tp")
    experts_part = expert_change[0]
    table_part = table_change[0][None]
    summed = lax.psum((experts_part, table_part), "rep")
    halves = (
        lax.all_gather(summed[0], "tp", axis=2, tiled=True),
        lax.all_gather(summed[1], "tp", axis=2, tiled=True),
    )
    regrouped = (
        lax.all_to_all(halves[0], "shard", split_axis=2, concat_axis=1, tiled=True),
        lax.all_to_all(halves[1], "shard", split_axis=2, concat_axis=1, tiled=True),
    )
    expert_sum = jnp.transpose(regrouped[0], (0, 2, 1))
    table_sum = jnp.transpose(regrouped[1][0])
    expert_mean = expert_sum / groups
    table_mean = table_sum / groups
    expert_velocity = momentum_coef * expert_moment + expert_mean
    expert_weights = expert_master - outer_rate * (expert_mean + momentum_coef * expert_velocity)
    table_velocity = momentum_coef * table_moment + table_mean
    table_weights = table_master - outer_rate * (table_mean + momentum_coef * table_velocity)
    expert_low = jnp.transpose(expert_weights, (0, 2, 1)).astype(jnp.bfloat16)
    table_low = jnp.transpose(table_weights).astype(jnp.bfloat16)[None]
    returned = (
        lax.all_to_all(expert_low, "shard", split_axis=1, concat_axis=2, tiled=True),
        lax.all_to_all(table_low, "shard", split_axis=1, concat_axis=2, tiled=True),
    )
    tensor_index = lax.axis_index("tp")
    expert_width = returned[0].shape[2] // tensor
    table_width = returned[1].shape[2] // tensor
    expert_copies = lax.dynamic_slice_in_dim(
        returned[0], tensor_index * expert_width, expert_width, 2
    )
    table_copies = lax.dynamic_slice_in_dim(
        returned[1][0], tensor_index * table_width, table_width, 1
    )
    return (
        expert_weights,
        expert_velocity,
        expert_copies,
        table_weights,
        table_velocity,
        table_copies,
    )


def solution(mesh):
    in_specs = (
        P("rep", None, "shard", "tp"),
        P("rep", "shard", "tp"),
        P(None, "shard", None),
        P(None, "shard", None),
        P("shard", None),
        P("shard", None),
    )
    out_specs = (
        P(None, "shard", None),
        P(None, "shard", None),
        P(None, "shard", "tp"),
        P("shard", None),
        P("shard", None),
        P("shard", "tp"),
    )
    return jax.shard_map(local, mesh=mesh, in_specs=in_specs, out_specs=out_specs, check_vma=False)
```

profile of v0, /device:TPU:0, one launch (start us, length us, event | category | flops | bytes accessed | tf_op | source)
XLA Modules:
  0.0 1391.5 jit_solution(4278130303618808561)
XLA Ops:
  7.9 201.0 %all-reduce.3.cloned.1.call-done = (f32[4,192,1536]{2,1,0:T(8,128)}, f32[1,192,8192]{2,1,0:T(8,128)}) async-done(((f32[4,192,1536]{2,1,0:T(8,128)}, f32[1,192,8192]{2,1,0:T(8,128)}), (f32[4,192,1536]{2,1,0:T(8,128)}, f32[1,192,8192]{2,1,0:T(8,128)})) %all-reduce.3.cloned.1.call-update) | async-done | bytes 11010064 | tf_op jit(solution)/shard_map/psum | solution.py:15
  209.0 119.7 %all-gather.3.cloned.1.call-done = f32[4,192,3072]{2,1,0:T(8,128)} async-done(((f32[4,192,1536]{2,1,0:T(8,128)}), f32[4,192,3072]{2,1,0:T(8,128)}) %all-gather.3.cloned.1.call-update) | async-done | bytes 9437200 | tf_op jit(solution)/shard_map/all_gather | solution.py:17
  328.7 13.2 copy.74
  348.9 154.6 %all-gather.5.cloned.1.call-done = f32[1,192,16384]{2,1,0:T(8,128)} async-done(((f32[1,192,8192]{2,1,0:T(8,128)}), f32[1,192,16384]{2,1,0:T(8,128)}) %all-gather.5.cloned.1.call-update) | async-done | bytes 12582928 | tf_op jit(solution)/shard_map/all_gather | solution.py:18
  503.6 34.6 %copy.82 = f32[1,192,16384]{1,0,2:T(1,128)} copy(f32[1,192,16384]{2,1,0:T(8,128)} %all-gather.5.cloned.1.call-done) | data formatting | bytes 25165824 | tf_op jit(solution)/shard_map/all_gather | solution.py:18
  538.2 83.2 %all-to-all-done = f32[4,192,3072]{1,0,2:T(4,128)} async-done(((f32[4,192,3072]{1,0,2:T(4,128)}), f32[4,192,3072]{1,0,2:T(4,128)}, u32[]{:S(2)}, u32[]{:S(2)}) %all-to-all-start) | async-done | bytes 9437216 | tf_op jit(solution)/shard_map/all_to_all | solution.py:21
  621.5 7.0 all-to-all-start.2
  628.4 9.6 copy.77
  638.0 9.6 copy.78
  647.6 13.4 copy.75
  661.1 9.1 broadcast_multiply_fusion.1
  670.2 12.4 div.30
  688.0 15.0 %convert_bitcast_fusion.1 = (bf16[4,768,768]{2,1,0:T(8,128)(2,1)S(1)}, f32[4,768,768]{1,2,0:T(8,128)}, f32[4,768,768]{1,2,0:T(8,128)}) fusion(f32[4,768,768]{1,2,0:T(8,128)} %copy.78, f32[4,768,768]{1,2,0:T(8,128)} %copy.77, f32[4,4,192,768]{3,2,1,0:T(8,128)S(1)} %copy.76), kind=kLoop, calls=%fused_computation.10 | loop fusion | flops 16515072 | bytes 51904512 | tf_op jit(solution)/shard_map/convert_element_type | solution.py:32
  708.7 282.1 %all-to-all-done.2 = f32[1,192,16384]{1,0,2:T(1,128)} async-done(((f32[1,192,16384]{1,0,2:T(1,128)}), f32[1,192,16384]{1,0,2:T(1,128)}, u32[]{:S(2)}, u32[]{:S(2)}) %all-to-all-start.2) | async-done | bytes 12582944 | tf_op jit(solution)/shard_map/all_to_all | solution.py:22
  996.3 12.6 copy.85
  1008.9 12.6 copy.86
  1021.5 34.1 %copy.83 = f32[1,192,16384]{2,1,0:T(8,128)} copy(f32[1,192,16384]{1,0,2:T(1,128)} %all-to-all-done.2) | data formatting | bytes 25165824 | tf_op jit(solution)/shard_map/all_to_all | solution.py:22
  1055.6 10.4 broadcast_multiply_fusion
  1066.1 15.6 %div.36 = f32[1,192,4,4096]{3,2,1,0:T(4,128)} reshape(f32[1,192,16384]{2,1,0:T(8,128)} %broadcast_multiply_fusion) | data formatting | bytes 25165824 | tf_op jit(solution)/shard_map/div | solution.py:27
  1081.7 16.3 %copy.84 = f32[1,4,192,4096]{3,2,1,0:T(8,128)} copy(f32[1,4,192,4096]{3,1,2,0:T(4,128)} %bitcast.48) | data formatting | bytes 25165824 | tf_op jit(solution)/shard_map/div | solution.py:27
  1098.0 23.3 %convert_bitcast_fusion = (bf16[1,768,4096]{2,1,0:T(8,128)(2,1)S(1)}, f32[4096,768]{0,1:T(8,128)}, f32[4096,768]{0,1:T(8,128)}) fusion(f32[4096,768]{0,1:T(8,128)} %copy.86, f32[4096,768]{0,1:T(8,128)} %copy.85, f32[1,4,192,4096]{3,2,1,0:T(8,128)} %copy.84), kind=kLoop, calls=%fused_computation.8 | loop fusion | flops 22020096 | bytes 69206016 | tf_op jit(solution)/shard_map/broadcast_in_dim | solution.py:33
  1121.4 32.8 %copy.97 = bf16[1,768,4096]{2,0,1:T(2,128)(2,1)} copy(bf16[1,768,4096]{2,1,0:T(8,128)(2,1)S(1)} %get-tuple-element.38) | data formatting | bytes 12582912 | tf_op jit(solution)/shard_map/broadcast_in_dim | solution.py:33
  1154.6 40.1 %reduce = bf16[768,4096]{1,0:T(8,128)(2,1)} reduce(bf16[768,1,4096]{2,1,0:T(2,128)(2,1)} %bitcast.50, bf16[]{:T(256)} %broadcast.36), dimensions={1}, to_apply=%bitcast.47.reduce_sub_computation | reduce | bytes 12582914
  1194.7 8.1 reshape.22
  1208.1 9.6 copy.89
  1217.7 9.6 copy.90
  1232.4 12.6 copy.91
  1245.0 12.6 copy.92
  1257.6 88.1 %all-to-all-done.3 = bf16[4,2,393216]{2,1,0:T(2,128)(2,1)} async-done(((bf16[4,2,393216]{2,1,0:T(2,128)(2,1)}), bf16[4,2,393216]{2,1,0:T(2,128)(2,1)}, u32[]{:S(2)}, u32[]{:S(2)}) %all-to-all-start.3) | async-done | bytes 6291488 | tf_op jit(solution)/shard_map/all_to_all | solution.py:36
  1345.7 10.2 reshape.23
  1355.9 14.3 %copy.93 = bf16[1,768,4096]{2,1,0:T(8,128)(2,1)} copy(bf16[1,768,4096]{2,0,1:T(2,128)(2,1)} %bitcast.49) | data formatting | bytes 12582912
  1370.2 7.9 copy.88
  (18 shorter events, 41.7 us)
Async XLA Ops:
  7.2 201.8 %all-reduce.3.cloned.1.call-start = ((), (), s32[]{:S(2)}) async-start(), calls=%async_computation.6 | async-start | bytes 22020096 | tf_op jit(solution)/shard_map/psum | solution.py:15
  7.9 320.8 %all-gather.3.cloned.1.call-start = ((), (), s32[]{:S(2)}) async-start(), calls=%async_computation.4 | async-start | bytes 14155776 | tf_op jit(solution)/shard_map/all_gather | solution.py:17
  341.9 279.5 %all-to-all-start = ((f32[4,192,3072]{1,0,2:T(4,128)}), f32[4,192,3072]{1,0,2:T(4,128)}, u32[]{:S(2)}, u32[]{:S(2)}) async-start(f32[4,192,3072]{1,0,2:T(4,128)} %copy.74), calls=%async_computation | async-start | bytes 25165824 | tf_op jit(solution)/shard_map/all_to_all | solution.py:21
  348.2 155.4 %all-gather.5.cloned.1.call-start = ((), (), s32[]{:S(2)}) async-start(), calls=%async_computation.5 | async-start | bytes 18874368 | tf_op jit(solution)/shard_map/all_gather | solution.py:18
  621.5 369.4 %all-to-all-start.2 = ((f32[1,192,16384]{1,0,2:T(1,128)}), f32[1,192,16384]{1,0,2:T(1,128)}, u32[]{:S(2)}, u32[]{:S(2)}) async-start(f32[1,192,16384]{1,0,2:T(1,128)} %copy.82), calls=%async_computation.2 | async-start | bytes 33554432 | tf_op jit(solution)/shard_map/all_to_all | solution.py:22
  990.8 212.0 %all-to-all-start.1 = ((bf16[4,768,768]{2,0,1:T(4,128)(2,1)}), bf16[4,768,768]{2,0,1:T(4,128)(2,1)}, u32[]{:S(2)}, u32[]{:S(2)}) async-start(bf16[4,768,768]{2,0,1:T(4,128)(2,1)} %copy.79), calls=%async_computation.1 | async-start | bytes 9437184 | tf_op jit(solution)/shard_map/all_to_all | solution.py:35
  1202.8 142.9 %all-to-all-start.3 = ((bf16[4,2,393216]{2,1,0:T(2,128)(2,1)}), bf16[4,2,393216]{2,1,0:T(2,128)(2,1)}, u32[]{:S(2)}, u32[]{:S(2)}) async-start(bf16[4,2,393216]{2,1,0:T(2,128)(2,1)} %reshape.22), calls=%async_computation.3 | async-start | bytes 12582912 | tf_op jit(solution)/shard_map/all_to_all | solution.py:36
Sparse Core Ops, SparseCore 0:
  10.6 198.2 all-reduce.2
  210.5 118.1 all-gather.2
  350.6 152.9 all-gather.4
where the time goes:
time: 1400 us; the launch traced here: 1390 us
  waiting for transfers between devices  930 us (66%)
  local copies, waits for them, and re-layouts  325 us (23%)
  other arithmetic  97.9 us (7%)
  starting transfers between devices  24.1 us (2%)
  between operations  14.3 us (1%)
    all_to_all x1, waiting for transfers between devices, local(): lax.all_to_all(halves[1], 'shard', split_axis=2, concat_axis=1, tiled=True)  282 us
    psum x1, waiting for transfers between devices, local(): summed = lax.psum((experts_part, table_part), 'rep')  201 us
    all_gather x1, waiting for transfers between devices, local(): lax.all_gather(summed[1], 'tp', axis=2, tiled=True)  155 us
    unnamed x13, local copies, waits for them, and re-layouts  126 us
    all_gather x1, waiting for transfers between devices, local(): lax.all_gather(summed[0], 'tp', axis=2, tiled=True)  120 us
    all_to_all x1, waiting for transfers between devices, local(): lax.all_to_all(table_low, 'shard', split_axis=1, concat_axis=2, tiled=True)  88.1 us
    all_to_all x1, waiting for transfers between devices, local(): lax.all_to_all(halves[0], 'shard', split_axis=2, concat_axis=1, tiled=True)  83.2 us
    unnamed x1, other arithmetic  40.1 us
  transfers between devices with their start and end apart: 7, of which 6 were waited for; matrix products, arithmetic and copies ran while one was open for 27% of the time, Pallas kernels for 0%

commit v1 on v0

v1 whole, which is shorter than its diff:
```python
import jax
import jax.numpy as jnp
from jax import lax
from jax.sharding import PartitionSpec as P

momentum_coef = 0.9
outer_rate = 0.7
axes = ("rep", "shard", "tp")
scale = 2048.0


def pairs(mesh_sizes, move):
    groups, shards, tensor = mesh_sizes
    result = []
    for r in range(groups):
        for z in range(shards):
            for y in range(tensor):
                r2, z2, y2 = move(r, z, y)
                result.append(((r * shards + z) * tensor + y, (r2 * shards + z2) * tensor + y2))
    return result


def local(expert_change, table_change, expert_master, expert_moment, table_master, table_moment):
    groups, shards, tensor = sizes = tuple(lax.axis_size(a) for a in axes)
    r, z, y = (lax.axis_index(a) for a in axes)
    core, x = r % 2, r // 2
    half_shards = shards // tensor
    mine = (z % half_shards) * tensor + y

    def send(value, move):
        return lax.ppermute(value, axes, pairs(sizes, move))

    def over_core(value):
        return send(value, lambda r, z, y: (r ^ 1, z, y))

    def over_x(value):
        return send(value, lambda r, z, y: (r ^ 2, z, y))

    def over_y(value):
        return send(value, lambda r, z, y: (r, z, y ^ 1))

    def scatter_to(k):
        def move(r, z, y):
            p = (z + k) % shards
            return r, y * half_shards + p // tensor, p % tensor

        return move

    def gather_from(k):
        def move(r, z, y):
            p = (z % half_shards) * tensor + y
            return r, (p - k) % shards, z // half_shards

        return move

    def piece(value, p, width):
        return lax.dynamic_slice_in_dim(value, p * width, width, value.ndim - 1)

    def reduce_part(own, other):
        half = own + over_core(other)
        sent = lax.dynamic_index_in_dim(half, 1 - x, 0, False)
        kept = lax.dynamic_index_in_dim(half, x, 0, False)
        received = over_x((sent * scale).astype(jnp.float16))
        return (kept * scale + received.astype(jnp.float32)).astype(jnp.float16)

    def scatter_part(total):
        rows, width = total.shape[0], total.shape[1] // shards
        result = jnp.zeros((shards, rows, width), total.dtype)
        for k in range(shards):
            got = send(piece(total, (z + k) % shards, width), scatter_to(k))
            result = lax.dynamic_update_index_in_dim(result, got, (mine - k) % shards, 0)
        return result

    def copies_part(low):
        rows, width = low.shape[1:]
        result = jnp.zeros((rows, shards * width), low.dtype)
        for k in range(shards):
            got = send(lax.dynamic_index_in_dim(low, (mine - k) % shards, 0, False), gather_from(k))
            result = lax.dynamic_update_slice_in_dim(result, got, ((z + k) % shards) * width, 1)
        return result

    def gather_part(own):
        result = jnp.zeros((2, 2, 2) + own.shape, own.dtype)
        near = over_x(own)
        pieces = {(0, 0): own, (1, 0): near, (0, 1): over_y(own), (1, 1): over_y(near)}
        for (dx, dy), value in pieces.items():
            for dc, part in ((0, value), (1, over_core(value))):
                place = (core ^ dc, x ^ dx, y ^ dy, 0, 0)
                result = lax.dynamic_update_slice(result, part[None, None, None], place)
        return result

    def quarter(a, width):
        return lax.dynamic_slice(a, (core, x, y, 0, 0), (1, 1, 1) + a.shape[3:])[0, 0, 0]

    def step(received, master, moment):
        rows, width = received.shape[1:]
        model = shards * rows
        summed = jnp.transpose(received, (2, 0, 1)).reshape(width, model)
        gathered = gather_part(summed)
        base = quarter(master, width) - outer_rate * momentum_coef * momentum_coef * quarter(moment, width)
        base = jnp.transpose(base).reshape(shards, rows, width)
        low = base - (outer_rate * (1 + momentum_coef) / (groups * scale)) * received.astype(jnp.float32)
        copies = copies_part(low.astype(jnp.bfloat16))
        mean = gathered.astype(jnp.float32) * (1 / (groups * scale))
        velocity = momentum_coef * moment + mean
        weights = master - outer_rate * (mean + momentum_coef * velocity)
        return weights, velocity, copies

    mats, rows, expert_columns = expert_change.shape[1:]
    change = expert_change[0].reshape(2, 2, rows, expert_columns)
    expert_total = reduce_part(
        lax.dynamic_index_in_dim(change, core, 0, False),
        lax.dynamic_index_in_dim(change, 1 - core, 0, False),
    )
    table = table_change[0]
    table_columns = table.shape[1]
    block = table_columns // half_shards
    width = block // 8

    def of_core(c):
        both = []
        for dx in range(2):
            both.append(
                jnp.concatenate(
                    [
                        lax.dynamic_slice_in_dim(table, a * block + c * 4 * width + dx * 2 * width, 2 * width, 1)
                        for a in range(half_shards)
                    ],
                    1,
                )
            )
        return jnp.stack(both)

    table_total = reduce_part(of_core(core), of_core(1 - core))
    expert_received = scatter_part(expert_total)
    table_received = scatter_part(table_total)

    model = expert_master.shape[-1]
    expert_shape = (2, 2, tensor, expert_master.shape[1] // tensor, model)
    table_shape = (2, 2, tensor, width, model)
    expert_weights, expert_velocity, expert_low = step(
        expert_received, expert_master.reshape(expert_shape), expert_moment.reshape(expert_shape)
    )
    table_weights, table_velocity, table_low = step(
        table_received, table_master.reshape(table_shape), table_moment.reshape(table_shape)
    )

    near = over_x(expert_low)
    result = jnp.zeros((2, 2) + expert_low.shape, expert_low.dtype)
    for dx, value in ((0, expert_low), (1, near)):
        for dc, part in ((0, value), (1, over_core(value))):
            result = lax.dynamic_update_slice(result, part[None, None], (core ^ dc, x ^ dx, 0, 0))
    expert_copies = result.reshape(mats, rows, expert_columns)
    near = over_x(table_low)
    table_copies = jnp.zeros((rows, table_columns), table_low.dtype)
    for dx, value in ((0, table_low), (1, near)):
        for dc, part in ((0, value), (1, over_core(value))):
            for a in range(half_shards):
                table_copies = lax.dynamic_update_slice(
                    table_copies,
                    part[:, a * 2 * width : (a + 1) * 2 * width],
                    (0, a * block + (core ^ dc) * 4 * width + (x ^ dx) * 2 * width),
                )
    return (
        expert_weights.reshape(expert_master.shape),
        expert_velocity.reshape(expert_master.shape),
        expert_copies,
        table_weights.reshape(table_master.shape),
        table_velocity.reshape(table_master.shape),
        table_copies,
    )


def solution(mesh):
    in_specs = (
        P("rep", None, "shard", "tp"),
        P("rep", "shard", "tp"),
        P(None, "shard", None),
        P(None, "shard", None),
        P("shard", None),
        P("shard", None),
    )
    out_specs = (
        P(None, "shard", None),
        P(None, "shard", None),
        P(None, "shard", "tp"),
        P("shard", None),
        P("shard", None),
        P("shard", "tp"),
    )
    return jax.shard_map(local, mesh=mesh, in_specs=in_specs, out_specs=out_specs, check_vma=False)
```

time: 1400 us -> 267 us (0.19)
  waiting for transfers between devices: 930 us -> 100 us
  local copies, waits for them, and re-layouts: 325 us -> 38.9 us
  starting transfers between devices: 24.1 us -> 77 us
  other arithmetic: 97.9 us -> 48.3 us
    all_to_all x4 -> x0, waiting for transfers between devices: 453 us -> none  [the longest x1 282 us: local(): lax.all_to_all(halves[1], 'shard', split_axis=2, concat_axis=1, tiled=True)]
    all_gather x2 -> x0, waiting for transfers between devices: 274 us -> none  [the longest x1 155 us: local(): lax.all_gather(summed[1], 'tp', axis=2, tiled=True)]
    psum x1 -> x0, waiting for transfers between devices: 201 us -> none  [local(): summed = lax.psum((experts_part, table_part), 'rep')]
    unnamed x13 -> x26, local copies, waits for them, and re-layouts: 126 us -> 2.74 us
    ppermute x0 -> x40, waiting for transfers between devices: none -> 100 us  [send(): return lax.ppermute(value, axes, pairs(sizes, move))]
    ppermute x0 -> x40, starting transfers between devices: none -> 77 us  [send(): return lax.ppermute(value, axes, pairs(sizes, move))]
    all_to_all x5 -> x0, local copies, waits for them, and re-layouts: 59 us -> none  [the longest x1 34.1 us: local(): lax.all_to_all(halves[1], 'shard', split_axis=2, concat_axis=1, tiled=True)]
    div x4 -> x0, local copies, waits for them, and re-layouts: 49.7 us -> none  [the longest x2 32 us: local(): table_mean = table_sum / groups]
  transfers between devices with their start and end apart: 7 -> 40, of which waited for: 6 -> 14; matrix products, arithmetic and copies ran while one was open for 27% -> 26% of each run, Pallas kernels for 0% -> 0%
where the time goes in v1:
time: 267 us; the launch traced here: 266 us
  waiting for transfers between devices  100 us (37%)
  starting transfers between devices  77 us (29%)
  other arithmetic  48.3 us (18%)
  local copies, waits for them, and re-layouts  38.9 us (15%)
    ppermute x40, waiting for transfers between devices, send(): return lax.ppermute(value, axes, pairs(sizes, move))  100 us
    ppermute x40, starting transfers between devices, send(): return lax.ppermute(value, axes, pairs(sizes, move))  77 us
    add x2, other arithmetic, step(): velocity = momentum_coef * moment + mean  29.5 us
    dynamic_update_slice x16, local copies, waits for them, and re-layouts, gather_part(): result = lax.dynamic_update_slice(result, part[None, None, None], place)  10.9 us
    transpose x2, other arithmetic, step(): base = jnp.transpose(base).reshape(shards, rows, width)  6.16 us
  transfers between devices with their start and end apart: 40, of which 14 were waited for; matrix products, arithmetic and copies ran while one was open for 26% of the time, Pallas kernels for 0%

profile of v1, /device:TPU:0, one launch (start us, length us, event | category | flops | bytes accessed | tf_op | source)
XLA Modules:
  0.0 265.9 jit_solution(7039152947578852774)
XLA Ops:
  3.0 4.6 %dynamic-slice_bitcast_fusion.8 = (f32[192,1024]{1,0:T(8,128)S(1)}, f32[192,1024]{1,0:T(8,128)S(1)}, f32[192,1024]{1,0:T(8,128)S(1)}, f32[192,1024]{1,0:T(8,128)...) fusion(f32[1,192,8192]{2,1,0:T(8,128)} %param.7, ...), kind=kLoop, calls=%fused_computation.39 | loop fusion | bytes 12582944 | tf_op jit(solution)/shard_map/dynamic_slice | solution.py:126
  7.8 2.0 pad_maximum_fusion
  9.9 2.8 %bitcast_add_fusion = f32[2,192,1536]{2,1,0:T(8,128)S(1)} fusion(f32[2,192,1536]{2,1,0:T(8,128)} %collective-permute-done, f32[2,2,192,1536]{3,2,1,0:T(8,128)} %bitcast.160, s32[]{:T(128)S(6)} %select_n.297), kind=kLoop, calls=%fused_computation.8 | loop fusion | flops 589824 | bytes 7077892 | tf_op jit(solution)/shard_map/add | solution.py:60
  13.6 2.9 %collective-permute-start.1 = (f16[192,1536]{1,0:T(8,128)(2,1)}, f16[192,1536]{1,0:T(8,128)(2,1)}, u32[]{:S(2)}, u32[]{:S(2)}) collective-permute-start(f16[192,1536]{1,0:T(8,128)(2,1)} %fusion.3), channel_id=1, source_target_pairs={{0,16},{1,17},{2,18},{3,19},{4,20},{5,21},{6,22},{7,23},{8,24},{9,... | collective-permute-start | bytes 1769480 | tf_op jit(solution)/shard_map/ppermute | solution.py:31
  16.5 3.4 %subtract_bitcast_fusion = f32[768,512]{0,1:T(8,128)} fusion(f32[2,2,2,512,768]{4,3,2,1,0:T(8,128)} %bitcast.140, s32[]{:T(128)S(6)} %select_n.297, s32[]{:T(128)S(6)} %select_n.300, s32[]{:T(128)S(6)} %select_n.319, f32[2,2,2,512,768]{4,3,2,1,0:T(8,128)} %bitcast.144), kind=kLoop, calls=%fused_computation.17 | loop fusion | flops 786432 | bytes 4718604 | tf_op jit(solution)/shard_map/transpose | solution.py:101
  19.9 2.0 maximum_bitcast_fusion
  21.9 8.5 %collective-permute-done.1 = f16[192,1536]{1,0:T(8,128)(2,1)} collective-permute-done((f16[192,1536]{1,0:T(8,128)(2,1)}, f16[192,1536]{1,0:T(8,128)(2,1)}, u32[]{:S(2)}, u32[]{:S(2)}) %collective-permute-start.1) | collective-permute-done | bytes 589856 | tf_op jit(solution)/shard_map/ppermute | solution.py:31
  35.7 2.8 %subtract_bitcast_fusion.1 = f32[768,384]{0,1:T(8,128)} fusion(f32[2,2,2,384,768]{4,3,2,1,0:T(8,128)} %bitcast.150, s32[]{:T(128)S(6)} %select_n.297, s32[]{:T(128)S(6)} %select_n.300, s32[]{:T(128)S(6)} %select_n.319, f32[2,2,2,384,768]{4,3,2,1,0:T(8,128)} %bitcast.152), kind=kLoop, calls=%fused_computation.22 | loop fusion | flops 589824 | bytes 3538956 | tf_op jit(solution)/shard_map/transpose | solution.py:101
  40.2 7.0 %collective-permute-start.3 = (f16[192,384]{1,0:T(8,128)(2,1)}, f16[192,384]{1,0:T(8,128)(2,1)S(1)}, u32[]{:S(2)}, u32[]{:S(2)}) collective-permute-start(f16[192,384]{1,0:T(8,128)(2,1)} %get-tuple-element.32), channel_id=1, source_target_pairs={{0,1},{1,5},{2,2},{3,6},{4,3},{5,7},{6,0},{7,4},{8,9},{9,13},{10,1... | collective-permute-start | bytes 442376 | tf_op jit(solution)/shard_map/ppermute | solution.py:31
  47.2 4.2 %collective-permute-start.5 = (f16[192,384]{1,0:T(8,128)(2,1)S(1)}, f16[192,384]{1,0:T(8,128)(2,1)S(1)}, u32[]{:S(2)}, u32[]{:S(2)}) collective-permute-start(f16[192,384]{1,0:T(8,128)(2,1)S(1)} %get-tuple-element.30), channel_id=1, source_target_pairs={{0,3},{1,7},{2,0},{3,4},{4,1},{5,5},{6,2},{7,6},{8,11},{9,15},{10,... | collective-permute-start | bytes 442376 | tf_op jit(solution)/shard_map/ppermute | solution.py:31
  52.5 11.4 %collective-permute-done.4 = f16[192,384]{1,0:T(8,128)(2,1)S(1)} collective-permute-done((f16[192,384]{1,0:T(8,128)(2,1)}, f16[192,384]{1,0:T(8,128)(2,1)S(1)}, u32[]{:S(2)}, u32[]{:S(2)}) %collective-permute-start.4) | collective-permute-done | bytes 147488 | tf_op jit(solution)/shard_map/ppermute | solution.py:31
  66.7 4.4 %collective-permute-start.9 = (f16[384,768]{1,0:T(8,128)(2,1)}, f16[384,768]{1,0:T(8,128)(2,1)}, u32[]{:S(2)}, u32[]{:S(2)}) collective-permute-start(f16[384,768]{1,0:T(8,128)(2,1)} %copy.26), channel_id=1, source_target_pairs={{0,1},{1,0},{2,3},{3,2},{4,5},{5,4},{6,7},{7,6},{8,9},{9,8},{10,11... | collective-permute-start | bytes 1769480 | tf_op jit(solution)/shard_map/ppermute | solution.py:31
  73.1 7.4 %collective-permute-start.14 = (bf16[192,384]{1,0:T(8,128)(2,1)S(1)}, bf16[192,384]{1,0:T(8,128)(2,1)S(1)}, u32[]{:S(2)}, u32[]{:S(2)}) collective-permute-start(bf16[192,384]{1,0:T(8,128)(2,1)S(1)} %get-tuple-element.28), channel_id=1, source_target_pairs={{0,6},{1,0},{2,2},{3,4},{4,7},{5,1},{6,3},{7,5},{8,14},{9,8},{10,1... | collective-permute-start | bytes 442376 | tf_op jit(solution)/shard_map/ppermute | solution.py:31
  80.5 2.6 maximum_add_fusion
  83.4 4.9 %collective-permute-done.14 = bf16[192,384]{1,0:T(8,128)(2,1)S(1)} collective-permute-done((bf16[192,384]{1,0:T(8,128)(2,1)S(1)}, bf16[192,384]{1,0:T(8,128)(2,1)S(1)}, u32[]{:S(2)}, u32[]{:S(2)}) %collective-permute-start.14) | collective-permute-done | bytes 147488 | tf_op jit(solution)/shard_map/ppermute | solution.py:31
  90.7 8.9 %collective-permute-done.16 = bf16[192,384]{1,0:T(8,128)(2,1)S(1)} collective-permute-done((bf16[192,384]{1,0:T(8,128)(2,1)S(1)}, bf16[192,384]{1,0:T(8,128)(2,1)S(1)}, u32[]{:S(2)}, u32[]{:S(2)}) %collective-permute-start.16) | collective-permute-done | bytes 147488 | tf_op jit(solution)/shard_map/ppermute | solution.py:31
  105.1 10.8 %collective-permute-done.18 = bf16[192,1536]{1,0:T(8,128)(2,1)} collective-permute-done((bf16[192,1536]{1,0:T(8,128)(2,1)S(1)}, bf16[192,1536]{1,0:T(8,128)(2,1)}, u32[]{:S(2)}, u32[]{:S(2)}) %collective-permute-start.18) | collective-permute-done | bytes 589856 | tf_op jit(solution)/shard_map/ppermute | solution.py:31
  116.0 16.2 %collective-permute-done.21 = f16[192,2048]{1,0:T(8,128)(2,1)S(1)} collective-permute-done((f16[192,2048]{1,0:T(8,128)(2,1)S(1)}, f16[192,2048]{1,0:T(8,128)(2,1)S(1)}, u32[]{:S(2)}, u32[]{:S(2)}) %collective-permute-start.21) | collective-permute-done | bytes 786464 | tf_op jit(solution)/shard_map/ppermute | solution.py:31
  134.6 6.8 %collective-permute-start.23 = (f16[192,512]{1,0:T(8,128)(2,1)S(1)}, f16[192,512]{1,0:T(8,128)(2,1)S(1)}, u32[]{:S(2)}, u32[]{:S(2)}) collective-permute-start(f16[192,512]{1,0:T(8,128)(2,1)S(1)} %get-tuple-element.24), channel_id=1, source_target_pairs={{0,1},{1,5},{2,2},{3,6},{4,3},{5,7},{6,0},{7,4},{8,9},{9,13},{10,1... | collective-permute-start | bytes 589832 | tf_op jit(solution)/shard_map/ppermute | solution.py:31
  141.6 4.9 %collective-permute-done.23 = f16[192,512]{1,0:T(8,128)(2,1)S(1)} collective-permute-done((f16[192,512]{1,0:T(8,128)(2,1)S(1)}, f16[192,512]{1,0:T(8,128)(2,1)S(1)}, u32[]{:S(2)}, u32[]{:S(2)}) %collective-permute-start.23) | collective-permute-done | bytes 196640 | tf_op jit(solution)/shard_map/ppermute | solution.py:31
  146.5 10.4 %collective-permute-done.24 = f16[192,512]{1,0:T(8,128)(2,1)S(1)} collective-permute-done((f16[192,512]{1,0:T(8,128)(2,1)S(1)}, f16[192,512]{1,0:T(8,128)(2,1)S(1)}, u32[]{:S(2)}, u32[]{:S(2)}) %collective-permute-start.24) | collective-permute-done | bytes 196640 | tf_op jit(solution)/shard_map/ppermute | solution.py:31
  156.9 5.3 %collective-permute-start.25 = (f16[192,512]{1,0:T(8,128)(2,1)S(1)}, f16[192,512]{1,0:T(8,128)(2,1)S(1)}, u32[]{:S(2)}, u32[]{:S(2)}) collective-permute-start(f16[192,512]{1,0:T(8,128)(2,1)S(1)} %get-tuple-element.22), channel_id=1, source_target_pairs={{0,3},{1,7},{2,0},{3,4},{4,1},{5,5},{6,2},{7,6},{8,11},{9,15},{10,... | collective-permute-start | bytes 589832 | tf_op jit(solution)/shard_map/ppermute | solution.py:31
  162.3 4.4 %collective-permute-done.25 = f16[192,512]{1,0:T(8,128)(2,1)S(1)} collective-permute-done((f16[192,512]{1,0:T(8,128)(2,1)S(1)}, f16[192,512]{1,0:T(8,128)(2,1)S(1)}, u32[]{:S(2)}, u32[]{:S(2)}) %collective-permute-start.25) | collective-permute-done | bytes 196640 | tf_op jit(solution)/shard_map/ppermute | solution.py:31
  175.6 9.9 %collective-permute-start.34 = (bf16[192,512]{1,0:T(8,128)(2,1)S(1)}, bf16[192,512]{1,0:T(8,128)(2,1)S(1)}, u32[]{:S(2)}, u32[]{:S(2)}) collective-permute-start(bf16[192,512]{1,0:T(8,128)(2,1)S(1)} %get-tuple-element.20), channel_id=1, source_target_pairs={{0,6},{1,0},{2,2},{3,4},{4,7},{5,1},{6,3},{7,5},{8,14},{9,8},{10,1... | collective-permute-start | bytes 589832 | tf_op jit(solution)/shard_map/ppermute | solution.py:31
  186.7 8.7 %collective-permute-start.35 = (bf16[192,512]{1,0:T(8,128)(2,1)S(1)}, bf16[192,512]{1,0:T(8,128)(2,1)S(1)}, u32[]{:S(2)}, u32[]{:S(2)}) collective-permute-start(bf16[192,512]{1,0:T(8,128)(2,1)S(1)} %get-tuple-element.19), channel_id=1, source_target_pairs={{0,4},{1,6},{2,0},{3,2},{4,5},{5,7},{6,1},{7,3},{8,12},{9,14},{10,... | collective-permute-start | bytes 589832 | tf_op jit(solution)/shard_map/ppermute | solution.py:31
  197.4 3.3 %collective-permute-done.35 = bf16[192,512]{1,0:T(8,128)(2,1)S(1)} collective-permute-done((bf16[192,512]{1,0:T(8,128)(2,1)S(1)}, bf16[192,512]{1,0:T(8,128)(2,1)S(1)}, u32[]{:S(2)}, u32[]{:S(2)}) %collective-permute-start.35) | collective-permute-done | bytes 196640 | tf_op jit(solution)/shard_map/ppermute | solution.py:31
  200.7 5.9 %collective-permute-start.29 = (f16[512,768]{1,0:T(8,128)(2,1)}, f16[512,768]{1,0:T(8,128)(2,1)}, u32[]{:S(2)}, u32[]{:S(2)}) collective-permute-start(f16[512,768]{1,0:T(8,128)(2,1)} %copy.31), channel_id=1, source_target_pairs={{0,1},{1,0},{2,3},{3,2},{4,5},{5,4},{6,7},{7,6},{8,9},{9,8},{10,11... | collective-permute-start | bytes 2359304 | tf_op jit(solution)/shard_map/ppermute | solution.py:31
  206.6 2.2 collective-permute-done.36
  209.9 2.1 bitcast_dynamic-update-slice_fusion.7
  212.6 15.9 %multiply_add_fusion.1 = (f32[2,2,2,384,768]{4,3,2,1,0:T(8,128)}, f32[2,2,2,384,768]{4,3,2,1,0:T(8,128)}) fusion(f32[2,2,2,384,768]{4,3,2,1,0:T(8,128)} %bitcast.151, f16[2,2,2,384,768]{4,3,2,1,0:T(8,128)(2,1)S(1)} %bitcast_dynamic-update-slice_fusion.11, f32[2,2,2,384,768]{4,3,2,1,0:T(8,128)} %bitcast.153), kind=kLoop, calls=%fused_computation.4 | loop fusion | flops 18874368 | bytes 42467328 | tf_op jit(solution)/shard_map/add | solution.py:105
  235.7 12.8 %collective-permute-done.31 = f16[512,768]{1,0:T(8,128)(2,1)S(1)} collective-permute-done((f16[512,768]{1,0:T(8,128)(2,1)S(1)}, f16[512,768]{1,0:T(8,128)(2,1)S(1)}, u32[]{:S(2)}, u32[]{:S(2)}) %collective-permute-start.31) | collective-permute-done | bytes 786464 | tf_op jit(solution)/shard_map/ppermute | solution.py:31
  252.3 13.6 %multiply_add_fusion = (f32[2,2,2,512,768]{4,3,2,1,0:T(8,128)}, f32[2,2,2,512,768]{4,3,2,1,0:T(8,128)}) fusion(f32[2,2,2,512,768]{4,3,2,1,0:T(8,128)S(1)} %bitcast.143, f16[2,2,2,512,768]{4,3,2,1,0:T(8,128)(2,1)S(1)} %bitcast_dynamic-update-slice_fusion, f32[2,2,2,512,768]{4,3,2,1,0:T(8,128)} %bitcast.145), kind=kLoop, calls=%fused_computation.1 | loop fusion | flops 25165824 | bytes 56623104 | tf_op jit(solution)/shard_map/add | solution.py:105
  (155 shorter events, 51.4 us)
Async XLA Ops:
  9.8 63.2 %collective-permute-start.20 = (f32[2,192,2048]{2,1,0:T(8,128)}, f32[2,192,2048]{2,1,0:T(8,128)}, u32[]{:S(2)}, u32[]{:S(2)}) collective-permute-start(f32[2,192,2048]{2,1,0:T(8,128)} %pad_maximum_fusion), channel_id=1, source_target_pairs={{0,8},{1,9},{2,10},{3,11},{4,12},{5,13},{6,14},{7,15},{8,0},{9,1},... | collective-permute-start | bytes 9437192 | tf_op jit(solution)/shard_map/ppermute | solution.py:31
  13.6 16.8 %collective-permute-start.1 = (f16[192,1536]{1,0:T(8,128)(2,1)}, f16[192,1536]{1,0:T(8,128)(2,1)}, u32[]{:S(2)}, u32[]{:S(2)}) collective-permute-start(f16[192,1536]{1,0:T(8,128)(2,1)} %fusion.3), channel_id=1, source_target_pairs={{0,16},{1,17},{2,18},{3,19},{4,20},{5,21},{6,22},{7,23},{8,24},{9,... | collective-permute-start | bytes 1769480 | tf_op jit(solution)/shard_map/ppermute | solution.py:31
  32.5 19.0 %collective-permute-start.2 = (f16[192,384]{1,0:T(8,128)(2,1)S(1)}, f16[192,384]{1,0:T(8,128)(2,1)}, u32[]{:S(2)}, u32[]{:S(2)}) collective-permute-start(f16[192,384]{1,0:T(8,128)(2,1)S(1)} %get-tuple-element.33), channel_id=1, source_target_pairs={{0,0},{1,4},{2,1},{3,5},{4,2},{5,6},{6,3},{7,7},{8,8},{9,12},{10,9... | collective-permute-start | bytes 442376 | tf_op jit(solution)/shard_map/ppermute | solution.py:31
  40.2 12.3 %collective-permute-start.3 = (f16[192,384]{1,0:T(8,128)(2,1)}, f16[192,384]{1,0:T(8,128)(2,1)S(1)}, u32[]{:S(2)}, u32[]{:S(2)}) collective-permute-start(f16[192,384]{1,0:T(8,128)(2,1)} %get-tuple-element.32), channel_id=1, source_target_pairs={{0,1},{1,5},{2,2},{3,6},{4,3},{5,7},{6,0},{7,4},{8,9},{9,13},{10,1... | collective-permute-start | bytes 442376 | tf_op jit(solution)/shard_map/ppermute | solution.py:31
  47.2 16.8 %collective-permute-start.4 = (f16[192,384]{1,0:T(8,128)(2,1)}, f16[192,384]{1,0:T(8,128)(2,1)S(1)}, u32[]{:S(2)}, u32[]{:S(2)}) collective-permute-start(f16[192,384]{1,0:T(8,128)(2,1)} %get-tuple-element.31), channel_id=1, source_target_pairs={{0,2},{1,6},{2,3},{3,7},{4,0},{5,4},{6,1},{7,5},{8,10},{9,14},{10,... | collective-permute-start | bytes 442376 | tf_op jit(solution)/shard_map/ppermute | solution.py:31
  47.2 16.8 %collective-permute-start.5 = (f16[192,384]{1,0:T(8,128)(2,1)S(1)}, f16[192,384]{1,0:T(8,128)(2,1)S(1)}, u32[]{:S(2)}, u32[]{:S(2)}) collective-permute-start(f16[192,384]{1,0:T(8,128)(2,1)S(1)} %get-tuple-element.30), channel_id=1, source_target_pairs={{0,3},{1,7},{2,0},{3,4},{4,1},{5,5},{6,2},{7,6},{8,11},{9,15},{10,... | collective-permute-start | bytes 442376 | tf_op jit(solution)/shard_map/ppermute | solution.py:31
  65.2 35.3 %collective-permute-start.6 = (f16[384,768]{1,0:T(8,128)(2,1)}, f16[384,768]{1,0:T(8,128)(2,1)}, u32[]{:S(2)}, u32[]{:S(2)}) collective-permute-start(f16[384,768]{1,0:T(8,128)(2,1)} %copy.26), channel_id=1, source_target_pairs={{0,8},{1,9},{2,10},{3,11},{4,12},{5,13},{6,14},{7,15},{8,0},{9,1},... | collective-permute-start | bytes 1769480 | tf_op jit(solution)/shard_map/ppermute | solution.py:31
  65.2 36.8 %collective-permute-start.7 = (f16[384,768]{1,0:T(8,128)(2,1)}, f16[384,768]{1,0:T(8,128)(2,1)}, u32[]{:S(2)}, u32[]{:S(2)}) collective-permute-start(f16[384,768]{1,0:T(8,128)(2,1)} %copy.26), channel_id=1, source_target_pairs={{0,16},{1,17},{2,18},{3,19},{4,20},{5,21},{6,22},{7,23},{8,24},{9,... | collective-permute-start | bytes 1769480 | tf_op jit(solution)/shard_map/ppermute | solution.py:31
  66.7 37.7 %collective-permute-start.9 = (f16[384,768]{1,0:T(8,128)(2,1)}, f16[384,768]{1,0:T(8,128)(2,1)}, u32[]{:S(2)}, u32[]{:S(2)}) collective-permute-start(f16[384,768]{1,0:T(8,128)(2,1)} %copy.26), channel_id=1, source_target_pairs={{0,1},{1,0},{2,3},{3,2},{4,5},{5,4},{6,7},{7,6},{8,9},{9,8},{10,11... | collective-permute-start | bytes 1769480 | tf_op jit(solution)/shard_map/ppermute | solution.py:31
  71.4 11.8 %collective-permute-start.13 = (bf16[192,384]{1,0:T(8,128)(2,1)S(1)}, bf16[192,384]{1,0:T(8,128)(2,1)S(1)}, u32[]{:S(2)}, u32[]{:S(2)}) collective-permute-start(bf16[192,384]{1,0:T(8,128)(2,1)S(1)} %get-tuple-element.29), channel_id=1, source_target_pairs={{0,0},{1,2},{2,4},{3,6},{4,1},{5,3},{6,5},{7,7},{8,8},{9,10},{10,1... | collective-permute-start | bytes 442376 | tf_op jit(solution)/shard_map/ppermute | solution.py:31
  73.1 15.2 %collective-permute-start.14 = (bf16[192,384]{1,0:T(8,128)(2,1)S(1)}, bf16[192,384]{1,0:T(8,128)(2,1)S(1)}, u32[]{:S(2)}, u32[]{:S(2)}) collective-permute-start(bf16[192,384]{1,0:T(8,128)(2,1)S(1)} %get-tuple-element.28), channel_id=1, source_target_pairs={{0,6},{1,0},{2,2},{3,4},{4,7},{5,1},{6,3},{7,5},{8,14},{9,8},{10,1... | collective-permute-start | bytes 442376 | tf_op jit(solution)/shard_map/ppermute | solution.py:31
  88.3 11.3 %collective-permute-start.16 = (bf16[192,384]{1,0:T(8,128)(2,1)S(1)}, bf16[192,384]{1,0:T(8,128)(2,1)S(1)}, u32[]{:S(2)}, u32[]{:S(2)}) collective-permute-start(bf16[192,384]{1,0:T(8,128)(2,1)S(1)} %get-tuple-element.26), channel_id=1, source_target_pairs={{0,2},{1,4},{2,6},{3,0},{4,3},{5,5},{6,7},{7,1},{8,10},{9,12},{10,... | collective-permute-start | bytes 442376 | tf_op jit(solution)/shard_map/ppermute | solution.py:31
  99.7 16.3 %collective-permute-start.18 = (bf16[192,1536]{1,0:T(8,128)(2,1)S(1)}, bf16[192,1536]{1,0:T(8,128)(2,1)}, u32[]{:S(2)}, u32[]{:S(2)}) collective-permute-start(bf16[192,1536]{1,0:T(8,128)(2,1)S(1)} %constant_dynamic-update-slice_fusion.5), channel_id=1, source_target_pairs={{0,16},{1,17},{2,18},{3,19},{4,20},{5,21},{6,22},{7,23},{8,24},{9,... | collective-permute-start | bytes 1769480 | tf_op jit(solution)/shard_map/ppermute | solution.py:31
  100.5 31.7 %collective-permute-start.21 = (f16[192,2048]{1,0:T(8,128)(2,1)S(1)}, f16[192,2048]{1,0:T(8,128)(2,1)S(1)}, u32[]{:S(2)}, u32[]{:S(2)}) collective-permute-start(f16[192,2048]{1,0:T(8,128)(2,1)S(1)} %fusion.2), channel_id=1, source_target_pairs={{0,16},{1,17},{2,18},{3,19},{4,20},{5,21},{6,22},{7,23},{8,24},{9,... | collective-permute-start | bytes 2359304 | tf_op jit(solution)/shard_map/ppermute | solution.py:31
  102.1 67.6 %collective-permute-start.8 = (f16[384,768]{1,0:T(8,128)(2,1)}, f16[384,768]{1,0:T(8,128)(2,1)}, u32[]{:S(2)}, u32[]{:S(2)}) collective-permute-start(f16[384,768]{1,0:T(8,128)(2,1)} %collective-permute-done.7), channel_id=1, source_target_pairs={{0,8},{1,9},{2,10},{3,11},{4,12},{5,13},{6,14},{7,15},{8,0},{9,1},... | collective-permute-start | bytes 1769480 | tf_op jit(solution)/shard_map/ppermute | solution.py:31
  104.5 71.1 %collective-permute-start.11 = (f16[384,768]{1,0:T(8,128)(2,1)}, f16[384,768]{1,0:T(8,128)(2,1)}, u32[]{:S(2)}, u32[]{:S(2)}) collective-permute-start(f16[384,768]{1,0:T(8,128)(2,1)} %collective-permute-done.7), channel_id=1, source_target_pairs={{0,1},{1,0},{2,3},{3,2},{4,5},{5,4},{6,7},{7,6},{8,9},{9,8},{10,11... | collective-permute-start | bytes 1769480 | tf_op jit(solution)/shard_map/ppermute | solution.py:31
  104.6 69.1 %collective-permute-start.10 = (f16[384,768]{1,0:T(8,128)(2,1)}, f16[384,768]{1,0:T(8,128)(2,1)}, u32[]{:S(2)}, u32[]{:S(2)}) collective-permute-start(f16[384,768]{1,0:T(8,128)(2,1)} %collective-permute-done.9), channel_id=1, source_target_pairs={{0,8},{1,9},{2,10},{3,11},{4,12},{5,13},{6,14},{7,15},{8,0},{9,1},... | collective-permute-start | bytes 1769480 | tf_op jit(solution)/shard_map/ppermute | solution.py:31
  116.0 93.3 %collective-permute-start.19 = (bf16[192,1536]{1,0:T(8,128)(2,1)}, bf16[192,1536]{1,0:T(8,128)(2,1)}, u32[]{:S(2)}, u32[]{:S(2)}) collective-permute-start(bf16[192,1536]{1,0:T(8,128)(2,1)} %collective-permute-done.18), channel_id=1, source_target_pairs={{0,8},{1,9},{2,10},{3,11},{4,12},{5,13},{6,14},{7,15},{8,0},{9,1},... | collective-permute-start | bytes 1769480 | tf_op jit(solution)/shard_map/ppermute | solution.py:31
  134.6 11.9 %collective-permute-start.23 = (f16[192,512]{1,0:T(8,128)(2,1)S(1)}, f16[192,512]{1,0:T(8,128)(2,1)S(1)}, u32[]{:S(2)}, u32[]{:S(2)}) collective-permute-start(f16[192,512]{1,0:T(8,128)(2,1)S(1)} %get-tuple-element.24), channel_id=1, source_target_pairs={{0,1},{1,5},{2,2},{3,6},{4,3},{5,7},{6,0},{7,4},{8,9},{9,13},{10,1... | collective-permute-start | bytes 589832 | tf_op jit(solution)/shard_map/ppermute | solution.py:31
  168.7 59.8 %collective-permute-start.26 = (f16[512,768]{1,0:T(8,128)(2,1)}, f16[512,768]{1,0:T(8,128)(2,1)}, u32[]{:S(2)}, u32[]{:S(2)}) collective-permute-start(f16[512,768]{1,0:T(8,128)(2,1)} %copy.31), channel_id=1, source_target_pairs={{0,8},{1,9},{2,10},{3,11},{4,12},{5,13},{6,14},{7,15},{8,0},{9,1},... | collective-permute-start | bytes 2359304 | tf_op jit(solution)/shard_map/ppermute | solution.py:31
  169.7 58.8 %collective-permute-start.27 = (f16[512,768]{1,0:T(8,128)(2,1)}, f16[512,768]{1,0:T(8,128)(2,1)S(1)}, u32[]{:S(2)}, u32[]{:S(2)}) collective-permute-start(f16[512,768]{1,0:T(8,128)(2,1)} %copy.31), channel_id=1, source_target_pairs={{0,16},{1,17},{2,18},{3,19},{4,20},{5,21},{6,22},{7,23},{8,24},{9,... | collective-permute-start | bytes 2359304 | tf_op jit(solution)/shard_map/ppermute | solution.py:31
  173.7 13.0 %collective-permute-start.33 = (bf16[192,512]{1,0:T(8,128)(2,1)S(1)}, bf16[192,512]{1,0:T(8,128)(2,1)S(1)}, u32[]{:S(2)}, u32[]{:S(2)}) collective-permute-start(bf16[192,512]{1,0:T(8,128)(2,1)S(1)} %get-tuple-element.21), channel_id=1, source_target_pairs={{0,0},{1,2},{2,4},{3,6},{4,1},{5,3},{6,5},{7,7},{8,8},{9,10},{10,1... | collective-permute-start | bytes 589832 | tf_op jit(solution)/shard_map/ppermute | solution.py:31
  175.6 19.9 %collective-permute-start.34 = (bf16[192,512]{1,0:T(8,128)(2,1)S(1)}, bf16[192,512]{1,0:T(8,128)(2,1)S(1)}, u32[]{:S(2)}, u32[]{:S(2)}) collective-permute-start(bf16[192,512]{1,0:T(8,128)(2,1)S(1)} %get-tuple-element.20), channel_id=1, source_target_pairs={{0,6},{1,0},{2,2},{3,4},{4,7},{5,1},{6,3},{7,5},{8,14},{9,8},{10,1... | collective-permute-start | bytes 589832 | tf_op jit(solution)/shard_map/ppermute | solution.py:31
  186.7 14.0 %collective-permute-start.35 = (bf16[192,512]{1,0:T(8,128)(2,1)S(1)}, bf16[192,512]{1,0:T(8,128)(2,1)S(1)}, u32[]{:S(2)}, u32[]{:S(2)}) collective-permute-start(bf16[192,512]{1,0:T(8,128)(2,1)S(1)} %get-tuple-element.19), channel_id=1, source_target_pairs={{0,4},{1,6},{2,0},{3,2},{4,5},{5,7},{6,1},{7,3},{8,12},{9,14},{10,... | collective-permute-start | bytes 589832 | tf_op jit(solution)/shard_map/ppermute | solution.py:31
  195.5 13.3 %collective-permute-start.36 = (bf16[192,512]{1,0:T(8,128)(2,1)S(1)}, bf16[192,512]{1,0:T(8,128)(2,1)S(1)}, u32[]{:S(2)}, u32[]{:S(2)}) collective-permute-start(bf16[192,512]{1,0:T(8,128)(2,1)S(1)} %get-tuple-element.18), channel_id=1, source_target_pairs={{0,2},{1,4},{2,6},{3,0},{4,3},{5,5},{6,7},{7,1},{8,10},{9,12},{10,... | collective-permute-start | bytes 589832 | tf_op jit(solution)/shard_map/ppermute | solution.py:31
  200.7 27.9 %collective-permute-start.29 = (f16[512,768]{1,0:T(8,128)(2,1)}, f16[512,768]{1,0:T(8,128)(2,1)}, u32[]{:S(2)}, u32[]{:S(2)}) collective-permute-start(f16[512,768]{1,0:T(8,128)(2,1)} %copy.31), channel_id=1, source_target_pairs={{0,1},{1,0},{2,3},{3,2},{4,5},{5,4},{6,7},{7,6},{8,9},{9,8},{10,11... | collective-permute-start | bytes 2359304 | tf_op jit(solution)/shard_map/ppermute | solution.py:31
  209.3 22.2 %collective-permute-start.37 = (bf16[192,2048]{1,0:T(8,128)(2,1)S(1)}, bf16[192,2048]{1,0:T(8,128)(2,1)}, u32[]{:S(2)}, u32[]{:S(2)}) collective-permute-start(bf16[192,2048]{1,0:T(8,128)(2,1)S(1)} %constant_dynamic-update-slice_fusion), channel_id=1, source_target_pairs={{0,8},{1,9},{2,10},{3,11},{4,12},{5,13},{6,14},{7,15},{8,0},{9,1},... | collective-permute-start | bytes 2359304 | tf_op jit(solution)/shard_map/ppermute | solution.py:31
  211.9 19.6 %collective-permute-start.38 = (bf16[192,2048]{1,0:T(8,128)(2,1)S(1)}, bf16[192,2048]{1,0:T(8,128)(2,1)}, u32[]{:S(2)}, u32[]{:S(2)}) collective-permute-start(bf16[192,2048]{1,0:T(8,128)(2,1)S(1)} %constant_dynamic-update-slice_fusion), channel_id=1, source_target_pairs={{0,16},{1,17},{2,18},{3,19},{4,20},{5,21},{6,22},{7,23},{8,24},{9,... | collective-permute-start | bytes 2359304 | tf_op jit(solution)/shard_map/ppermute | solution.py:31
  228.5 20.0 %collective-permute-start.28 = (f16[512,768]{1,0:T(8,128)(2,1)S(1)}, f16[512,768]{1,0:T(8,128)(2,1)S(1)}, u32[]{:S(2)}, u32[]{:S(2)}) collective-permute-start(f16[512,768]{1,0:T(8,128)(2,1)S(1)} %collective-permute-done.27), channel_id=1, source_target_pairs={{0,8},{1,9},{2,10},{3,11},{4,12},{5,13},{6,14},{7,15},{8,0},{9,1},... | collective-permute-start | bytes 2359304 | tf_op jit(solution)/shard_map/ppermute | solution.py:31
  228.5 20.0 %collective-permute-start.31 = (f16[512,768]{1,0:T(8,128)(2,1)S(1)}, f16[512,768]{1,0:T(8,128)(2,1)S(1)}, u32[]{:S(2)}, u32[]{:S(2)}) collective-permute-start(f16[512,768]{1,0:T(8,128)(2,1)S(1)} %collective-permute-done.27), channel_id=1, source_target_pairs={{0,1},{1,0},{2,3},{3,2},{4,5},{5,4},{6,7},{7,6},{8,9},{9,8},{10,11... | collective-permute-start | bytes 2359304 | tf_op jit(solution)/shard_map/ppermute | solution.py:31
  228.6 21.3 %collective-permute-start.30 = (f16[512,768]{1,0:T(8,128)(2,1)}, f16[512,768]{1,0:T(8,128)(2,1)S(1)}, u32[]{:S(2)}, u32[]{:S(2)}) collective-permute-start(f16[512,768]{1,0:T(8,128)(2,1)} %collective-permute-done.29), channel_id=1, source_target_pairs={{0,8},{1,9},{2,10},{3,11},{4,12},{5,13},{6,14},{7,15},{8,0},{9,1},... | collective-permute-start | bytes 2359304 | tf_op jit(solution)/shard_map/ppermute | solution.py:31
  231.5 18.8 %collective-permute-start.39 = (bf16[192,2048]{1,0:T(8,128)(2,1)}, bf16[192,2048]{1,0:T(8,128)(2,1)S(1)}, u32[]{:S(2)}, u32[]{:S(2)}) collective-permute-start(bf16[192,2048]{1,0:T(8,128)(2,1)} %collective-permute-done.38), channel_id=1, source_target_pairs={{0,8},{1,9},{2,10},{3,11},{4,12},{5,13},{6,14},{7,15},{8,0},{9,1},... | collective-permute-start | bytes 2359304 | tf_op jit(solution)/shard_map/ppermute | solution.py:31
  (21 other events, 264.5 us)

commit v2 on v0

v2 whole, which is shorter than its diff:
```python
import jax
import jax.numpy as jnp
from jax import lax
from jax.experimental import pallas as pl
from jax.experimental.pallas import tpu as pltpu
from jax.sharding import PartitionSpec as P

momentum_coef = 0.9
outer_rate = 0.7
axes = ("rep", "shard", "tp")
scale = 2048.0
vmem = 52 * 2**20


def pairs(mesh_sizes, move):
    groups, shards, tensor = mesh_sizes
    result = []
    for r in range(groups):
        for z in range(shards):
            for y in range(tensor):
                r2, z2, y2 = move(r, z, y)
                result.append(((r * shards + z) * tensor + y, (r2 * shards + z2) * tensor + y2))
    return result


class Table:
    def __init__(self, rows, width, half_shards, tensor):
        self.shape = (rows, half_shards * 4 * tensor * width)
        self.tensor, self.width = tensor, width

    def block(self, c, x, a, h):
        rows = self.shape[0]
        if h is None:
            return (rows, self.tensor * self.width), (0, (a * 2 + c) * 2 + x)
        return (rows, self.width), (0, ((a * 2 + c) * 2 + x) * self.tensor + h)


class Expert:
    def __init__(self, rows, width, half_shards, tensor):
        self.shape = (2, 2, rows, half_shards * tensor * width)
        self.tensor, self.width = tensor, width

    def block(self, c, x, a, h):
        rows = self.shape[2]
        if h is None:
            return (1, 1, rows, self.tensor * self.width), (c, x, 0, a)
        return (1, 1, rows, self.width), (c, x, 0, a * self.tensor + h)


def aligned(rows, width):
    return rows % 16 == 0 and width % 128 == 0


def cut(layout, value, c, x, a):
    shape, at = layout.block(c, x, a, None)
    start = [i * n for i, n in zip(at, shape)]
    return lax.dynamic_slice(value, start, shape).reshape(layout.shape[-2], layout.tensor * layout.width)


def call(kernel, name, grid, scalars, inputs, outputs, aliases, cost):
    in_specs = [
        pl.BlockSpec(memory_space=pl.ANY) if block is None else pl.BlockSpec(block, at)
        for _, block, at in inputs
    ]
    grid_spec = pltpu.PrefetchScalarGridSpec(
        num_scalar_prefetch=1,
        grid=grid,
        in_specs=in_specs,
        out_specs=[pl.BlockSpec(block, at) for _, _, block, at in outputs],
    )
    return pl.pallas_call(
        kernel,
        grid_spec=grid_spec,
        out_shape=[jax.ShapeDtypeStruct(shape, dtype) for shape, dtype, _, _ in outputs],
        input_output_aliases=aliases,
        compiler_params=pltpu.CompilerParams(vmem_limit_bytes=vmem),
        cost_estimate=pl.CostEstimate(flops=20000000000, bytes_accessed=1000000, transcendentals=0),
        name=name,
    )(scalars, *[array for array, _, _ in inputs])


def pick(layout, value, here, half_shards):
    rows, wide = layout.shape[-2], layout.tensor * layout.width
    if not aligned(rows, layout.width):
        parts = [cut(layout, value, here[0], x, a) for x in range(2) for a in range(half_shards)]
        return jnp.stack(parts).reshape(2, half_shards, rows, wide)

    def kernel(here, value_ref, out_ref):
        out_ref[...] = value_ref[...].reshape(out_ref.shape)

    block = layout.block(0, 0, 0, None)[0]
    return call(
        kernel,
        "pick",
        (2, half_shards),
        here,
        [(value, block, lambda x, a, here: layout.block(here[0], x, a, None)[1])],
        [((2, half_shards, rows, wide), value.dtype, (1, 1, rows, wide), lambda x, a, here: (x, a, 0, 0))],
        {},
        2 * half_shards * rows * wide * 16,
    )[0]


def add_split(layout, value, received, here, half_shards):
    rows, tensor, width = layout.shape[-2], layout.tensor, layout.width
    if not aligned(rows, width):
        halves = []
        for x in (1 - here[1], here[1]):
            own = jnp.stack([cut(layout, value, here[0], x, a) for a in range(half_shards)])
            halves.append(own + lax.dynamic_index_in_dim(received, x, 0, False))
        return halves

    def kernel(here, own_sent, own_kept, got_sent, got_kept, sent_ref, kept_ref):
        shape = sent_ref.shape
        sent_ref[...] = own_sent[...].reshape(shape) + got_sent[...].reshape(shape)
        kept_ref[...] = own_kept[...].reshape(shape) + got_kept[...].reshape(shape)

    block = layout.block(0, 0, 0, 0)[0]
    got_block = (1, 1, rows, width)
    out_block = (1, rows, width)
    out_at = lambda a, h, here: (a, 0, h)
    out = ((half_shards, rows, tensor * width), jnp.float32, out_block, out_at)
    return call(
        kernel,
        "add_split",
        (half_shards, tensor),
        here,
        [
            (value, block, lambda a, h, here: layout.block(here[0], 1 - here[1], a, h)[1]),
            (value, block, lambda a, h, here: layout.block(here[0], here[1], a, h)[1]),
            (received, got_block, lambda a, h, here: (1 - here[1], a, 0, h)),
            (received, got_block, lambda a, h, here: (here[1], a, 0, h)),
        ],
        [out, out],
        {},
        half_shards * rows * tensor * width * 24,
    )


def transposed_base(master, moment, here):
    width, model = master.shape[-2:]
    step = 128
    if not aligned(model, width):
        start, shape = (here[0], here[1], here[2], 0, 0), (1, 1, 1, width, model)
        base = lax.dynamic_slice(master, start, shape) - (
            outer_rate * momentum_coef * momentum_coef
        ) * lax.dynamic_slice(moment, start, shape)
        return base[0, 0, 0].T

    def kernel(here, master_ref, moment_ref, out_ref):
        shape = (step, model)
        base = master_ref[...].reshape(shape) - (
            outer_rate * momentum_coef * momentum_coef
        ) * moment_ref[...].reshape(shape)
        out_ref[...] = base.T

    at = lambda i, here: (here[0], here[1], here[2], i, 0)
    block = (1, 1, 1, step, model)
    return call(
        kernel,
        "transposed_base",
        (width // step,),
        here,
        [(master, block, at), (moment, block, at)],
        [((model, width), jnp.float32, (model, step), lambda i, here: (0, i))],
        {},
        model * width * 12,
    )[0]


def update(parts, master, moment, here, before):
    width, model = master.shape[-2:]
    if not aligned(model, width):
        weights, velocity = before or (jnp.zeros_like(master), jnp.zeros_like(moment))
        for d in range(2):
            start, shape = (here[0], here[1] ^ d, here[2], 0, 0), (1, 1, 1, width, model)
            mean = parts[d].reshape(shape) * (1 / (4 * scale))
            new = momentum_coef * lax.dynamic_slice(moment, start, shape) + mean
            velocity = lax.dynamic_update_slice(velocity, new, start)
            new = lax.dynamic_slice(master, start, shape) - outer_rate * (mean + momentum_coef * new)
            weights = lax.dynamic_update_slice(weights, new, start)
        return weights, velocity

    def kernel(here, own_ref, near_ref, master_ref, moment_ref, *refs):
        weights_ref, velocity_ref = refs[-2:]

        def compute(summed_ref):
            mean = summed_ref[...].reshape(weights_ref.shape) * (1 / (4 * scale))
            velocity = momentum_coef * moment_ref[...] + mean
            velocity_ref[...] = velocity
            weights_ref[...] = master_ref[...] - outer_rate * (mean + momentum_coef * velocity)

        @pl.when(pl.program_id(0) == 0)
        def _():
            compute(own_ref)

        @pl.when(pl.program_id(0) == 1)
        def _():
            compute(near_ref)

    at = lambda d, here: (here[0], here[1] ^ d, here[2], 0, 0)
    block = (1, 1, 1, width, model)
    out = (master.shape, jnp.float32, block, at)
    inputs = [(part, (width, model), lambda d, here: (0, 0)) for part in parts]
    inputs += [(master, block, at), (moment, block, at)]
    aliases = {}
    if before is not None:
        inputs += [(value, None, None) for value in before]
        aliases = {5: 0, 6: 1}
    return call(kernel, "update", (2,), here, inputs, [out, out], aliases, 2 * width * model * 20)


def place(layout, parts, here, before, half_shards):
    rows, width, tensor = layout.shape[-2], layout.width, layout.tensor
    if not aligned(rows, width):
        result = jnp.zeros(layout.shape, jnp.bfloat16) if before is None else before
        for j, part in enumerate(parts):
            for a in range(half_shards):
                shape, at = layout.block(here[0], here[1] ^ (j // 2), a, here[2] ^ (j % 2))
                start = [i * n for i, n in zip(at, shape)]
                result = lax.dynamic_update_slice(result, part[a].reshape(shape), start)
        return result

    def kernel(here, *refs):
        out_ref = refs[-1]
        lead = (0,) * (len(out_ref.shape) - 2)
        for x in range(2):
            for y in range(tensor):

                @pl.when((pl.program_id(0) == x) & (here[2] == y))
                def _():
                    for t in range(tensor):
                        out_ref[lead + (slice(None), slice((y ^ t) * width, ((y ^ t) + 1) * width))] = refs[2 * x + t][0]

    def part_at(x):
        if x == 0:
            return lambda d, a, here: (jnp.where(d == 0, a, half_shards - 1), 0, 0)
        return lambda d, a, here: (jnp.where(d == 1, a, 0), 0, 0)

    block = layout.block(0, 0, 0, None)[0]
    out_at = lambda d, a, here: layout.block(here[0], here[1] ^ d, a, None)[1]
    inputs = [(part, (1, rows, width), part_at(j // 2)) for j, part in enumerate(parts)]
    aliases = {}
    if before is not None:
        inputs.append((before, None, None))
        aliases = {5: 0}
    return call(
        kernel,
        "place",
        (2, half_shards),
        here,
        inputs,
        [(layout.shape, jnp.bfloat16, block, out_at)],
        aliases,
        4 * half_shards * rows * width * 4,
    )[0]


def local(expert_change, table_change, expert_master, expert_moment, table_master, table_moment):
    groups, shards, tensor = sizes = tuple(lax.axis_size(a) for a in axes)
    r, z, y = (lax.axis_index(a) for a in axes)
    core, x = r % 2, r // 2
    half_shards = shards // tensor
    here = jnp.stack([core, x, y]).astype(jnp.int32)
    other = jnp.stack([1 - core, x, y]).astype(jnp.int32)
    here_far = jnp.stack([core, x, 1 - y]).astype(jnp.int32)
    other_far = jnp.stack([1 - core, x, 1 - y]).astype(jnp.int32)

    def send(name, value, move):
        with jax.named_scope(name):
            return lax.ppermute(value, axes, pairs(sizes, move))

    def over_core(name, value):
        return send(name + "_core", value, lambda r, z, y: (r ^ 1, z, y))

    def over_x(name, value):
        return send(name + "_x", value, lambda r, z, y: (r ^ 2, z, y))

    def over_y(name, value):
        return send(name + "_y", value, lambda r, z, y: (r, z, y ^ 1))

    def over_z(name, value):
        with jax.named_scope(name + "_z"):
            return lax.all_to_all(value, "shard", split_axis=0, concat_axis=0, tiled=True)

    def index(value, i):
        return lax.dynamic_index_in_dim(value, i, 0, False)

    last = []

    def after(*values):
        if not last:
            return values if len(values) > 1 else values[0]
        values = lax.optimization_barrier((*values, last[0]))[:-1]
        return values if len(values) > 1 else values[0]

    def mark(value):
        last[:] = [value]
        return value

    def unmix(got):
        k = 1
        while k < shards:
            swap = (z & k) != 0
            got = [jnp.where(swap, got[i ^ k], got[i]) for i in range(shards)]
            k *= 2
        return got

    model = expert_master.shape[-1]
    mats, rows, expert_columns = expert_change.shape[1:]

    class Part:
        def __init__(self, name, layout, change, master, moment):
            self.name, self.layout, self.change = name, layout, change
            shape = (2, 2, tensor, layout.width, model)
            self.master, self.moment = master.reshape(shape), moment.reshape(shape)
            self.result = None

        def start(self):
            picked = mark(pick(self.layout, after(self.change), other, half_shards))
            self.got = over_core(self.name, picked)

        def sum_core(self):
            change, got = after(self.change, self.got)
            sent, self.kept = add_split(self.layout, change, got, here, half_shards)
            self.received = over_x(self.name, mark((sent * scale).astype(jnp.float16)))

        def bases(self):
            master, moment = after(self.master, self.moment)
            self.base = mark(transposed_base(master, moment, here))

        def sum_x(self):
            kept, received = after(self.kept, self.received)
            width = self.layout.width
            total = (kept * scale + received.astype(jnp.float32)).astype(jnp.float16)
            self.near = lax.dynamic_slice_in_dim(total, y * width, width, 2)
            self.far = over_y(self.name, mark(lax.dynamic_slice_in_dim(total, (1 - y) * width, width, 2)))

        def scatter(self):
            near, far = after(self.near, self.far)

            def of_shard(s):
                a = s % half_shards
                return jnp.where(s // half_shards == y, index(near, a), index(far, a))

            sent = [of_shard(z ^ k) for k in range(shards)]
            mark(sent[-1])
            self.sums = [sent[0]] + [
                send(f"{self.name}_z{k}", sent[k], lambda r, z, y: (r, z ^ k, y)) for k in range(1, shards)
            ]

        def low_part(self):
            received = after(self.received)
            base = self.base.reshape(received.shape)
            low = base - (outer_rate * (1 + momentum_coef) / (groups * scale)) * received.astype(jnp.float32)
            self.low = mark(low.astype(jnp.bfloat16))

        def copies_z(self):
            self.low = over_z(self.name + "_back", mark(after(self.low)))

        def gather(self):
            self.received = received = jnp.stack(unmix(after(*self.sums)))
            own = mark(jnp.transpose(received, (2, 0, 1)).reshape(received.shape[2], model))
            self.near = over_x(self.name + "_gather", own)
            self.far = over_y(self.name + "_gather", own)
            self.own = own

        def gather_x(self):
            near = after(self.near)
            self.far2 = over_y(self.name + "_gather2", near)
            own, near = self.own.astype(jnp.float32), near.astype(jnp.float32)
            mark(near)
            self.pair = own, near
            self.pair_core = over_core(self.name + "_gather", own), over_core(self.name + "_gather", near)

        def gather_y(self):
            far, far2 = after(self.far, self.far2)
            far, far2 = far.astype(jnp.float32), far2.astype(jnp.float32)
            mark(far2)
            self.far_pair = far, far2
            self.far_core = over_core(self.name + "_gather2", far), over_core(self.name + "_gather2", far2)

        def wait(self, name):
            setattr(self, name, mark(after(getattr(self, name))))

        def update(self, which):
            parts, where = {
                "pair": lambda: (self.pair, here),
                "pair_core": lambda: (self.pair_core, other),
                "far_pair": lambda: (self.far_pair, here_far),
                "far_core": lambda: (self.far_core, other_far),
            }[which]()
            parts = after(*parts)
            self.result = update(parts, self.master, self.moment, where, self.result)
            mark(self.result[0])

        def copies_y(self):
            got = after(self.low)
            near = lax.dynamic_slice_in_dim(got, y * half_shards, half_shards, 0)
            far = mark(lax.dynamic_slice_in_dim(got, (1 - y) * half_shards, half_shards, 0))
            self.low_near = near
            self.low_far = over_y(self.name + "_back", far)
            self.low_near_x = over_x(self.name + "_back", near)
            self.low_near_core = over_core(self.name + "_back", near)

        def copies_x(self):
            far = mark(after(self.low_far))
            self.low_far = far
            self.low_far_x = over_x(self.name + "_back2", far)
            self.low_far_core = over_core(self.name + "_back2", far)

        def copies_core(self):
            near_x, far_x = after(self.low_near_x, self.low_far_x)
            mark(far_x)
            self.parts = [self.low_near, self.low_far, near_x, far_x]
            self.parts_core = [
                self.low_near_core,
                self.low_far_core,
                over_core(self.name + "_back", near_x),
                over_core(self.name + "_back2", far_x),
            ]

        def place(self):
            parts = after(*self.parts)
            self.copies = mark(place(self.layout, parts, here, None, half_shards))

        def place_core(self):
            parts = after(*self.parts_core)
            self.copies = mark(place(self.layout, parts, other, self.copies, half_shards))

    t = Part(
        "table",
        Table(rows, table_change.shape[2] // (4 * shards), half_shards, tensor),
        table_change[0],
        table_master,
        table_moment,
    )
    expert_layout = Expert(rows, expert_columns // shards, half_shards, tensor)
    e = Part(
        "expert", expert_layout, expert_change[0].reshape(expert_layout.shape), expert_master, expert_moment
    )
    e.start()
    t.start()
    e.sum_core()
    t.sum_core()
    e.bases()
    t.bases()
    e.sum_x()
    e.scatter()
    t.sum_x()
    e.gather()
    t.scatter()
    e.low_part()
    e.wait("near")
    e.wait("far")
    e.gather_x()
    e.update("pair")
    t.gather()
    e.copies_z()
    e.update("pair_core")
    e.wait("far2")
    e.gather_y()
    t.low_part()
    e.update("far_pair")
    e.copies_y()
    t.copies_z()
    t.wait("near")
    t.wait("far")
    t.gather_x()
    e.update("far_core")
    e.wait("low_near_x")
    e.copies_x()
    t.update("pair")
    t.update("pair_core")
    t.copies_y()
    t.wait("far2")
    t.gather_y()
    e.copies_core()
    e.place()
    e.place_core()
    t.wait("low_near_x")
    t.copies_x()
    t.update("far_pair")
    t.copies_core()
    t.update("far_core")
    t.place()
    t.place_core()
    return (
        e.result[0].reshape(expert_master.shape),
        e.result[1].reshape(expert_master.shape),
        e.copies.reshape(mats, rows, expert_columns),
        t.result[0].reshape(table_master.shape),
        t.result[1].reshape(table_master.shape),
        t.copies,
    )


def solution(mesh):
    in_specs = (
        P("rep", None, "shard", "tp"),
        P("rep", "shard", "tp"),
        P(None, "shard", None),
        P(None, "shard", None),
        P("shard", None),
        P("shard", None),
    )
    out_specs = (
        P(None, "shard", None),
        P(None, "shard", None),
        P(None, "shard", "tp"),
        P("shard", None),
        P("shard", None),
        P("shard", "tp"),
    )
    return jax.shard_map(local, mesh=mesh, in_specs=in_specs, out_specs=out_specs, check_vma=False)
```

time: 1400 us -> 195 us (0.14)
  waiting for transfers between devices: 930 us -> 30.1 us
  local copies, waits for them, and re-layouts: 325 us -> 13.4 us
  Pallas kernels: 0 us -> 84.2 us
  other arithmetic: 97.9 us -> 21.1 us
  starting transfers between devices: 24.1 us -> 44.6 us
    all_to_all x4 -> x2, waiting for transfers between devices: 453 us -> 0.01 us  [over_z(): lax.all_to_all(value, 'shard', split_axis=0, concat_axis=0, tiled=True)]
    all_gather x2 -> x0, waiting for transfers between devices: 274 us -> none  [the longest x1 155 us: local(): lax.all_gather(summed[1], 'tp', axis=2, tiled=True)]
    psum x1 -> x0, waiting for transfers between devices: 201 us -> none  [local(): summed = lax.psum((experts_part, table_part), 'rep')]
    unnamed x13 -> x24, local copies, waits for them, and re-layouts: 126 us -> 5.68 us
    pallas_call x0 -> x18, Pallas kernels: none -> 84.2 us  [call(): pl.pallas_call(kernel, grid_spec=grid_spec, out_shape=[jax.ShapeDtypeStru...]
    all_to_all x5 -> x0, local copies, waits for them, and re-layouts: 59 us -> none  [the longest x1 34.1 us: local(): lax.all_to_all(halves[1], 'shard', split_axis=2, concat_axis=1, tiled=True)]
    div x4 -> x0, local copies, waits for them, and re-layouts: 49.7 us -> none  [the longest x2 32 us: local(): table_mean = table_sum / groups]
    all_gather x2 -> x0, local copies, waits for them, and re-layouts: 47.8 us -> none  [the longest x1 34.6 us: local(): lax.all_gather(summed[1], 'tp', axis=2, tiled=True)]
  transfers between devices with their start and end apart: 7 -> 42, of which waited for: 6 -> 8; matrix products, arithmetic and copies ran while one was open for 27% -> 15% of each run, Pallas kernels for 0% -> 40%
where the time goes in v2:
time: 195 us; the launch traced here: 194 us
  Pallas kernels  84.2 us (43%)
  starting transfers between devices  44.6 us (23%)
  waiting for transfers between devices  30.1 us (15%)
  other arithmetic  21.1 us (11%)
  local copies, waits for them, and re-layouts  13.4 us (7%)
    pallas_call x18, Pallas kernels, call(): pl.pallas_call(kernel, grid_spec=grid_spec, out_shape=[jax.ShapeDtypeStru...  84.2 us
    ppermute x40, starting transfers between devices, send(): return lax.ppermute(value, axes, pairs(sizes, move))  35.9 us
    ppermute x40, waiting for transfers between devices, send(): return lax.ppermute(value, axes, pairs(sizes, move))  30.1 us
    all_to_all x2, starting transfers between devices, over_z(): lax.all_to_all(value, 'shard', split_axis=0, concat_axis=0, tiled=True)  8.72 us
    convert_element_type x4, other arithmetic, gather_y(): far, far2 = (far.astype(jnp.float32), far2.astype(jnp.float32))  6.87 us
    convert_element_type x4, other arithmetic, gather_x(): own, near = (self.own.astype(jnp.float32), near.astype(jnp.float32))  6.83 us
    unnamed x24, local copies, waits for them, and re-layouts  5.68 us
  transfers between devices with their start and end apart: 42, of which 8 were waited for; matrix products, arithmetic and copies ran while one was open for 15% of the time, Pallas kernels for 40%

profile of v2, /device:TPU:0, one launch (start us, length us, event | category | flops | bytes accessed | tf_op | source)
XLA Modules:
  0.0 194.3 jit_solution(1556998854136537298)
XLA Ops:
  0.7 4.4 %pick.2 = f32[2,2,192,768]{3,2,1,0:T(8,128)} custom-call(s32[3]{0:T(128)S(1)} %pad_add_fusion.4.here, f32[2,2,192,1536]{3,2,1,0:T(8,128)} %bitcast.83), custom_call_target="tpu_custom_call" | custom-call | flops 20000000000 | bytes 1000000 | tf_op jit(solution)/shard_map/pick/pallas_call | solution.py:71
  5.6 4.7 %pick.3 = f32[2,2,192,1024]{3,2,1,0:T(8,128)} custom-call(s32[3]{0:T(128)S(1)} %pad_add_fusion.4.here, f32[192,8192]{1,0:T(8,128)} %bitcast.80), custom_call_target="tpu_custom_call" | custom-call | flops 20000000000 | bytes 1000000 | tf_op jit(solution)/shard_map/pick/pallas_call | solution.py:71
  10.5 4.7 %add_split.2 = (f32[2,192,768]{2,1,0:T(8,128)S(1)}, f32[2,192,768]{2,1,0:T(8,128)}) custom-call(s32[3]{0:T(128)S(1)} %pad_add_fusion.5.here, f32[2,2,192,1536]{3,2,1,0:T(8,128)} %bitcast.84, f32[2,2,192,1536]{3,2,1,0:T(8,128)} %bitcast.85, f32[2,2,192,768]{3,2,1,0:T(8,128)} %collective-permute-done.got_sent.got_kept, ...), custom_call_target="tpu_custom_call" | custom-call | flops 20000000000 | bytes 1000000 | tf_op jit(solution)/shard_map/add_split/pallas_call | solution.py:71
  15.3 3.0 %collective-permute-start.1 = (f16[2,192,768]{2,1,0:T(8,128)(2,1)S(1)}, f16[2,192,768]{2,1,0:T(8,128)(2,1)S(1)}, u32[]{:S(2)}, u32[]{:S(2)}) collective-permute-start(f16[2,192,768]{2,1,0:T(8,128)(2,1)S(1)} %multiply_convert_fusion.1), channel_id=1, source_target_pairs={{0,16},{1,17},{2,18},{3,19},{4,20},{5,21},{6,22},{7,23},{8,24},{9,... | collective-permute-start | bytes 1769480 | tf_op jit(solution)/shard_map/expert_x/ppermute | solution.py:271
  20.0 5.1 %add_split.3 = (f32[2,192,1024]{2,1,0:T(8,128)S(1)}, f32[2,192,1024]{2,1,0:T(8,128)}) custom-call(s32[3]{0:T(128)S(1)} %pad_add_fusion.5.here, f32[192,8192]{1,0:T(8,128)} %bitcast.81, f32[192,8192]{1,0:T(8,128)} %bitcast.82, f32[2,2,192,1024]{3,2,1,0:T(8,128)} %copy-done.9, f32[2,2,192,1024]{3,2,1,0:T(8,128)} %copy-done.9), custom_call_target="tpu_custom_call" | custom-call | flops 20000000000 | bytes 1000000 | tf_op jit(solution)/shard_map/add_split/pallas_call | solution.py:71
  26.7 3.2 %transposed_base.2 = f32[768,384]{1,0:T(8,128)S(1)} custom-call(s32[3]{0:T(128)S(1)} %pad_add_fusion.5.here, f32[2,2,2,384,768]{4,3,2,1,0:T(8,128)} %bitcast.70, f32[2,2,2,384,768]{4,3,2,1,0:T(8,128)} %bitcast.75), custom_call_target="tpu_custom_call" | custom-call | flops 20000000000 | bytes 1000000 | tf_op jit(solution)/shard_map/transposed_base/pallas_call | solution.py:71
  29.9 3.5 %transposed_base.3 = f32[768,512]{1,0:T(8,128)S(1)} custom-call(s32[3]{0:T(128)S(1)} %pad_add_fusion.5.here, f32[2,2,2,512,768]{4,3,2,1,0:T(8,128)} %bitcast.60, f32[2,2,2,512,768]{4,3,2,1,0:T(8,128)} %bitcast.65), custom_call_target="tpu_custom_call" | custom-call | flops 20000000000 | bytes 1000000 | tf_op jit(solution)/shard_map/transposed_base/pallas_call | solution.py:71
  36.0 7.7 %collective-permute-done.3 = f16[2,192,384]{2,1,0:T(8,128)(2,1)S(1)} collective-permute-done((f16[2,192,384]{2,1,0:T(8,128)(2,1)}, f16[2,192,384]{2,1,0:T(8,128)(2,1)S(1)}, u32[]{:S(2)}, u32[]{:S(2)}) %collective-permute-start.3) | collective-permute-done | bytes 294944 | tf_op jit(solution)/shard_map/expert_y/ppermute | solution.py:271
  45.6 2.6 %collective-permute-start.5 = (f16[192,384]{1,0:T(8,128)(2,1)S(1)}, f16[192,384]{1,0:T(8,128)(2,1)S(1)}, u32[]{:S(2)}, u32[]{:S(2)}) collective-permute-start(f16[192,384]{1,0:T(8,128)(2,1)S(1)} %get-tuple-element.231), channel_id=1, source_target_pairs={{0,4},{1,5},{2,6},{3,7},{4,0},{5,1},{6,2},{7,3},{8,12},{9,13},{10,... | collective-permute-start | bytes 442376 | tf_op jit(solution)/shard_map/expert_z2/ppermute | solution.py:271
  53.0 6.2 %collective-permute-done.5 = f16[192,384]{1,0:T(8,128)(2,1)S(1)} collective-permute-done((f16[192,384]{1,0:T(8,128)(2,1)S(1)}, f16[192,384]{1,0:T(8,128)(2,1)S(1)}, u32[]{:S(2)}, u32[]{:S(2)}) %collective-permute-start.5) | collective-permute-done | bytes 147488 | tf_op jit(solution)/shard_map/expert_z2/ppermute | solution.py:271
  60.4 2.3 %copy.26 = f16[384,768]{1,0:T(8,128)(2,1)} copy(f16[384,768]{0,1:T(8,128)(2,1)} %bitcast.59) | data formatting | bytes 1179648 | tf_op jit(solution)/shard_map/reshape | solution.py:363
  64.4 2.2 %convert_element_type.62.own_ref = f32[384,768]{1,0:T(8,128)} convert(f16[384,768]{1,0:T(8,128)(2,1)} %copy.26) | non-fusion elementwise | flops 294912 | bytes 1769472 | tf_op jit(solution)/shard_map/convert_element_type | solution.py:371
  66.8 2.6 %collective-permute-start.16 = (f16[192,512]{1,0:T(8,128)(2,1)S(1)}, f16[192,512]{1,0:T(8,128)(2,1)S(1)}, u32[]{:S(2)}, u32[]{:S(2)}) collective-permute-start(f16[192,512]{1,0:T(8,128)(2,1)S(1)} %get-tuple-element.221), channel_id=1, source_target_pairs={{0,6},{1,7},{2,4},{3,5},{4,2},{5,3},{6,0},{7,1},{8,14},{9,15},{10,... | collective-permute-start | bytes 589832 | tf_op jit(solution)/shard_map/table_z3/ppermute | solution.py:271
  71.7 2.9 %collective-permute-done.9 = f16[384,768]{1,0:T(8,128)(2,1)} collective-permute-done((f16[384,768]{1,0:T(8,128)(2,1)}, f16[384,768]{1,0:T(8,128)(2,1)}, u32[]{:S(2)}, u32[]{:S(2)}) %collective-permute-start.9) | collective-permute-done | bytes 589856 | tf_op jit(solution)/shard_map/expert_gather_x/ppermute | solution.py:271
  74.6 5.5 %collective-permute-start.15 = (f16[192,512]{1,0:T(8,128)(2,1)S(1)}, f16[192,512]{1,0:T(8,128)(2,1)S(1)}, u32[]{:S(2)}, u32[]{:S(2)}) collective-permute-start(f16[192,512]{1,0:T(8,128)(2,1)S(1)} %get-tuple-element.218), channel_id=1, source_target_pairs={{0,4},{1,5},{2,6},{3,7},{4,0},{5,1},{6,2},{7,3},{8,12},{9,13},{10,... | collective-permute-start | bytes 589832 | tf_op jit(solution)/shard_map/table_z2/ppermute | solution.py:271
  82.2 5.6 %update.8 = (f32[2,2,2,384,768]{4,3,2,1,0:T(8,128)}, f32[2,2,2,384,768]{4,3,2,1,0:T(8,128)}) custom-call(s32[3]{0:T(128)S(1)} %pad_add_fusion.5.here, f32[384,768]{1,0:T(8,128)} %convert_element_type.62.own_ref, f32[384,768]{1,0:T(8,128)} %convert_element_type.63.near_ref, f32[2,2,2,384,768]{4,3,2,1,0:T(8,128)} %bitcast.71, f32[2,2,2,384,768]{4,3,2,1,0:T(8,128)} %bitcast.76), custom_call_target="tpu_custom_call" | custom-call | flops 20000000000 | bytes 1000000 | tf_op jit(solution)/shard_map/update/pallas_call | solution.py:71
  94.0 4.2 %all-to-all-start = ((bf16[4,192,384]{2,1,0:T(8,128)(2,1)}), bf16[4,192,384]{2,1,0:T(8,128)(2,1)}, u32[]{:S(2)}, u32[]{:S(2)}) async-start(bf16[4,192,384]{2,1,0:T(8,128)(2,1)} %subtract_convert_fusion.1), calls=%async_computation | async-start | bytes 1179648 | tf_op jit(solution)/shard_map/expert_back_z/all_to_all | solution.py:284
  98.3 5.6 %update.9 = (f32[2,2,2,384,768]{4,3,2,1,0:T(8,128)}, f32[2,2,2,384,768]{4,3,2,1,0:T(8,128)}) custom-call(s32[3]{0:T(128)S(1)} %pad_add_fusion.4.here, f32[384,768]{1,0:T(8,128)} %collective-permute-done.12.own_ref, f32[384,768]{1,0:T(8,128)} %collective-permute-done.13.near_ref, ...), custom_call_target="tpu_custom_call", output_to_operand_aliasing={{0}: (5, {}), {1}: (6, {})} | custom-call | flops 20000000000 | bytes 1000000 | tf_op jit(solution)/shard_map/update/pallas_call | solution.py:71
  104.3 2.2 %convert_element_type.65.near_ref = f32[384,768]{1,0:T(8,128)} convert(f16[384,768]{1,0:T(8,128)(2,1)} %collective-permute-done.11) | non-fusion elementwise | flops 294912 | bytes 1769472 | tf_op jit(solution)/shard_map/convert_element_type | solution.py:378
  110.4 5.6 %update.10 = (f32[2,2,2,384,768]{4,3,2,1,0:T(8,128)}, f32[2,2,2,384,768]{4,3,2,1,0:T(8,128)}) custom-call(s32[3]{0:T(128)S(1)} %get-tuple-element.236.here, f32[384,768]{1,0:T(8,128)} %convert_element_type.64.own_ref, f32[384,768]{1,0:T(8,128)} %convert_element_type.65.near_ref, ...), custom_call_target="tpu_custom_call", output_to_operand_aliasing={{0}: (5, {}), {1}: (6, {})} | custom-call | flops 20000000000 | bytes 1000000 | tf_op jit(solution)/shard_map/update/pallas_call | solution.py:71
  117.1 4.5 %all-to-all-start.1 = ((bf16[4,192,512]{2,1,0:T(8,128)(2,1)}), bf16[4,192,512]{2,1,0:T(8,128)(2,1)}, u32[]{:S(2)}, u32[]{:S(2)}) async-start(bf16[4,192,512]{2,1,0:T(8,128)(2,1)} %subtract_convert_fusion), calls=%async_computation.1 | async-start | bytes 1572864 | tf_op jit(solution)/shard_map/table_back_z/all_to_all | solution.py:284
  126.1 5.6 %update.11 = (f32[2,2,2,384,768]{4,3,2,1,0:T(8,128)}, f32[2,2,2,384,768]{4,3,2,1,0:T(8,128)}) custom-call(s32[3]{0:T(128)S(1)} %get-tuple-element.237.here, f32[384,768]{1,0:T(8,128)} %collective-permute-done.17.own_ref, f32[384,768]{1,0:T(8,128)} %collective-permute-done.18.near_ref, ...), custom_call_target="tpu_custom_call", output_to_operand_aliasing={{0}: (5, {}), {1}: (6, {})} | custom-call | flops 20000000000 | bytes 1000000 | tf_op jit(solution)/shard_map/update/pallas_call | solution.py:71
  134.6 6.2 %update.12 = (f32[2,2,2,512,768]{4,3,2,1,0:T(8,128)}, f32[2,2,2,512,768]{4,3,2,1,0:T(8,128)}) custom-call(s32[3]{0:T(128)S(1)} %pad_add_fusion.5.here, f32[512,768]{1,0:T(8,128)S(1)} %convert_element_type.69.own_ref, f32[512,768]{1,0:T(8,128)} %copy-done.7, f32[2,2,2,512,768]{4,3,2,1,0:T(8,128)} %bitcast.61, f32[2,2,2,512,768]{4,3,2,1,0:T(8,128)} %bitcast.66), custom_call_target="tpu_custom_call" | custom-call | flops 20000000000 | bytes 1000000 | tf_op jit(solution)/shard_map/update/pallas_call | solution.py:71
  142.3 6.7 %update.13 = (f32[2,2,2,512,768]{4,3,2,1,0:T(8,128)}, f32[2,2,2,512,768]{4,3,2,1,0:T(8,128)}) custom-call(s32[3]{0:T(128)S(1)} %pad_add_fusion.4.here, f32[512,768]{1,0:T(8,128)} %collective-permute-done.27.own_ref, f32[512,768]{1,0:T(8,128)} %copy-done.11, f32[2,2,2,512,768]{4,3,2,1,0:T(8,128)} %bitcast.62, ...), custom_call_target="tpu_custom_call", output_to_operand_aliasing={{0}: (5, {}), {1}: (6, {})} | custom-call | flops 20000000000 | bytes 1000000 | tf_op jit(solution)/shard_map/update/pallas_call | solution.py:71
  153.5 3.9 %place.4.refs_4_ = bf16[2,2,192,1536]{3,2,1,0:T(8,128)(2,1)} custom-call(s32[3]{0:T(128)S(1)} %pad_add_fusion.5.here, bf16[2,192,384]{2,1,0:T(8,128)(2,1)S(1)} %get-tuple-element.182.refs_0_, bf16[2,192,384]{2,1,0:T(8,128)(2,1)S(1)} %collective-permute-done.22.refs_1_, bf16[2,192,384]{2,1,0:T(8,128)(2,1)S(1)} %collective-permute-done.23.refs_2_, ...), custom_call_target="tpu_custom_call" | custom-call | flops 20000000000 | bytes 1000000 | tf_op jit(solution)/shard_map/place/pallas_call | solution.py:71
  161.9 2.2 %place.5 = bf16[2,2,192,1536]{3,2,1,0:T(8,128)(2,1)} custom-call(s32[3]{0:T(128)S(1)} %pad_add_fusion.4.here, bf16[2,192,384]{2,1,0:T(8,128)(2,1)S(1)} %copy-done.1, bf16[2,192,384]{2,1,0:T(8,128)(2,1)S(1)} %collective-permute-done.24.refs_1_, bf16[2,192,384]{2,1,0:T(8,128)(2,1)S(1)} %collective-permute-done.29.refs_2_, ...), custom_call_target="tpu_custom_call", output_to_operand_aliasing={{}: (5, {})} | custom-call | flops 20000000000 | bytes 1000000 | tf_op jit(solution)/shard_map/place/pallas_call | solution.py:71
  164.1 6.9 %collective-permute-done.33.refs_2_ = bf16[2,192,512]{2,1,0:T(8,128)(2,1)S(1)} collective-permute-done((bf16[2,192,512]{2,1,0:T(8,128)(2,1)S(1)}, bf16[2,192,512]{2,1,0:T(8,128)(2,1)S(1)}, u32[]{:S(2)}, u32[]{:S(2)}) %collective-permute-start.33) | collective-permute-done | bytes 393248 | tf_op jit(solution)/shard_map/table_back_x/ppermute | solution.py:271
  172.0 6.3 %update.14 = (f32[2,2,2,512,768]{4,3,2,1,0:T(8,128)}, f32[2,2,2,512,768]{4,3,2,1,0:T(8,128)}) custom-call(s32[3]{0:T(128)S(1)} %get-tuple-element.236.here, f32[512,768]{1,0:T(8,128)S(1)} %convert_element_type.71.own_ref, f32[512,768]{1,0:T(8,128)} %copy-done.6, f32[2,2,2,512,768]{4,3,2,1,0:T(8,128)} %bitcast.63, ...), custom_call_target="tpu_custom_call", output_to_operand_aliasing={{0}: (5, {}), {1}: (6, {})} | custom-call | flops 20000000000 | bytes 1000000 | tf_op jit(solution)/shard_map/update/pallas_call | solution.py:71
  178.3 3.5 %collective-permute-done.35.refs_3_ = bf16[2,192,512]{2,1,0:T(8,128)(2,1)S(1)} collective-permute-done((bf16[2,192,512]{2,1,0:T(8,128)(2,1)S(1)}, bf16[2,192,512]{2,1,0:T(8,128)(2,1)S(1)}, u32[]{:S(2)}, u32[]{:S(2)}) %collective-permute-start.35) | collective-permute-done | bytes 393248 | tf_op jit(solution)/shard_map/table_back2_x/ppermute | solution.py:271
  183.4 6.3 %update.15 = (f32[2,2,2,512,768]{4,3,2,1,0:T(8,128)}, f32[2,2,2,512,768]{4,3,2,1,0:T(8,128)}) custom-call(s32[3]{0:T(128)S(1)} %get-tuple-element.237.here, f32[512,768]{1,0:T(8,128)S(1)} %collective-permute-done.31.own_ref, f32[512,768]{1,0:T(8,128)} %copy-done.10, f32[2,2,2,512,768]{4,3,2,1,0:T(8,128)} %bitcast.64, ...), custom_call_target="tpu_custom_call", output_to_operand_aliasing={{0}: (5, {}), {1}: (6, {})} | custom-call | flops 20000000000 | bytes 1000000 | tf_op jit(solution)/shard_map/update/pallas_call | solution.py:71
  189.7 2.3 %place.6.refs_4_ = bf16[192,8192]{1,0:T(8,128)(2,1)} custom-call(s32[3]{0:T(128)S(1)} %pad_add_fusion.5.here, bf16[2,192,512]{2,1,0:T(8,128)(2,1)S(1)} %get-tuple-element.204.refs_0_, bf16[2,192,512]{2,1,0:T(8,128)(2,1)S(1)} %collective-permute-done.34.refs_1_, bf16[2,192,512]{2,1,0:T(8,128)(2,1)S(1)} %collective-permute-done.33.refs_2_, ...), custom_call_target="tpu_custom_call" | custom-call | flops 20000000000 | bytes 1000000 | tf_op jit(solution)/shard_map/place/pallas_call | solution.py:71
  192.0 2.3 %place.7 = bf16[192,8192]{1,0:T(8,128)(2,1)} custom-call(s32[3]{0:T(128)S(1)} %pad_add_fusion.4.here, bf16[2,192,512]{2,1,0:T(8,128)(2,1)S(1)} %collective-permute-done.36.refs_0_, bf16[2,192,512]{2,1,0:T(8,128)(2,1)S(1)} %collective-permute-done.37.refs_1_, ...), custom_call_target="tpu_custom_call", output_to_operand_aliasing={{}: (5, {})} | custom-call | flops 20000000000 | bytes 1000000 | tf_op jit(solution)/shard_map/place/pallas_call | solution.py:71
  (123 shorter events, 53.0 us)
Async XLA Ops:
  15.3 18.1 %collective-permute-start.1 = (f16[2,192,768]{2,1,0:T(8,128)(2,1)S(1)}, f16[2,192,768]{2,1,0:T(8,128)(2,1)S(1)}, u32[]{:S(2)}, u32[]{:S(2)}) collective-permute-start(f16[2,192,768]{2,1,0:T(8,128)(2,1)S(1)} %multiply_convert_fusion.1), channel_id=1, source_target_pairs={{0,16},{1,17},{2,18},{3,19},{4,20},{5,21},{6,22},{7,23},{8,24},{9,... | collective-permute-start | bytes 1769480 | tf_op jit(solution)/shard_map/expert_x/ppermute | solution.py:271
  26.1 22.6 %collective-permute-start.7 = (f16[2,192,1024]{2,1,0:T(8,128)(2,1)}, f16[2,192,1024]{2,1,0:T(8,128)(2,1)}, u32[]{:S(2)}, u32[]{:S(2)}) collective-permute-start(f16[2,192,1024]{2,1,0:T(8,128)(2,1)} %multiply_convert_fusion), channel_id=1, source_target_pairs={{0,16},{1,17},{2,18},{3,19},{4,20},{5,21},{6,22},{7,23},{8,24},{9,... | collective-permute-start | bytes 2359304 | tf_op jit(solution)/shard_map/table_x/ppermute | solution.py:271
  45.6 13.7 %collective-permute-start.5 = (f16[192,384]{1,0:T(8,128)(2,1)S(1)}, f16[192,384]{1,0:T(8,128)(2,1)S(1)}, u32[]{:S(2)}, u32[]{:S(2)}) collective-permute-start(f16[192,384]{1,0:T(8,128)(2,1)S(1)} %get-tuple-element.231), channel_id=1, source_target_pairs={{0,4},{1,5},{2,6},{3,7},{4,0},{5,1},{6,2},{7,3},{8,12},{9,13},{10,... | collective-permute-start | bytes 442376 | tf_op jit(solution)/shard_map/expert_z2/ppermute | solution.py:271
  48.1 11.1 %collective-permute-start.6 = (f16[192,384]{1,0:T(8,128)(2,1)S(1)}, f16[192,384]{1,0:T(8,128)(2,1)S(1)}, u32[]{:S(2)}, u32[]{:S(2)}) collective-permute-start(f16[192,384]{1,0:T(8,128)(2,1)S(1)} %get-tuple-element.230), channel_id=1, source_target_pairs={{0,6},{1,7},{2,4},{3,5},{4,2},{5,3},{6,0},{7,1},{8,14},{9,15},{10,... | collective-permute-start | bytes 442376 | tf_op jit(solution)/shard_map/expert_z3/ppermute | solution.py:271
  51.2 15.3 %collective-permute-start.10 = (f16[2,192,512]{2,1,0:T(8,128)(2,1)}, f16[2,192,512]{2,1,0:T(8,128)(2,1)S(1)}, u32[]{:S(2)}, u32[]{:S(2)}) collective-permute-start(f16[2,192,512]{2,1,0:T(8,128)(2,1)} %get-tuple-element.223), channel_id=1, source_target_pairs={{0,1},{1,0},{2,3},{3,2},{4,5},{5,4},{6,7},{7,6},{8,9},{9,8},{10,11... | collective-permute-start | bytes 1179656 | tf_op jit(solution)/shard_map/table_y/ppermute | solution.py:271
  62.7 11.9 %collective-permute-start.9 = (f16[384,768]{1,0:T(8,128)(2,1)}, f16[384,768]{1,0:T(8,128)(2,1)}, u32[]{:S(2)}, u32[]{:S(2)}) collective-permute-start(f16[384,768]{1,0:T(8,128)(2,1)} %copy.26), channel_id=1, source_target_pairs={{0,16},{1,17},{2,18},{3,19},{4,20},{5,21},{6,22},{7,23},{8,24},{9,... | collective-permute-start | bytes 1769480 | tf_op jit(solution)/shard_map/expert_gather_x/ppermute | solution.py:271
  62.8 17.3 %collective-permute-start.8 = (f16[384,768]{1,0:T(8,128)(2,1)}, f16[384,768]{1,0:T(8,128)(2,1)}, u32[]{:S(2)}, u32[]{:S(2)}) collective-permute-start(f16[384,768]{1,0:T(8,128)(2,1)} %copy.26), channel_id=1, source_target_pairs={{0,1},{1,0},{2,3},{3,2},{4,5},{5,4},{6,7},{7,6},{8,9},{9,8},{10,11... | collective-permute-start | bytes 1769480 | tf_op jit(solution)/shard_map/expert_gather_y/ppermute | solution.py:271
  66.5 31.6 %collective-permute-start.12 = (f32[384,768]{1,0:T(8,128)}, f32[384,768]{1,0:T(8,128)}, u32[]{:S(2)}, u32[]{:S(2)}) collective-permute-start(f32[384,768]{1,0:T(8,128)} %convert_element_type.62.own_ref), channel_id=1, source_target_pairs={{0,8},{1,9},{2,10},{3,11},{4,12},{5,13},{6,14},{7,15},{8,0},{9,1},... | collective-permute-start | bytes 3538952 | tf_op jit(solution)/shard_map/expert_gather_core/ppermute | solution.py:271
  66.8 22.5 %collective-permute-start.16 = (f16[192,512]{1,0:T(8,128)(2,1)S(1)}, f16[192,512]{1,0:T(8,128)(2,1)S(1)}, u32[]{:S(2)}, u32[]{:S(2)}) collective-permute-start(f16[192,512]{1,0:T(8,128)(2,1)S(1)} %get-tuple-element.221), channel_id=1, source_target_pairs={{0,6},{1,7},{2,4},{3,5},{4,2},{5,3},{6,0},{7,1},{8,14},{9,15},{10,... | collective-permute-start | bytes 589832 | tf_op jit(solution)/shard_map/table_z3/ppermute | solution.py:271
  69.4 18.4 %collective-permute-start.14 = (f16[192,512]{1,0:T(8,128)(2,1)S(1)}, f16[192,512]{1,0:T(8,128)(2,1)S(1)}, u32[]{:S(2)}, u32[]{:S(2)}) collective-permute-start(f16[192,512]{1,0:T(8,128)(2,1)S(1)} %get-tuple-element.219), channel_id=1, source_target_pairs={{0,2},{1,3},{2,0},{3,1},{4,6},{5,7},{6,4},{7,5},{8,10},{9,11},{10,... | collective-permute-start | bytes 589832 | tf_op jit(solution)/shard_map/table_z1/ppermute | solution.py:271
  74.6 14.8 %collective-permute-start.15 = (f16[192,512]{1,0:T(8,128)(2,1)S(1)}, f16[192,512]{1,0:T(8,128)(2,1)S(1)}, u32[]{:S(2)}, u32[]{:S(2)}) collective-permute-start(f16[192,512]{1,0:T(8,128)(2,1)S(1)} %get-tuple-element.218), channel_id=1, source_target_pairs={{0,4},{1,5},{2,6},{3,7},{4,0},{5,1},{6,2},{7,3},{8,12},{9,13},{10,... | collective-permute-start | bytes 589832 | tf_op jit(solution)/shard_map/table_z2/ppermute | solution.py:271
  82.2 16.1 %collective-permute-start.13 = (f32[384,768]{1,0:T(8,128)}, f32[384,768]{1,0:T(8,128)}, u32[]{:S(2)}, u32[]{:S(2)}) collective-permute-start(f32[384,768]{1,0:T(8,128)} %convert_element_type.63.near_ref), channel_id=1, source_target_pairs={{0,8},{1,9},{2,10},{3,11},{4,12},{5,13},{6,14},{7,15},{8,0},{9,1},... | collective-permute-start | bytes 3538952 | tf_op jit(solution)/shard_map/expert_gather_core/ppermute | solution.py:271
  87.8 16.5 %collective-permute-start.11 = (f16[384,768]{1,0:T(8,128)(2,1)}, f16[384,768]{1,0:T(8,128)(2,1)}, u32[]{:S(2)}, u32[]{:S(2)}) collective-permute-start(f16[384,768]{1,0:T(8,128)(2,1)} %collective-permute-done.9), channel_id=1, source_target_pairs={{0,1},{1,0},{2,3},{3,2},{4,5},{5,4},{6,7},{7,6},{8,9},{9,8},{10,11... | collective-permute-start | bytes 1769480 | tf_op jit(solution)/shard_map/expert_gather2_y/ppermute | solution.py:271
  91.2 30.4 %collective-permute-start.19 = (f16[512,768]{1,0:T(8,128)(2,1)}, f16[512,768]{1,0:T(8,128)(2,1)}, u32[]{:S(2)}, u32[]{:S(2)}) collective-permute-start(f16[512,768]{1,0:T(8,128)(2,1)} %copy.29), channel_id=1, source_target_pairs={{0,16},{1,17},{2,18},{3,19},{4,20},{5,21},{6,22},{7,23},{8,24},{9,... | collective-permute-start | bytes 2359304 | tf_op jit(solution)/shard_map/table_gather_x/ppermute | solution.py:271
  92.2 31.0 %collective-permute-start.20 = (f16[512,768]{1,0:T(8,128)(2,1)}, f16[512,768]{1,0:T(8,128)(2,1)}, u32[]{:S(2)}, u32[]{:S(2)}) collective-permute-start(f16[512,768]{1,0:T(8,128)(2,1)} %copy.29), channel_id=1, source_target_pairs={{0,1},{1,0},{2,3},{3,2},{4,5},{5,4},{6,7},{7,6},{8,9},{9,8},{10,11... | collective-permute-start | bytes 2359304 | tf_op jit(solution)/shard_map/table_gather_y/ppermute | solution.py:271
  94.0 22.0 %all-to-all-start = ((bf16[4,192,384]{2,1,0:T(8,128)(2,1)}), bf16[4,192,384]{2,1,0:T(8,128)(2,1)}, u32[]{:S(2)}, u32[]{:S(2)}) async-start(bf16[4,192,384]{2,1,0:T(8,128)(2,1)} %subtract_convert_fusion.1), calls=%async_computation | async-start | bytes 1179648 | tf_op jit(solution)/shard_map/expert_back_z/all_to_all | solution.py:284
  98.2 42.7 %collective-permute-start.27 = (f32[512,768]{1,0:T(8,128)S(1)}, f32[512,768]{1,0:T(8,128)}, u32[]{:S(2)}, u32[]{:S(2)}) collective-permute-start(f32[512,768]{1,0:T(8,128)S(1)} %convert_element_type.69.own_ref), channel_id=1, source_target_pairs={{0,8},{1,9},{2,10},{3,11},{4,12},{5,13},{6,14},{7,15},{8,0},{9,1},... | collective-permute-start | bytes 4718600 | tf_op jit(solution)/shard_map/table_gather_core/ppermute | solution.py:271
  106.5 19.6 %collective-permute-start.18 = (f32[384,768]{1,0:T(8,128)}, f32[384,768]{1,0:T(8,128)}, u32[]{:S(2)}, u32[]{:S(2)}) collective-permute-start(f32[384,768]{1,0:T(8,128)} %convert_element_type.65.near_ref), channel_id=1, source_target_pairs={{0,8},{1,9},{2,10},{3,11},{4,12},{5,13},{6,14},{7,15},{8,0},{9,1},... | collective-permute-start | bytes 3538952 | tf_op jit(solution)/shard_map/expert_gather2_core/ppermute | solution.py:271
  108.7 16.3 %collective-permute-start.17 = (f32[384,768]{1,0:T(8,128)}, f32[384,768]{1,0:T(8,128)}, u32[]{:S(2)}, u32[]{:S(2)}) collective-permute-start(f32[384,768]{1,0:T(8,128)} %convert_element_type.64.own_ref), channel_id=1, source_target_pairs={{0,8},{1,9},{2,10},{3,11},{4,12},{5,13},{6,14},{7,15},{8,0},{9,1},... | collective-permute-start | bytes 3538952 | tf_op jit(solution)/shard_map/expert_gather2_core/ppermute | solution.py:271
  117.1 31.9 %all-to-all-start.1 = ((bf16[4,192,512]{2,1,0:T(8,128)(2,1)}), bf16[4,192,512]{2,1,0:T(8,128)(2,1)}, u32[]{:S(2)}, u32[]{:S(2)}) async-start(bf16[4,192,512]{2,1,0:T(8,128)(2,1)} %subtract_convert_fusion), calls=%async_computation.1 | async-start | bytes 1572864 | tf_op jit(solution)/shard_map/table_back_z/all_to_all | solution.py:284
  121.6 11.9 %collective-permute-start.22 = (bf16[2,192,384]{2,1,0:T(8,128)(2,1)S(1)}, bf16[2,192,384]{2,1,0:T(8,128)(2,1)S(1)}, u32[]{:S(2)}, u32[]{:S(2)}) collective-permute-start(bf16[2,192,384]{2,1,0:T(8,128)(2,1)S(1)} %get-tuple-element.225), channel_id=1, source_target_pairs={{0,1},{1,0},{2,3},{3,2},{4,5},{5,4},{6,7},{7,6},{8,9},{9,8},{10,11... | collective-permute-start | bytes 884744 | tf_op jit(solution)/shard_map/expert_back_y/ppermute | solution.py:271
  124.4 25.7 %collective-permute-start.26 = (f16[512,768]{1,0:T(8,128)(2,1)}, f16[512,768]{1,0:T(8,128)(2,1)}, u32[]{:S(2)}, u32[]{:S(2)}) collective-permute-start(f16[512,768]{1,0:T(8,128)(2,1)} %collective-permute-done.19), channel_id=1, source_target_pairs={{0,1},{1,0},{2,3},{3,2},{4,5},{5,4},{6,7},{7,6},{8,9},{9,8},{10,11... | collective-permute-start | bytes 2359304 | tf_op jit(solution)/shard_map/table_gather2_y/ppermute | solution.py:271
  126.1 15.1 %collective-permute-start.28 = (f32[512,768]{1,0:T(8,128)S(1)}, f32[512,768]{1,0:T(8,128)S(1)}, u32[]{:S(2)}, u32[]{:S(2)}) collective-permute-start(f32[512,768]{1,0:T(8,128)S(1)} %convert_element_type.68.near_ref), channel_id=1, source_target_pairs={{0,8},{1,9},{2,10},{3,11},{4,12},{5,13},{6,14},{7,15},{8,0},{9,1},... | collective-permute-start | bytes 4718600 | tf_op jit(solution)/shard_map/table_gather_core/ppermute | solution.py:271
  133.6 25.2 %collective-permute-start.21 = (bf16[2,192,384]{2,1,0:T(8,128)(2,1)S(1)}, bf16[2,192,384]{2,1,0:T(8,128)(2,1)S(1)}, u32[]{:S(2)}, u32[]{:S(2)}) collective-permute-start(bf16[2,192,384]{2,1,0:T(8,128)(2,1)S(1)} %get-tuple-element.182.refs_0_), channel_id=1, source_target_pairs={{0,8},{1,9},{2,10},{3,11},{4,12},{5,13},{6,14},{7,15},{8,0},{9,1},... | collective-permute-start | bytes 884744 | tf_op jit(solution)/shard_map/expert_back_core/ppermute | solution.py:271
  133.6 17.9 %collective-permute-start.25 = (bf16[2,192,384]{2,1,0:T(8,128)(2,1)S(1)}, bf16[2,192,384]{2,1,0:T(8,128)(2,1)}, u32[]{:S(2)}, u32[]{:S(2)}) collective-permute-start(bf16[2,192,384]{2,1,0:T(8,128)(2,1)S(1)} %collective-permute-done.22.refs_1_), channel_id=1, source_target_pairs={{0,16},{1,17},{2,18},{3,19},{4,20},{5,21},{6,22},{7,23},{8,24},{9,... | collective-permute-start | bytes 884744 | tf_op jit(solution)/shard_map/expert_back2_x/ppermute | solution.py:271
  140.9 18.6 %collective-permute-start.24 = (bf16[2,192,384]{2,1,0:T(8,128)(2,1)S(1)}, bf16[2,192,384]{2,1,0:T(8,128)(2,1)S(1)}, u32[]{:S(2)}, u32[]{:S(2)}) collective-permute-start(bf16[2,192,384]{2,1,0:T(8,128)(2,1)S(1)} %collective-permute-done.22.refs_1_), channel_id=1, source_target_pairs={{0,8},{1,9},{2,10},{3,11},{4,12},{5,13},{6,14},{7,15},{8,0},{9,1},... | collective-permute-start | bytes 884744 | tf_op jit(solution)/shard_map/expert_back2_core/ppermute | solution.py:271
  152.0 19.0 %collective-permute-start.34 = (bf16[2,192,512]{2,1,0:T(8,128)(2,1)S(1)}, bf16[2,192,512]{2,1,0:T(8,128)(2,1)S(1)}, u32[]{:S(2)}, u32[]{:S(2)}) collective-permute-start(bf16[2,192,512]{2,1,0:T(8,128)(2,1)S(1)} %get-tuple-element.213), channel_id=1, source_target_pairs={{0,1},{1,0},{2,3},{3,2},{4,5},{5,4},{6,7},{7,6},{8,9},{9,8},{10,11... | collective-permute-start | bytes 1179656 | tf_op jit(solution)/shard_map/table_back_y/ppermute | solution.py:271
  159.5 22.8 %collective-permute-start.32 = (f32[512,768]{1,0:T(8,128)S(1)}, f32[512,768]{1,0:T(8,128)S(1)}, u32[]{:S(2)}, u32[]{:S(2)}) collective-permute-start(f32[512,768]{1,0:T(8,128)S(1)} %convert_element_type.70.near_ref), channel_id=1, source_target_pairs={{0,8},{1,9},{2,10},{3,11},{4,12},{5,13},{6,14},{7,15},{8,0},{9,1},... | collective-permute-start | bytes 4718600 | tf_op jit(solution)/shard_map/table_gather2_core/ppermute | solution.py:271
  159.5 11.5 %collective-permute-start.33 = (bf16[2,192,512]{2,1,0:T(8,128)(2,1)S(1)}, bf16[2,192,512]{2,1,0:T(8,128)(2,1)S(1)}, u32[]{:S(2)}, u32[]{:S(2)}) collective-permute-start(bf16[2,192,512]{2,1,0:T(8,128)(2,1)S(1)} %get-tuple-element.204.refs_0_), channel_id=1, source_target_pairs={{0,16},{1,17},{2,18},{3,19},{4,20},{5,21},{6,22},{7,23},{8,24},{9,... | collective-permute-start | bytes 1179656 | tf_op jit(solution)/shard_map/table_back_x/ppermute | solution.py:271
  160.5 31.5 %collective-permute-start.36 = (bf16[2,192,512]{2,1,0:T(8,128)(2,1)S(1)}, bf16[2,192,512]{2,1,0:T(8,128)(2,1)S(1)}, u32[]{:S(2)}, u32[]{:S(2)}) collective-permute-start(bf16[2,192,512]{2,1,0:T(8,128)(2,1)S(1)} %get-tuple-element.204.refs_0_), channel_id=1, source_target_pairs={{0,8},{1,9},{2,10},{3,11},{4,12},{5,13},{6,14},{7,15},{8,0},{9,1},... | collective-permute-start | bytes 1179656 | tf_op jit(solution)/shard_map/table_back_core/ppermute | solution.py:271
  160.7 21.1 %collective-permute-start.31 = (f32[512,768]{1,0:T(8,128)S(1)}, f32[512,768]{1,0:T(8,128)S(1)}, u32[]{:S(2)}, u32[]{:S(2)}) collective-permute-start(f32[512,768]{1,0:T(8,128)S(1)} %convert_element_type.71.own_ref), channel_id=1, source_target_pairs={{0,8},{1,9},{2,10},{3,11},{4,12},{5,13},{6,14},{7,15},{8,0},{9,1},... | collective-permute-start | bytes 4718600 | tf_op jit(solution)/shard_map/table_gather2_core/ppermute | solution.py:271
  172.0 20.0 %collective-permute-start.37 = (bf16[2,192,512]{2,1,0:T(8,128)(2,1)S(1)}, bf16[2,192,512]{2,1,0:T(8,128)(2,1)S(1)}, u32[]{:S(2)}, u32[]{:S(2)}) collective-permute-start(bf16[2,192,512]{2,1,0:T(8,128)(2,1)S(1)} %collective-permute-done.34.refs_1_), channel_id=1, source_target_pairs={{0,8},{1,9},{2,10},{3,11},{4,12},{5,13},{6,14},{7,15},{8,0},{9,1},... | collective-permute-start | bytes 1179656 | tf_op jit(solution)/shard_map/table_back2_core/ppermute | solution.py:271
  (22 other events, 137.2 us)

commit v3 on v2

--- a/solution.py
+++ b/solution.py
@@ -2,6 +2,7 @@
 import jax.numpy as jnp
 from jax import lax
 from jax.experimental import pallas as pl
+from jax.experimental.layout import Layout, with_layout_constraint
 from jax.experimental.pallas import tpu as pltpu
 from jax.sharding import PartitionSpec as P
 
@@ -24,6 +25,8 @@
 
 
 class Table:
+    table = True
+
     def __init__(self, rows, width, half_shards, tensor):
         self.shape = (rows, half_shards * 4 * tensor * width)
         self.tensor, self.width = tensor, width
@@ -36,6 +39,8 @@
 
 
 class Expert:
+    table = False
+
     def __init__(self, rows, width, half_shards, tensor):
         self.shape = (2, 2, rows, half_shards * tensor * width)
         self.tensor, self.width = tensor, width
@@ -57,7 +62,7 @@
     return lax.dynamic_slice(value, start, shape).reshape(layout.shape[-2], layout.tensor * layout.width)
 
 
-def call(kernel, name, grid, scalars, inputs, outputs, aliases, cost):
+def call(kernel, name, grid, scalars, inputs, outputs, aliases):
     in_specs = [
         pl.BlockSpec(memory_space=pl.ANY) if block is None else pl.BlockSpec(block, at)
         for _, block, at in inputs
@@ -79,67 +84,79 @@
     )(scalars, *[array for array, _, _ in inputs])
 
 
-def pick(layout, value, here, half_shards):
-    rows, wide = layout.shape[-2], layout.tensor * layout.width
+def pick_table(layout, value, here, half_shards):
+    rows, wide = layout.shape[-2], 2 * layout.tensor * layout.width
     if not aligned(rows, layout.width):
-        parts = [cut(layout, value, here[0], x, a) for x in range(2) for a in range(half_shards)]
-        return jnp.stack(parts).reshape(2, half_shards, rows, wide)
+        parts = [cut(layout, value, here[0], x, a) for a in range(half_shards) for x in range(2)]
+        parts = [jnp.concatenate(parts[2 * a : 2 * a + 2], 1) for a in range(half_shards)]
+        return jnp.stack(parts)
 
     def kernel(here, value_ref, out_ref):
-        out_ref[...] = value_ref[...].reshape(out_ref.shape)
-
-    block = layout.block(0, 0, 0, None)[0]
+        out_ref[0] = value_ref[...]
+
     return call(
         kernel,
         "pick",
-        (2, half_shards),
+        (half_shards,),
         here,
-        [(value, block, lambda x, a, here: layout.block(here[0], x, a, None)[1])],
-        [((2, half_shards, rows, wide), value.dtype, (1, 1, rows, wide), lambda x, a, here: (x, a, 0, 0))],
+        [(value, (rows, wide), lambda a, here: (0, a * 2 + here[0]))],
+        [((half_shards, rows, wide), value.dtype, (1, rows, wide), lambda a, here: (a, 0, 0))],
         {},
-        2 * half_shards * rows * wide * 16,
     )[0]
 
 
 def add_split(layout, value, received, here, half_shards):
     rows, tensor, width = layout.shape[-2], layout.tensor, layout.width
+    wide = tensor * width
+
+    def got(x, a):
+        return (a, 0, x) if layout.table else (x, 0, a)
+
     if not aligned(rows, width):
         halves = []
         for x in (1 - here[1], here[1]):
-            own = jnp.stack([cut(layout, value, here[0], x, a) for a in range(half_shards)])
-            halves.append(own + lax.dynamic_index_in_dim(received, x, 0, False))
+            parts = []
+            for a in range(half_shards):
+                first, _, last = got(x, a)
+                part = lax.dynamic_slice(received, (first, 0, last * wide), (1, rows, wide))[0]
+                parts.append(part + cut(layout, value, here[0], x, a))
+            for y in (1 - here[2], here[2]):
+                halves.append(lax.dynamic_slice_in_dim(jnp.stack(parts), y * width, width, 2))
         return halves
 
-    def kernel(here, own_sent, own_kept, got_sent, got_kept, sent_ref, kept_ref):
-        shape = sent_ref.shape
-        sent_ref[...] = own_sent[...].reshape(shape) + got_sent[...].reshape(shape)
-        kept_ref[...] = own_kept[...].reshape(shape) + got_kept[...].reshape(shape)
-
-    block = layout.block(0, 0, 0, 0)[0]
-    got_block = (1, 1, rows, width)
-    out_block = (1, rows, width)
-    out_at = lambda a, h, here: (a, 0, h)
-    out = ((half_shards, rows, tensor * width), jnp.float32, out_block, out_at)
+    def kernel(here, own_sent, own_kept, got_sent, got_kept, *out_refs):
+        for y in range(tensor):
+
+            @pl.when(here[2] == y)
+            def _():
+                for j, (own, got) in enumerate(((own_sent, got_sent), (own_kept, got_kept))):
+                    lead = (0,) * (len(own.shape) - 2) + (slice(None),)
+                    for h in range(2):
+                        start = (y ^ h ^ 1) * width
+                        columns = slice(start, start + width)
+                        out_refs[2 * j + h][0] = own[lead + (columns,)] + got[0, :, columns]
+
+    block = layout.block(0, 0, 0, None)[0]
+    out = ((half_shards, rows, width), jnp.float32, (1, rows, width), lambda a, here: (a, 0, 0))
     return call(
         kernel,
         "add_split",
-        (half_shards, tensor),
+        (half_shards,),
         here,
         [
-            (value, block, lambda a, h, here: layout.block(here[0], 1 - here[1], a, h)[1]),
-            (value, block, lambda a, h, here: layout.block(here[0], here[1], a, h)[1]),
-            (received, got_block, lambda a, h, here: (1 - here[1], a, 0, h)),
-            (received, got_block, lambda a, h, here: (here[1], a, 0, h)),
+            (value, block, lambda a, here: layout.block(here[0], 1 - here[1], a, None)[1]),
+            (value, block, lambda a, here: layout.block(here[0], here[1], a, None)[1]),
+            (received, (1, rows, wide), lambda a, here: got(1 - here[1], a)),
+            (received, (1, rows, wide), lambda a, here: got(here[1], a)),
         ],
-        [out, out],
+        [out] * 4,
         {},
-        half_shards * rows * tensor * width * 24,
     )
 
 
 def transposed_base(master, moment, here):
     width, model = master.shape[-2:]
-    step = 128
+    step = 256 if width % 256 == 0 else width
     if not aligned(model, width):
         start, shape = (here[0], here[1], here[2], 0, 0), (1, 1, 1, width, model)
         base = lax.dynamic_slice(master, start, shape) - (
@@ -164,24 +181,26 @@
         [(master, block, at), (moment, block, at)],
         [((model, width), jnp.float32, (model, step), lambda i, here: (0, i))],
         {},
-        model * width * 12,
     )[0]
 
 
-def update(parts, master, moment, here, before):
+def update(stacks, master, moment, here, before):
     width, model = master.shape[-2:]
     if not aligned(model, width):
         weights, velocity = before or (jnp.zeros_like(master), jnp.zeros_like(moment))
-        for d in range(2):
-            start, shape = (here[0], here[1] ^ d, here[2], 0, 0), (1, 1, 1, width, model)
-            mean = parts[d].reshape(shape) * (1 / (4 * scale))
+        for d in range(2 * len(stacks)):
+            start = (here[0] ^ (d // 2), here[1] ^ (d % 2), here[2], 0, 0)
+            shape = (1, 1, 1, width, model)
+            mean = stacks[d // 2][d % 2].reshape(shape) * (1 / (4 * scale))
             new = momentum_coef * lax.dynamic_slice(moment, start, shape) + mean
             velocity = lax.dynamic_update_slice(velocity, new, start)
             new = lax.dynamic_slice(master, start, shape) - outer_rate * (mean + momentum_coef * new)
             weights = lax.dynamic_update_slice(weights, new, start)
         return weights, velocity
-
-    def kernel(here, own_ref, near_ref, master_ref, moment_ref, *refs):
+    count = len(stacks)
+
+    def kernel(here, *refs):
+        master_ref, moment_ref = refs[count : count + 2]
         weights_ref, velocity_ref = refs[-2:]
 
         def compute(summed_ref):
@@ -190,69 +209,71 @@
             velocity_ref[...] = velocity
             weights_ref[...] = master_ref[...] - outer_rate * (mean + momentum_coef * velocity)
 
-        @pl.when(pl.program_id(0) == 0)
-        def _():
-            compute(own_ref)
-
-        @pl.when(pl.program_id(0) == 1)
-        def _():
-            compute(near_ref)
-
-    at = lambda d, here: (here[0], here[1] ^ d, here[2], 0, 0)
+        if count == 1:
+            compute(refs[0])
+        else:
+            for j in range(count):
+                pl.when(pl.program_id(0) // 2 == j)(lambda: compute(refs[j]))
+
+    def stack_at(j):
+        return lambda d, here: (jnp.clip(d - 2 * j, 0, 1), 0, 0)
+
+    at = lambda d, here: (here[0] ^ (d // 2), here[1] ^ (d % 2), here[2], 0, 0)
     block = (1, 1, 1, width, model)
     out = (master.shape, jnp.float32, block, at)
-    inputs = [(part, (width, model), lambda d, here: (0, 0)) for part in parts]
+    inputs = [(stack, (1, width, model), stack_at(j)) for j, stack in enumerate(stacks)]
     inputs += [(master, block, at), (moment, block, at)]
     aliases = {}
     if before is not None:
         inputs += [(value, None, None) for value in before]
-        aliases = {5: 0, 6: 1}
-    return call(kernel, "update", (2,), here, inputs, [out, out], aliases, 2 * width * model * 20)
-
-
-def place(layout, parts, here, before, half_shards):
+        aliases = {count + 3: 0, count + 4: 1}
+    return call(kernel, "update", (2 * count,), here, inputs, [out, out], aliases)
+
+
+def place(layout, parts, here, half_shards):
     rows, width, tensor = layout.shape[-2], layout.width, layout.tensor
     if not aligned(rows, width):
-        result = jnp.zeros(layout.shape, jnp.bfloat16) if before is None else before
+        result = jnp.zeros(layout.shape, jnp.bfloat16)
         for j, part in enumerate(parts):
             for a in range(half_shards):
-                shape, at = layout.block(here[0], here[1] ^ (j // 2), a, here[2] ^ (j % 2))
+                at = here[0] ^ (j // 4), here[1] ^ (j // 2 % 2), a, here[2] ^ (j % 2)
+                shape, at = layout.block(*at)
                 start = [i * n for i, n in zip(at, shape)]
                 result = lax.dynamic_update_slice(result, part[a].reshape(shape), start)
         return result
 
     def kernel(here, *refs):
         out_ref = refs[-1]
-        lead = (0,) * (len(out_ref.shape) - 2)
-        for x in range(2):
+        for j in range(8):
             for y in range(tensor):
 
-                @pl.when((pl.program_id(0) == x) & (here[2] == y))
+                @pl.when(here[2] == y)
                 def _():
-                    for t in range(tensor):
-                        out_ref[lead + (slice(None), slice((y ^ t) * width, ((y ^ t) + 1) * width))] = refs[2 * x + t][0]
-
-    def part_at(x):
-        if x == 0:
-            return lambda d, a, here: (jnp.where(d == 0, a, half_shards - 1), 0, 0)
-        return lambda d, a, here: (jnp.where(d == 1, a, 0), 0, 0)
-
-    block = layout.block(0, 0, 0, None)[0]
-    out_at = lambda d, a, here: layout.block(here[0], here[1] ^ d, a, None)[1]
-    inputs = [(part, (1, rows, width), part_at(j // 2)) for j, part in enumerate(parts)]
-    aliases = {}
-    if before is not None:
-        inputs.append((before, None, None))
-        aliases = {5: 0}
+                    h = y ^ (j % 2)
+                    c, x = here[0] ^ (j // 4), here[1] ^ (j // 2 % 2)
+                    if layout.table:
+                        for place in range(4):
+
+                            @pl.when(c * 2 + x == place)
+                            def _():
+                                start = (place * tensor + h) * width
+                                out_ref[:, start : start + width] = refs[j][0]
+
+                    else:
+                        out_ref[c, x, :, h * width : (h + 1) * width] = refs[j][0]
+
+    if layout.table:
+        block, out_at = (rows, 4 * tensor * width), lambda a, here: (0, a)
+    else:
+        block, out_at = (2, 2, rows, tensor * width), lambda a, here: (0, 0, 0, a)
     return call(
         kernel,
         "place",
-        (2, half_shards),
+        (half_shards,),
         here,
-        inputs,
+        [(part, (1, rows, width), lambda a, here: (a, 0, 0)) for part in parts],
         [(layout.shape, jnp.bfloat16, block, out_at)],
-        aliases,
-        4 * half_shards * rows * width * 4,
+        {},
     )[0]
 
 
@@ -315,26 +336,41 @@
             shape = (2, 2, tensor, layout.width, model)
             self.master, self.moment = master.reshape(shape), moment.reshape(shape)
             self.result = None
+            self.split = False
 
         def start(self):
-            picked = mark(pick(self.layout, after(self.change), other, half_shards))
-            self.got = over_core(self.name, picked)
+            change = after(self.change)
+            if self.layout.table:
+                picked = pick_table(self.layout, change, other, half_shards)
+            else:
+                picked = index(change, 1 - core)
+            self.got = over_core(self.name, mark(picked))
 
         def sum_core(self):
             change, got = after(self.change, self.got)
-            sent, self.kept = add_split(self.layout, change, got, here, half_shards)
-            self.received = over_x(self.name, mark((sent * scale).astype(jnp.float16)))
+            sent = add_split(self.layout, change, got, here, half_shards)
+            self.kept = sent[2:]
+            far = mark((sent[0] * scale).astype(jnp.float16))
+            self.received = [over_x(self.name + "_far", far)]
+            self.sent_near = sent[1]
+
+        def send_near(self):
+            near = mark((after(self.sent_near) * scale).astype(jnp.float16))
+            self.received.append(over_x(self.name + "_near", near))
 
         def bases(self):
             master, moment = after(self.master, self.moment)
             self.base = mark(transposed_base(master, moment, here))
 
-        def sum_x(self):
-            kept, received = after(self.kept, self.received)
-            width = self.layout.width
-            total = (kept * scale + received.astype(jnp.float32)).astype(jnp.float16)
-            self.near = lax.dynamic_slice_in_dim(total, y * width, width, 2)
-            self.far = over_y(self.name, mark(lax.dynamic_slice_in_dim(total, (1 - y) * width, width, 2)))
+        def sum_half(self, i):
+            kept, received = after(self.kept[i], self.received[i])
+            return mark((kept * scale + received.astype(jnp.float32)).astype(jnp.float16))
+
+        def sum_far(self):
+            self.far = over_y(self.name, self.sum_half(0))
+
+        def sum_near(self):
+            self.near = self.sum_half(1)
 
         def scatter(self):
             near, far = after(self.near, self.far)
@@ -360,38 +396,41 @@
 
         def gather(self):
             self.received = received = jnp.stack(unmix(after(*self.sums)))
-            own = mark(jnp.transpose(received, (2, 0, 1)).reshape(received.shape[2], model))
+            own = jnp.transpose(received, (2, 0, 1)).reshape(received.shape[2], model)
+            own = mark(with_layout_constraint(own, Layout(major_to_minor=(0, 1))))
             self.near = over_x(self.name + "_gather", own)
             self.far = over_y(self.name + "_gather", own)
             self.own = own
 
         def gather_x(self):
             near = after(self.near)
-            self.far2 = over_y(self.name + "_gather2", near)
-            own, near = self.own.astype(jnp.float32), near.astype(jnp.float32)
-            mark(near)
-            self.pair = own, near
-            self.pair_core = over_core(self.name + "_gather", own), over_core(self.name + "_gather", near)
+            if self.split:
+                half = self.layout.width // 2
+                first, second = near[:half], self.far[half:]
+                mark(first)
+                second = mark(after(second))
+                self.far2 = over_y(self.name + "_gather2", first)
+                self.far2_x = over_x(self.name + "_gather2", second)
+            else:
+                self.far2 = over_y(self.name + "_gather2", near)
+            self.pair = mark(jnp.stack([self.own, after(near)]).astype(jnp.float32))
+            self.pair_core = over_core(self.name + "_gather", self.pair)
 
         def gather_y(self):
-            far, far2 = after(self.far, self.far2)
-            far, far2 = far.astype(jnp.float32), far2.astype(jnp.float32)
-            mark(far2)
-            self.far_pair = far, far2
-            self.far_core = over_core(self.name + "_gather2", far), over_core(self.name + "_gather2", far2)
+            far, *far2 = after(self.far, self.far2, *([self.far2_x] if self.split else []))
+            mark(far2[-1])
+            far2 = jnp.concatenate(far2)
+            self.far_pair = mark(jnp.stack([far, far2]).astype(jnp.float32))
+            self.far_core = over_core(self.name + "_gather2", self.far_pair)
 
         def wait(self, name):
             setattr(self, name, mark(after(getattr(self, name))))
 
-        def update(self, which):
-            parts, where = {
-                "pair": lambda: (self.pair, here),
-                "pair_core": lambda: (self.pair_core, other),
-                "far_pair": lambda: (self.far_pair, here_far),
-                "far_core": lambda: (self.far_core, other_far),
-            }[which]()
-            parts = after(*parts)
-            self.result = update(parts, self.master, self.moment, where, self.result)
+        def update(self, *which):
+            stacks = after(*[getattr(self, name) for name in which])
+            stacks = stacks if len(which) > 1 else (stacks,)
+            where = {"pair": here, "pair_core": other, "far_pair": here_far, "far_core": other_far}[which[0]]
+            self.result = update(stacks, self.master, self.moment, where, self.result)
             mark(self.result[0])
 
         def copies_y(self):
@@ -421,12 +460,8 @@
             ]
 
         def place(self):
-            parts = after(*self.parts)
-            self.copies = mark(place(self.layout, parts, here, None, half_shards))
-
-        def place_core(self):
-            parts = after(*self.parts_core)
-            self.copies = mark(place(self.layout, parts, other, self.copies, half_shards))
+            parts = after(*self.parts, *self.parts_core)
+            self.copies = mark(place(self.layout, parts, here, half_shards))
 
     t = Part(
         "table",
@@ -442,49 +477,54 @@
     e.start()
     t.start()
     e.sum_core()
+    e.send_near()
     t.sum_core()
+    e.sum_far()
+    t.send_near()
     e.bases()
+    e.sum_near()
+    e.scatter()
+    t.sum_far()
     t.bases()
-    e.sum_x()
-    e.scatter()
-    t.sum_x()
     e.gather()
+    t.sum_near()
     t.scatter()
     e.low_part()
+    e.copies_z()
     e.wait("near")
     e.wait("far")
     e.gather_x()
     e.update("pair")
-    t.gather()
-    e.copies_z()
-    e.update("pair_core")
     e.wait("far2")
     e.gather_y()
+    e.copies_y()
+    t.gather()
     t.low_part()
+    e.update("pair_core")
     e.update("far_pair")
-    e.copies_y()
-    t.copies_z()
+    e.update("far_core")
     t.wait("near")
     t.wait("far")
+    e.wait("low_far")
+    e.wait("low_near_x")
     t.gather_x()
-    e.update("far_core")
-    e.wait("low_near_x")
     e.copies_x()
+    t.copies_z()
     t.update("pair")
     t.update("pair_core")
+    t.wait("far2")
+    e.wait("low_far_x")
+    t.gather_y()
     t.copies_y()
-    t.wait("far2")
-    t.gather_y()
+    t.update("far_pair")
+    t.wait("low_near_x")
+    t.wait("low_far")
+    t.copies_x()
     e.copies_core()
+    t.update("far_core")
+    t.copies_core()
     e.place()
-    e.place_core()
-    t.wait("low_near_x")
-    t.copies_x()
-    t.update("far_pair")
-    t.copies_core()
-    t.update("far_core")
     t.place()
-    t.place_core()
     return (
         e.result[0].reshape(expert_master.shape),
         e.result[1].reshape(expert_master.shape),

time: 195 us -> 172 us (0.88)
  Pallas kernels: 84.2 us -> 71.1 us
  waiting for transfers between devices: 30.1 us -> 21.2 us
  local copies, waits for them, and re-layouts: 13.4 us -> 7.84 us
  starting transfers between devices: 44.6 us -> 49.2 us
    ppermute x40 -> x38, waiting for transfers between devices: 30.1 us -> 14.8 us  [send(): return lax.ppermute(value, axes, pairs(sizes, move))]
    pallas_call x18 -> x15, Pallas kernels: 84.2 us -> 71.1 us  [call(): pl.pallas_call(kernel, grid_spec=grid_spec, out_shape=[jax.ShapeDtypeStru...]
    all_to_all x2, waiting for transfers between devices: 0.01 us -> 6.46 us  [over_z(): lax.all_to_all(value, 'shard', split_axis=0, concat_axis=0, tiled=True)]
    ppermute x40 -> x38, starting transfers between devices: 35.9 us -> 41.2 us  [send(): return lax.ppermute(value, axes, pairs(sizes, move))]
    unnamed x24 -> x20, local copies, waits for them, and re-layouts: 5.68 us -> 2.63 us
    convert_element_type x12, other arithmetic: 16.5 us -> 14.1 us  [the longest x2 6.1 us: gather_x(): self.pair = mark(jnp.stack([self.own, after(near)]).astype(jnp.float32))]
    select_n x2, other arithmetic: 0.45 us -> 2.41 us  [of_shard(): return jnp.where(s // half_shards == y, index(near, a), index(far, a))]
  transfers between devices with their start and end apart: 42 -> 40, of which waited for: 8 -> 13; matrix products, arithmetic and copies ran while one was open for 15% -> 12% of each run, Pallas kernels for 40% -> 39%
where the time goes in v3:
time: 172 us; the launch traced here: 171 us
  Pallas kernels  71.1 us (41%)
  starting transfers between devices  49.2 us (29%)
  waiting for transfers between devices  21.2 us (12%)
  other arithmetic  20.8 us (12%)
  local copies, waits for them, and re-layouts  7.84 us (5%)
    pallas_call x15, Pallas kernels, call(): pl.pallas_call(kernel, grid_spec=grid_spec, out_shape=[jax.ShapeDtypeStru...  71.1 us
    ppermute x38, starting transfers between devices, send(): return lax.ppermute(value, axes, pairs(sizes, move))  41.2 us
    ppermute x38, waiting for transfers between devices, send(): return lax.ppermute(value, axes, pairs(sizes, move))  14.8 us
    all_to_all x2, starting transfers between devices, over_z(): lax.all_to_all(value, 'shard', split_axis=0, concat_axis=0, tiled=True)  8.06 us
    all_to_all x2, waiting for transfers between devices, over_z(): lax.all_to_all(value, 'shard', split_axis=0, concat_axis=0, tiled=True)  6.46 us
    convert_element_type x2, other arithmetic, gather_x(): self.pair = mark(jnp.stack([self.own, after(near)]).astype(jnp.float32))  6.1 us
    convert_element_type x2, other arithmetic, gather_y(): self.far_pair = mark(jnp.stack([far, far2]).astype(jnp.float32))  4.55 us
  transfers between devices with their start and end apart: 40, of which 13 were waited for; matrix products, arithmetic and copies ran while one was open for 12% of the time, Pallas kernels for 39%

profile of v3, /device:TPU:0, one launch (start us, length us, event | category | flops | bytes accessed | tf_op | source)
XLA Modules:
  0.0 171.1 jit_solution(13844975124337417548)
XLA Ops:
  3.1 3.7 %pick.1 = f32[2,192,2048]{2,1,0:T(8,128)} custom-call(s32[3]{0:T(128)S(1)} %pad_add_fusion.4.here, f32[192,8192]{1,0:T(8,128)} %bitcast.97), custom_call_target="tpu_custom_call" | custom-call | flops 20000000000 | bytes 1000000 | tf_op jit(solution)/shard_map/pick/pallas_call | solution.py:76
  7.3 3.7 %add_split.2 = (f32[2,192,384]{2,1,0:T(8,128)S(1)}, f32[2,192,384]{2,1,0:T(8,128)S(1)}, f32[2,192,384]{2,1,0:T(8,128)S(1)}, f32[2,192,384]{2,1,0:T(8,128)}) custom-call(s32[3]{0:T(128)S(1)} %pad_add_fusion.5.here, f32[2,2,192,1536]{3,2,1,0:T(8,128)} %bitcast.72, f32[2,2,192,1536]{3,2,1,0:T(8,128)} %bitcast.73, ...), custom_call_target="tpu_custom_call" | custom-call | flops 20000000000 | bytes 1000000 | tf_op jit(solution)/shard_map/add_split/pallas_call | solution.py:76
  11.1 2.9 %collective-permute-start.3 = (f16[2,192,384]{2,1,0:T(8,128)(2,1)S(1)}, f16[2,192,384]{2,1,0:T(8,128)(2,1)S(1)}, u32[]{:S(2)}, u32[]{:S(2)}) collective-permute-start(f16[2,192,384]{2,1,0:T(8,128)(2,1)S(1)} %multiply_convert_fusion.3), channel_id=1, source_target_pairs={{0,16},{1,17},{2,18},{3,19},{4,20},{5,21},{6,22},{7,23},{8,24},{9,... | collective-permute-start | bytes 884744 | tf_op jit(solution)/shard_map/expert_far_x/ppermute | solution.py:292
  14.2 4.4 %add_split.3 = (f32[2,192,512]{2,1,0:T(8,128)S(1)}, f32[2,192,512]{2,1,0:T(8,128)S(1)}, f32[2,192,512]{2,1,0:T(8,128)}, f32[2,192,512]{2,1,0:T(8,128)}) custom-call(s32[3]{0:T(128)S(1)} %pad_add_fusion.5.here, f32[192,8192]{1,0:T(8,128)} %bitcast.98, f32[192,8192]{1,0:T(8,128)} %bitcast.99, f32[2,192,2048]{2,1,0:T(8,128)} %collective-permute-done.2.got_sent.got_kept, ...), custom_call_target="tpu_custom_call" | custom-call | flops 20000000000 | bytes 1000000 | tf_op jit(solution)/shard_map/add_split/pallas_call | solution.py:76
  18.7 2.1 %collective-permute-start.8 = (f16[2,192,512]{2,1,0:T(8,128)(2,1)S(1)}, f16[2,192,512]{2,1,0:T(8,128)(2,1)S(1)}, u32[]{:S(2)}, u32[]{:S(2)}) collective-permute-start(f16[2,192,512]{2,1,0:T(8,128)(2,1)S(1)} %multiply_convert_fusion.1), channel_id=1, source_target_pairs={{0,16},{1,17},{2,18},{3,19},{4,20},{5,21},{6,22},{7,23},{8,24},{9,... | collective-permute-start | bytes 1179656 | tf_op jit(solution)/shard_map/table_far_x/ppermute | solution.py:292
  21.9 2.1 %collective-permute-start.4 = (f16[2,192,384]{2,1,0:T(8,128)(2,1)S(1)}, f16[2,192,384]{2,1,0:T(8,128)(2,1)S(1)}, u32[]{:S(2)}, u32[]{:S(2)}) collective-permute-start(f16[2,192,384]{2,1,0:T(8,128)(2,1)S(1)} %add_convert_fusion.3), channel_id=1, source_target_pairs={{0,1},{1,0},{2,3},{3,2},{4,5},{5,4},{6,7},{7,6},{8,9},{9,8},{10,11... | collective-permute-start | bytes 884744 | tf_op jit(solution)/shard_map/expert_y/ppermute | solution.py:292
  26.3 2.5 %transposed_base.2 = f32[768,384]{1,0:T(8,128)S(1)} custom-call(s32[3]{0:T(128)S(1)} %pad_add_fusion.5.here, f32[2,2,2,384,768]{4,3,2,1,0:T(8,128)} %bitcast.87, f32[2,2,2,384,768]{4,3,2,1,0:T(8,128)} %bitcast.92), custom_call_target="tpu_custom_call" | custom-call | flops 20000000000 | bytes 1000000 | tf_op jit(solution)/shard_map/transposed_base/pallas_call | solution.py:76
  31.8 2.6 %collective-permute-start.6 = (f16[192,384]{1,0:T(8,128)(2,1)S(1)}, f16[192,384]{1,0:T(8,128)(2,1)S(1)}, u32[]{:S(2)}, u32[]{:S(2)}) collective-permute-start(f16[192,384]{1,0:T(8,128)(2,1)S(1)} %get-tuple-element.239), channel_id=1, source_target_pairs={{0,4},{1,5},{2,6},{3,7},{4,0},{5,1},{6,2},{7,3},{8,12},{9,13},{10,... | collective-permute-start | bytes 442376 | tf_op jit(solution)/shard_map/expert_z2/ppermute | solution.py:292
  37.4 2.1 %collective-permute-start.12 = (f16[2,192,512]{2,1,0:T(8,128)(2,1)}, f16[2,192,512]{2,1,0:T(8,128)(2,1)}, u32[]{:S(2)}, u32[]{:S(2)}) collective-permute-start(f16[2,192,512]{2,1,0:T(8,128)(2,1)} %add_convert_fusion.1), channel_id=1, source_target_pairs={{0,1},{1,0},{2,3},{3,2},{4,5},{5,4},{6,7},{7,6},{8,9},{9,8},{10,11... | collective-permute-start | bytes 1179656 | tf_op jit(solution)/shard_map/table_y/ppermute | solution.py:292
  39.5 2.7 %transposed_base.3 = f32[768,512]{1,0:T(8,128)S(1)} custom-call(s32[3]{0:T(128)S(1)} %pad_add_fusion.5.here, f32[2,2,2,512,768]{4,3,2,1,0:T(8,128)} %bitcast.77, f32[2,2,2,512,768]{4,3,2,1,0:T(8,128)} %bitcast.82), custom_call_target="tpu_custom_call" | custom-call | flops 20000000000 | bytes 1000000 | tf_op jit(solution)/shard_map/transposed_base/pallas_call | solution.py:76
  49.6 2.2 %select_bitcast_fusion.4 = (f16[192,512]{1,0:T(8,128)(2,1)}, f16[192,512]{1,0:T(8,128)(2,1)}, f16[192,512]{1,0:T(8,128)(2,1)S(1)}, f16[192,512]{1,0:T(8,128)(2,1)}) fusion(f16[2,192,512]{2,1,0:T(8,128)(2,1)} %collective-permute-done.12, s32[]{:T(128)S(6)} %select_n.257, f16[2,192,512]{2,1,0:T(8,128)(2,1)S(1)} %add_convert_fusion, pred[]{:T(512)S(6)} %eq.28, ...), kind=kLoop, calls=%fused_computation.21 | loop fusion | flops 393216 | bytes 2359316 | tf_op jit(solution)/shard_map/jit(_where)/select_n | solution.py:380
  51.9 3.3 %collective-permute-start.18 = (f16[192,512]{1,0:T(8,128)(2,1)}, f16[192,512]{1,0:T(8,128)(2,1)}, u32[]{:S(2)}, u32[]{:S(2)}) collective-permute-start(f16[192,512]{1,0:T(8,128)(2,1)} %get-tuple-element.231), channel_id=1, source_target_pairs={{0,6},{1,7},{2,4},{3,5},{4,2},{5,3},{6,0},{7,1},{8,14},{9,15},{10,... | collective-permute-start | bytes 589832 | tf_op jit(solution)/shard_map/table_z3/ppermute | solution.py:292
  56.2 3.5 %all-to-all-start = ((bf16[4,192,384]{2,1,0:T(8,128)(2,1)}), bf16[4,192,384]{2,1,0:T(8,128)(2,1)S(1)}, u32[]{:S(2)}, u32[]{:S(2)}) async-start(bf16[4,192,384]{2,1,0:T(8,128)(2,1)} %subtract_convert_fusion.1), calls=%async_computation | async-start | bytes 1179648 | tf_op jit(solution)/shard_map/expert_back_z/all_to_all | solution.py:305
  61.7 2.4 %collective-permute-start.17 = (f16[192,512]{1,0:T(8,128)(2,1)}, f16[192,512]{1,0:T(8,128)(2,1)S(1)}, u32[]{:S(2)}, u32[]{:S(2)}) collective-permute-start(f16[192,512]{1,0:T(8,128)(2,1)} %get-tuple-element.228), channel_id=1, source_target_pairs={{0,4},{1,5},{2,6},{3,7},{4,0},{5,1},{6,2},{7,3},{8,12},{9,13},{10,... | collective-permute-start | bytes 589832 | tf_op jit(solution)/shard_map/table_z2/ppermute | solution.py:292
  64.1 2.5 %collective-permute-start.13 = (f16[384,768]{1,0:T(8,128)(2,1)}, f16[384,768]{1,0:T(8,128)(2,1)S(1)}, u32[]{:S(2)}, u32[]{:S(2)}) collective-permute-start(f16[384,768]{1,0:T(8,128)(2,1)} %collective-permute-done.10), channel_id=1, source_target_pairs={{0,1},{1,0},{2,3},{3,2},{4,5},{5,4},{6,7},{7,6},{8,9},{9,8},{10,11... | collective-permute-start | bytes 1769480 | tf_op jit(solution)/shard_map/expert_gather2_y/ppermute | solution.py:292
  66.5 2.8 %maximum_convert_fusion.2.refs_0_ = f32[2,384,768]{2,1,0:T(8,128)} fusion(f16[1,384,768]{2,1,0:T(8,128)(2,1)} %bitcast.25, f16[1,384,768]{2,1,0:T(8,128)(2,1)} %bitcast.70), kind=kLoop, calls=%fused_computation.4 | loop fusion | flops 1179648 | bytes 3538944 | tf_op jit(solution)/shard_map/convert_element_type | solution.py:416
  69.4 5.3 %update.8 = (f32[2,2,2,384,768]{4,3,2,1,0:T(8,128)}, f32[2,2,2,384,768]{4,3,2,1,0:T(8,128)}) custom-call(s32[3]{0:T(128)S(1)} %pad_add_fusion.5.here, f32[2,384,768]{2,1,0:T(8,128)} %maximum_convert_fusion.2.refs_0_, f32[2,2,2,384,768]{4,3,2,1,0:T(8,128)} %bitcast.88, f32[2,2,2,384,768]{4,3,2,1,0:T(8,128)} %bitcast.93), custom_call_target="tpu_custom_call" | custom-call | flops 20000000000 | bytes 1000000 | tf_op jit(solution)/shard_map/update/pallas_call | solution.py:76
  74.7 2.6 %maximum_convert_fusion.3.refs_0_ = f32[2,384,768]{2,1,0:T(8,128)} fusion(f16[1,384,768]{2,1,0:T(8,128)(2,1)S(1)} %bitcast.76, f16[1,384,768]{2,1,0:T(8,128)(2,1)} %bitcast.26), kind=kLoop, calls=%fused_computation.5 | loop fusion | flops 1179648 | bytes 3538944 | tf_op jit(solution)/shard_map/convert_element_type | solution.py:423
  77.8 2.2 %all-to-all-done = bf16[4,192,384]{2,1,0:T(8,128)(2,1)S(1)} async-done(((bf16[4,192,384]{2,1,0:T(8,128)(2,1)}), bf16[4,192,384]{2,1,0:T(8,128)(2,1)S(1)}, u32[]{:S(2)}, u32[]{:S(2)}) %all-to-all-start) | async-done | bytes 589856 | tf_op jit(solution)/shard_map/expert_back_z/all_to_all | solution.py:305
  91.3 5.3 %update.9 = (f32[2,2,2,384,768]{4,3,2,1,0:T(8,128)}, f32[2,2,2,384,768]{4,3,2,1,0:T(8,128)}) custom-call(s32[3]{0:T(128)S(1)} %pad_add_fusion.4.here, f32[2,384,768]{2,1,0:T(8,128)} %collective-permute-done.15.refs_0_, f32[2,2,2,384,768]{4,3,2,1,0:T(8,128)} %bitcast.89, ...), custom_call_target="tpu_custom_call", output_to_operand_aliasing={{0}: (4, {}), {1}: (5, {})} | custom-call | flops 20000000000 | bytes 1000000 | tf_op jit(solution)/shard_map/update/pallas_call | solution.py:76
  96.6 5.3 %update.10 = (f32[2,2,2,384,768]{4,3,2,1,0:T(8,128)}, f32[2,2,2,384,768]{4,3,2,1,0:T(8,128)}) custom-call(s32[3]{0:T(128)S(1)} %get-tuple-element.242.here, f32[2,384,768]{2,1,0:T(8,128)} %maximum_convert_fusion.3.refs_0_, f32[2,2,2,384,768]{4,3,2,1,0:T(8,128)} %bitcast.90, ...), custom_call_target="tpu_custom_call", output_to_operand_aliasing={{0}: (4, {}), {1}: (5, {})} | custom-call | flops 20000000000 | bytes 1000000 | tf_op jit(solution)/shard_map/update/pallas_call | solution.py:76
  101.9 5.3 %update.11 = (f32[2,2,2,384,768]{4,3,2,1,0:T(8,128)}, f32[2,2,2,384,768]{4,3,2,1,0:T(8,128)}) custom-call(s32[3]{0:T(128)S(1)} %get-tuple-element.243.here, f32[2,384,768]{2,1,0:T(8,128)} %collective-permute-done.14.refs_0_, f32[2,2,2,384,768]{4,3,2,1,0:T(8,128)} %bitcast.91, ...), custom_call_target="tpu_custom_call", output_to_operand_aliasing={{0}: (4, {}), {1}: (5, {})} | custom-call | flops 20000000000 | bytes 1000000 | tf_op jit(solution)/shard_map/update/pallas_call | solution.py:76
  107.7 3.8 %collective-permute-done.19.refs_1_ = bf16[2,192,384]{2,1,0:T(8,128)(2,1)S(1)} collective-permute-done((bf16[2,192,384]{2,1,0:T(8,128)(2,1)}, bf16[2,192,384]{2,1,0:T(8,128)(2,1)S(1)}, u32[]{:S(2)}, u32[]{:S(2)}) %collective-permute-start.19) | collective-permute-done | bytes 294944 | tf_op jit(solution)/shard_map/expert_back_y/ppermute | solution.py:292
  111.5 3.3 %maximum_convert_fusion.refs_0_ = f32[2,512,768]{2,1,0:T(8,128)} fusion(f16[1,512,768]{2,1,0:T(8,128)(2,1)} %bitcast.41, f16[1,512,768]{2,1,0:T(8,128)(2,1)} %bitcast.40), kind=kLoop, calls=%fused_computation.1 | loop fusion | flops 1572864 | bytes 4718592 | tf_op jit(solution)/shard_map/convert_element_type | solution.py:416
  116.8 4.6 %all-to-all-start.1 = ((bf16[4,192,512]{2,1,0:T(8,128)(2,1)}), bf16[4,192,512]{2,1,0:T(8,128)(2,1)S(1)}, u32[]{:S(2)}, u32[]{:S(2)}) async-start(bf16[4,192,512]{2,1,0:T(8,128)(2,1)} %subtract_convert_fusion), calls=%async_computation.1 | async-start | bytes 1572864 | tf_op jit(solution)/shard_map/table_back_z/all_to_all | solution.py:305
  121.4 6.4 %update.12 = (f32[2,2,2,512,768]{4,3,2,1,0:T(8,128)}, f32[2,2,2,512,768]{4,3,2,1,0:T(8,128)}) custom-call(s32[3]{0:T(128)S(1)} %pad_add_fusion.5.here, f32[2,512,768]{2,1,0:T(8,128)} %maximum_convert_fusion.refs_0_, f32[2,2,2,512,768]{4,3,2,1,0:T(8,128)} %bitcast.78, f32[2,2,2,512,768]{4,3,2,1,0:T(8,128)} %bitcast.83), custom_call_target="tpu_custom_call" | custom-call | flops 20000000000 | bytes 1000000 | tf_op jit(solution)/shard_map/update/pallas_call | solution.py:76
  127.8 6.5 %update.13 = (f32[2,2,2,512,768]{4,3,2,1,0:T(8,128)}, f32[2,2,2,512,768]{4,3,2,1,0:T(8,128)}) custom-call(s32[3]{0:T(128)S(1)} %pad_add_fusion.4.here, f32[2,512,768]{2,1,0:T(8,128)} %collective-permute-done.25.refs_0_, f32[2,2,2,512,768]{4,3,2,1,0:T(8,128)} %bitcast.79, ...), custom_call_target="tpu_custom_call", output_to_operand_aliasing={{0}: (4, {}), {1}: (5, {})} | custom-call | flops 20000000000 | bytes 1000000 | tf_op jit(solution)/shard_map/update/pallas_call | solution.py:76
  137.3 4.3 %all-to-all-done.1 = bf16[4,192,512]{2,1,0:T(8,128)(2,1)S(1)} async-done(((bf16[4,192,512]{2,1,0:T(8,128)(2,1)}), bf16[4,192,512]{2,1,0:T(8,128)(2,1)S(1)}, u32[]{:S(2)}, u32[]{:S(2)}) %all-to-all-start.1) | async-done | bytes 786464 | tf_op jit(solution)/shard_map/table_back_z/all_to_all | solution.py:305
  143.8 6.4 %update.14 = (f32[2,2,2,512,768]{4,3,2,1,0:T(8,128)}, f32[2,2,2,512,768]{4,3,2,1,0:T(8,128)}) custom-call(s32[3]{0:T(128)S(1)} %get-tuple-element.242.here, f32[2,512,768]{2,1,0:T(8,128)} %maximum_convert_fusion.1.refs_0_, f32[2,2,2,512,768]{4,3,2,1,0:T(8,128)} %bitcast.80, ...), custom_call_target="tpu_custom_call", output_to_operand_aliasing={{0}: (4, {}), {1}: (5, {})} | custom-call | flops 20000000000 | bytes 1000000 | tf_op jit(solution)/shard_map/update/pallas_call | solution.py:76
  154.1 6.4 %update.15 = (f32[2,2,2,512,768]{4,3,2,1,0:T(8,128)}, f32[2,2,2,512,768]{4,3,2,1,0:T(8,128)}) custom-call(s32[3]{0:T(128)S(1)} %get-tuple-element.243.here, f32[2,512,768]{2,1,0:T(8,128)} %collective-permute-done.33.refs_0_, f32[2,2,2,512,768]{4,3,2,1,0:T(8,128)} %bitcast.81, ...), custom_call_target="tpu_custom_call", output_to_operand_aliasing={{0}: (4, {}), {1}: (5, {})} | custom-call | flops 20000000000 | bytes 1000000 | tf_op jit(solution)/shard_map/update/pallas_call | solution.py:76
  162.5 3.2 %place.2 = bf16[2,2,192,1536]{3,2,1,0:T(8,128)(2,1)} custom-call(s32[3]{0:T(128)S(1)} %pad_add_fusion.5.here, bf16[2,192,384]{2,1,0:T(8,128)(2,1)S(1)} %get-tuple-element.204.refs_0_, bf16[2,192,384]{2,1,0:T(8,128)(2,1)S(1)} %collective-permute-done.19.refs_1_, bf16[2,192,384]{2,1,0:T(8,128)(2,1)S(1)} %collective-permute-done.22.refs_2_, ...), custom_call_target="tpu_custom_call" | custom-call | flops 20000000000 | bytes 1000000 | tf_op jit(solution)/shard_map/place/pallas_call | solution.py:76
  167.4 3.7 %place.3 = bf16[192,8192]{1,0:T(8,128)(2,1)} custom-call(s32[3]{0:T(128)S(1)} %pad_add_fusion.5.here, bf16[2,192,512]{2,1,0:T(8,128)(2,1)S(1)} %get-tuple-element.214.refs_0_, bf16[2,192,512]{2,1,0:T(8,128)(2,1)S(1)} %collective-permute-done.26.refs_1_, bf16[2,192,512]{2,1,0:T(8,128)(2,1)S(1)} %collective-permute-done.27.refs_2_, ...), custom_call_target="tpu_custom_call" | custom-call | flops 20000000000 | bytes 1000000 | tf_op jit(solution)/shard_map/place/pallas_call | solution.py:76
  (111 shorter events, 49.8 us)
Async XLA Ops:
  11.1 10.7 %collective-permute-start.3 = (f16[2,192,384]{2,1,0:T(8,128)(2,1)S(1)}, f16[2,192,384]{2,1,0:T(8,128)(2,1)S(1)}, u32[]{:S(2)}, u32[]{:S(2)}) collective-permute-start(f16[2,192,384]{2,1,0:T(8,128)(2,1)S(1)} %multiply_convert_fusion.3), channel_id=1, source_target_pairs={{0,16},{1,17},{2,18},{3,19},{4,20},{5,21},{6,22},{7,23},{8,24},{9,... | collective-permute-start | bytes 884744 | tf_op jit(solution)/shard_map/expert_far_x/ppermute | solution.py:292
  14.1 14.8 %collective-permute-start.1 = (f16[2,192,384]{2,1,0:T(8,128)(2,1)S(1)}, f16[2,192,384]{2,1,0:T(8,128)(2,1)S(1)}, u32[]{:S(2)}, u32[]{:S(2)}) collective-permute-start(f16[2,192,384]{2,1,0:T(8,128)(2,1)S(1)} %multiply_convert_fusion.2), channel_id=1, source_target_pairs={{0,16},{1,17},{2,18},{3,19},{4,20},{5,21},{6,22},{7,23},{8,24},{9,... | collective-permute-start | bytes 884744 | tf_op jit(solution)/shard_map/expert_near_x/ppermute | solution.py:292
  18.7 17.9 %collective-permute-start.8 = (f16[2,192,512]{2,1,0:T(8,128)(2,1)S(1)}, f16[2,192,512]{2,1,0:T(8,128)(2,1)S(1)}, u32[]{:S(2)}, u32[]{:S(2)}) collective-permute-start(f16[2,192,512]{2,1,0:T(8,128)(2,1)S(1)} %multiply_convert_fusion.1), channel_id=1, source_target_pairs={{0,16},{1,17},{2,18},{3,19},{4,20},{5,21},{6,22},{7,23},{8,24},{9,... | collective-permute-start | bytes 1179656 | tf_op jit(solution)/shard_map/table_far_x/ppermute | solution.py:292
  24.9 23.4 %collective-permute-start.11 = (f16[2,192,512]{2,1,0:T(8,128)(2,1)}, f16[2,192,512]{2,1,0:T(8,128)(2,1)}, u32[]{:S(2)}, u32[]{:S(2)}) collective-permute-start(f16[2,192,512]{2,1,0:T(8,128)(2,1)} %multiply_convert_fusion), channel_id=1, source_target_pairs={{0,16},{1,17},{2,18},{3,19},{4,20},{5,21},{6,22},{7,23},{8,24},{9,... | collective-permute-start | bytes 1179656 | tf_op jit(solution)/shard_map/table_near_x/ppermute | solution.py:292
  30.2 12.0 %collective-permute-start.5 = (f16[192,384]{1,0:T(8,128)(2,1)S(1)}, f16[192,384]{1,0:T(8,128)(2,1)S(1)}, u32[]{:S(2)}, u32[]{:S(2)}) collective-permute-start(f16[192,384]{1,0:T(8,128)(2,1)S(1)} %get-tuple-element.240), channel_id=1, source_target_pairs={{0,2},{1,3},{2,0},{3,1},{4,6},{5,7},{6,4},{7,5},{8,10},{9,11},{10,... | collective-permute-start | bytes 442376 | tf_op jit(solution)/shard_map/expert_z1/ppermute | solution.py:292
  31.8 11.9 %collective-permute-start.6 = (f16[192,384]{1,0:T(8,128)(2,1)S(1)}, f16[192,384]{1,0:T(8,128)(2,1)S(1)}, u32[]{:S(2)}, u32[]{:S(2)}) collective-permute-start(f16[192,384]{1,0:T(8,128)(2,1)S(1)} %get-tuple-element.239), channel_id=1, source_target_pairs={{0,4},{1,5},{2,6},{3,7},{4,0},{5,1},{6,2},{7,3},{8,12},{9,13},{10,... | collective-permute-start | bytes 442376 | tf_op jit(solution)/shard_map/expert_z2/ppermute | solution.py:292
  34.4 9.3 %collective-permute-start.7 = (f16[192,384]{1,0:T(8,128)(2,1)S(1)}, f16[192,384]{1,0:T(8,128)(2,1)S(1)}, u32[]{:S(2)}, u32[]{:S(2)}) collective-permute-start(f16[192,384]{1,0:T(8,128)(2,1)S(1)} %get-tuple-element.238), channel_id=1, source_target_pairs={{0,6},{1,7},{2,4},{3,5},{4,2},{5,3},{6,0},{7,1},{8,14},{9,15},{10,... | collective-permute-start | bytes 442376 | tf_op jit(solution)/shard_map/expert_z3/ppermute | solution.py:292
  37.4 12.2 %collective-permute-start.12 = (f16[2,192,512]{2,1,0:T(8,128)(2,1)}, f16[2,192,512]{2,1,0:T(8,128)(2,1)}, u32[]{:S(2)}, u32[]{:S(2)}) collective-permute-start(f16[2,192,512]{2,1,0:T(8,128)(2,1)} %add_convert_fusion.1), channel_id=1, source_target_pairs={{0,1},{1,0},{2,3},{3,2},{4,5},{5,4},{6,7},{7,6},{8,9},{9,8},{10,11... | collective-permute-start | bytes 1179656 | tf_op jit(solution)/shard_map/table_y/ppermute | solution.py:292
  45.2 18.8 %collective-permute-start.10 = (f16[384,768]{1,0:T(8,128)(2,1)}, f16[384,768]{1,0:T(8,128)(2,1)}, u32[]{:S(2)}, u32[]{:S(2)}) collective-permute-start(f16[384,768]{1,0:T(8,128)(2,1)} %copy.24), channel_id=1, source_target_pairs={{0,16},{1,17},{2,18},{3,19},{4,20},{5,21},{6,22},{7,23},{8,24},{9,... | collective-permute-start | bytes 1769480 | tf_op jit(solution)/shard_map/expert_gather_x/ppermute | solution.py:292
  46.7 17.3 %collective-permute-start.9 = (f16[384,768]{1,0:T(8,128)(2,1)}, f16[384,768]{1,0:T(8,128)(2,1)}, u32[]{:S(2)}, u32[]{:S(2)}) collective-permute-start(f16[384,768]{1,0:T(8,128)(2,1)} %copy.24), channel_id=1, source_target_pairs={{0,1},{1,0},{2,3},{3,2},{4,5},{5,4},{6,7},{7,6},{8,9},{9,8},{10,11... | collective-permute-start | bytes 1769480 | tf_op jit(solution)/shard_map/expert_gather_y/ppermute | solution.py:292
  51.9 30.6 %collective-permute-start.18 = (f16[192,512]{1,0:T(8,128)(2,1)}, f16[192,512]{1,0:T(8,128)(2,1)}, u32[]{:S(2)}, u32[]{:S(2)}) collective-permute-start(f16[192,512]{1,0:T(8,128)(2,1)} %get-tuple-element.231), channel_id=1, source_target_pairs={{0,6},{1,7},{2,4},{3,5},{4,2},{5,3},{6,0},{7,1},{8,14},{9,15},{10,... | collective-permute-start | bytes 589832 | tf_op jit(solution)/shard_map/table_z3/ppermute | solution.py:292
  56.2 23.9 %all-to-all-start = ((bf16[4,192,384]{2,1,0:T(8,128)(2,1)}), bf16[4,192,384]{2,1,0:T(8,128)(2,1)S(1)}, u32[]{:S(2)}, u32[]{:S(2)}) async-start(bf16[4,192,384]{2,1,0:T(8,128)(2,1)} %subtract_convert_fusion.1), calls=%async_computation | async-start | bytes 1179648 | tf_op jit(solution)/shard_map/expert_back_z/all_to_all | solution.py:305
  59.7 21.1 %collective-permute-start.16 = (f16[192,512]{1,0:T(8,128)(2,1)}, f16[192,512]{1,0:T(8,128)(2,1)S(1)}, u32[]{:S(2)}, u32[]{:S(2)}) collective-permute-start(f16[192,512]{1,0:T(8,128)(2,1)} %get-tuple-element.229), channel_id=1, source_target_pairs={{0,2},{1,3},{2,0},{3,1},{4,6},{5,7},{6,4},{7,5},{8,10},{9,11},{10,... | collective-permute-start | bytes 589832 | tf_op jit(solution)/shard_map/table_z1/ppermute | solution.py:292
  61.7 20.8 %collective-permute-start.17 = (f16[192,512]{1,0:T(8,128)(2,1)}, f16[192,512]{1,0:T(8,128)(2,1)S(1)}, u32[]{:S(2)}, u32[]{:S(2)}) collective-permute-start(f16[192,512]{1,0:T(8,128)(2,1)} %get-tuple-element.228), channel_id=1, source_target_pairs={{0,4},{1,5},{2,6},{3,7},{4,0},{5,1},{6,2},{7,3},{8,12},{9,13},{10,... | collective-permute-start | bytes 589832 | tf_op jit(solution)/shard_map/table_z2/ppermute | solution.py:292
  64.1 10.6 %collective-permute-start.13 = (f16[384,768]{1,0:T(8,128)(2,1)}, f16[384,768]{1,0:T(8,128)(2,1)S(1)}, u32[]{:S(2)}, u32[]{:S(2)}) collective-permute-start(f16[384,768]{1,0:T(8,128)(2,1)} %collective-permute-done.10), channel_id=1, source_target_pairs={{0,1},{1,0},{2,3},{3,2},{4,5},{5,4},{6,7},{7,6},{8,9},{9,8},{10,11... | collective-permute-start | bytes 1769480 | tf_op jit(solution)/shard_map/expert_gather2_y/ppermute | solution.py:292
  69.4 20.8 %collective-permute-start.15 = (f32[2,384,768]{2,1,0:T(8,128)}, f32[2,384,768]{2,1,0:T(8,128)}, u32[]{:S(2)}, u32[]{:S(2)}) collective-permute-start(f32[2,384,768]{2,1,0:T(8,128)} %maximum_convert_fusion.2.refs_0_), channel_id=1, source_target_pairs={{0,8},{1,9},{2,10},{3,11},{4,12},{5,13},{6,14},{7,15},{8,0},{9,1},... | collective-permute-start | bytes 7077896 | tf_op jit(solution)/shard_map/expert_gather_core/ppermute | solution.py:292
  77.3 24.6 %collective-permute-start.14 = (f32[2,384,768]{2,1,0:T(8,128)}, f32[2,384,768]{2,1,0:T(8,128)}, u32[]{:S(2)}, u32[]{:S(2)}) collective-permute-start(f32[2,384,768]{2,1,0:T(8,128)} %maximum_convert_fusion.3.refs_0_), channel_id=1, source_target_pairs={{0,8},{1,9},{2,10},{3,11},{4,12},{5,13},{6,14},{7,15},{8,0},{9,1},... | collective-permute-start | bytes 7077896 | tf_op jit(solution)/shard_map/expert_gather2_core/ppermute | solution.py:292
  86.0 21.2 %collective-permute-start.21 = (f16[512,768]{1,0:T(8,128)(2,1)}, f16[512,768]{1,0:T(8,128)(2,1)}, u32[]{:S(2)}, u32[]{:S(2)}) collective-permute-start(f16[512,768]{1,0:T(8,128)(2,1)} %copy.25), channel_id=1, source_target_pairs={{0,16},{1,17},{2,18},{3,19},{4,20},{5,21},{6,22},{7,23},{8,24},{9,... | collective-permute-start | bytes 2359304 | tf_op jit(solution)/shard_map/table_gather_x/ppermute | solution.py:292
  87.0 20.7 %collective-permute-start.20 = (f16[512,768]{1,0:T(8,128)(2,1)}, f16[512,768]{1,0:T(8,128)(2,1)S(1)}, u32[]{:S(2)}, u32[]{:S(2)}) collective-permute-start(f16[512,768]{1,0:T(8,128)(2,1)} %copy.25), channel_id=1, source_target_pairs={{0,1},{1,0},{2,3},{3,2},{4,5},{5,4},{6,7},{7,6},{8,9},{9,8},{10,11... | collective-permute-start | bytes 2359304 | tf_op jit(solution)/shard_map/table_gather_y/ppermute | solution.py:292
  88.1 23.4 %collective-permute-start.19 = (bf16[2,192,384]{2,1,0:T(8,128)(2,1)}, bf16[2,192,384]{2,1,0:T(8,128)(2,1)S(1)}, u32[]{:S(2)}, u32[]{:S(2)}) collective-permute-start(bf16[2,192,384]{2,1,0:T(8,128)(2,1)} %get-tuple-element.233), channel_id=1, source_target_pairs={{0,1},{1,0},{2,3},{3,2},{4,5},{5,4},{6,7},{7,6},{8,9},{9,8},{10,11... | collective-permute-start | bytes 884744 | tf_op jit(solution)/shard_map/expert_back_y/ppermute | solution.py:292
  90.2 21.3 %collective-permute-start.22 = (bf16[2,192,384]{2,1,0:T(8,128)(2,1)S(1)}, bf16[2,192,384]{2,1,0:T(8,128)(2,1)S(1)}, u32[]{:S(2)}, u32[]{:S(2)}) collective-permute-start(bf16[2,192,384]{2,1,0:T(8,128)(2,1)S(1)} %get-tuple-element.204.refs_0_), channel_id=1, source_target_pairs={{0,16},{1,17},{2,18},{3,19},{4,20},{5,21},{6,22},{7,23},{8,24},{9,... | collective-permute-start | bytes 884744 | tf_op jit(solution)/shard_map/expert_back_x/ppermute | solution.py:292
  114.7 13.1 %collective-permute-start.25 = (f32[2,512,768]{2,1,0:T(8,128)}, f32[2,512,768]{2,1,0:T(8,128)}, u32[]{:S(2)}, u32[]{:S(2)}) collective-permute-start(f32[2,512,768]{2,1,0:T(8,128)} %maximum_convert_fusion.refs_0_), channel_id=1, source_target_pairs={{0,8},{1,9},{2,10},{3,11},{4,12},{5,13},{6,14},{7,15},{8,0},{9,1},... | collective-permute-start | bytes 9437192 | tf_op jit(solution)/shard_map/table_gather_core/ppermute | solution.py:292
  114.7 20.2 %collective-permute-start.24 = (f16[512,768]{1,0:T(8,128)(2,1)}, f16[512,768]{1,0:T(8,128)(2,1)S(1)}, u32[]{:S(2)}, u32[]{:S(2)}) collective-permute-start(f16[512,768]{1,0:T(8,128)(2,1)} %collective-permute-done.21), channel_id=1, source_target_pairs={{0,1},{1,0},{2,3},{3,2},{4,5},{5,4},{6,7},{7,6},{8,9},{9,8},{10,11... | collective-permute-start | bytes 2359304 | tf_op jit(solution)/shard_map/table_gather2_y/ppermute | solution.py:292
  115.4 19.5 %collective-permute-start.23 = (bf16[2,192,384]{2,1,0:T(8,128)(2,1)S(1)}, bf16[2,192,384]{2,1,0:T(8,128)(2,1)S(1)}, u32[]{:S(2)}, u32[]{:S(2)}) collective-permute-start(bf16[2,192,384]{2,1,0:T(8,128)(2,1)S(1)} %collective-permute-done.19.refs_1_), channel_id=1, source_target_pairs={{0,16},{1,17},{2,18},{3,19},{4,20},{5,21},{6,22},{7,23},{8,24},{9,... | collective-permute-start | bytes 884744 | tf_op jit(solution)/shard_map/expert_back2_x/ppermute | solution.py:292
  116.8 24.8 %all-to-all-start.1 = ((bf16[4,192,512]{2,1,0:T(8,128)(2,1)}), bf16[4,192,512]{2,1,0:T(8,128)(2,1)S(1)}, u32[]{:S(2)}, u32[]{:S(2)}) async-start(bf16[4,192,512]{2,1,0:T(8,128)(2,1)} %subtract_convert_fusion), calls=%async_computation.1 | async-start | bytes 1572864 | tf_op jit(solution)/shard_map/table_back_z/all_to_all | solution.py:305
  136.8 16.8 %collective-permute-start.33 = (f32[2,512,768]{2,1,0:T(8,128)}, f32[2,512,768]{2,1,0:T(8,128)}, u32[]{:S(2)}, u32[]{:S(2)}) collective-permute-start(f32[2,512,768]{2,1,0:T(8,128)} %maximum_convert_fusion.1.refs_0_), channel_id=1, source_target_pairs={{0,8},{1,9},{2,10},{3,11},{4,12},{5,13},{6,14},{7,15},{8,0},{9,1},... | collective-permute-start | bytes 9437192 | tf_op jit(solution)/shard_map/table_gather2_core/ppermute | solution.py:292
  136.8 24.3 %collective-permute-start.28 = (bf16[2,192,384]{2,1,0:T(8,128)(2,1)S(1)}, bf16[2,192,384]{2,1,0:T(8,128)(2,1)S(1)}, u32[]{:S(2)}, u32[]{:S(2)}) collective-permute-start(bf16[2,192,384]{2,1,0:T(8,128)(2,1)S(1)} %get-tuple-element.204.refs_0_), channel_id=1, source_target_pairs={{0,8},{1,9},{2,10},{3,11},{4,12},{5,13},{6,14},{7,15},{8,0},{9,1},... | collective-permute-start | bytes 884744 | tf_op jit(solution)/shard_map/expert_back_core/ppermute | solution.py:292
  137.3 24.3 %collective-permute-start.29 = (bf16[2,192,384]{2,1,0:T(8,128)(2,1)S(1)}, bf16[2,192,384]{2,1,0:T(8,128)(2,1)S(1)}, u32[]{:S(2)}, u32[]{:S(2)}) collective-permute-start(bf16[2,192,384]{2,1,0:T(8,128)(2,1)S(1)} %collective-permute-done.19.refs_1_), channel_id=1, source_target_pairs={{0,8},{1,9},{2,10},{3,11},{4,12},{5,13},{6,14},{7,15},{8,0},{9,1},... | collective-permute-start | bytes 884744 | tf_op jit(solution)/shard_map/expert_back2_core/ppermute | solution.py:292
  141.6 10.6 %collective-permute-start.26 = (bf16[2,192,512]{2,1,0:T(8,128)(2,1)S(1)}, bf16[2,192,512]{2,1,0:T(8,128)(2,1)S(1)}, u32[]{:S(2)}, u32[]{:S(2)}) collective-permute-start(bf16[2,192,512]{2,1,0:T(8,128)(2,1)S(1)} %get-tuple-element.223), channel_id=1, source_target_pairs={{0,1},{1,0},{2,3},{3,2},{4,5},{5,4},{6,7},{7,6},{8,9},{9,8},{10,11... | collective-permute-start | bytes 1179656 | tf_op jit(solution)/shard_map/table_back_y/ppermute | solution.py:292
  142.4 9.8 %collective-permute-start.27 = (bf16[2,192,512]{2,1,0:T(8,128)(2,1)S(1)}, bf16[2,192,512]{2,1,0:T(8,128)(2,1)S(1)}, u32[]{:S(2)}, u32[]{:S(2)}) collective-permute-start(bf16[2,192,512]{2,1,0:T(8,128)(2,1)S(1)} %get-tuple-element.214.refs_0_), channel_id=1, source_target_pairs={{0,16},{1,17},{2,18},{3,19},{4,20},{5,21},{6,22},{7,23},{8,24},{9,... | collective-permute-start | bytes 1179656 | tf_op jit(solution)/shard_map/table_back_x/ppermute | solution.py:292
  152.2 8.9 %collective-permute-start.32 = (bf16[2,192,512]{2,1,0:T(8,128)(2,1)S(1)}, bf16[2,192,512]{2,1,0:T(8,128)(2,1)S(1)}, u32[]{:S(2)}, u32[]{:S(2)}) collective-permute-start(bf16[2,192,512]{2,1,0:T(8,128)(2,1)S(1)} %collective-permute-done.26.refs_1_), channel_id=1, source_target_pairs={{0,16},{1,17},{2,18},{3,19},{4,20},{5,21},{6,22},{7,23},{8,24},{9,... | collective-permute-start | bytes 1179656 | tf_op jit(solution)/shard_map/table_back2_x/ppermute | solution.py:292
  153.6 8.1 %collective-permute-start.30 = (bf16[2,192,384]{2,1,0:T(8,128)(2,1)S(1)}, bf16[2,192,384]{2,1,0:T(8,128)(2,1)S(1)}, u32[]{:S(2)}, u32[]{:S(2)}) collective-permute-start(bf16[2,192,384]{2,1,0:T(8,128)(2,1)S(1)} %collective-permute-done.22.refs_2_), channel_id=1, source_target_pairs={{0,8},{1,9},{2,10},{3,11},{4,12},{5,13},{6,14},{7,15},{8,0},{9,1},... | collective-permute-start | bytes 884744 | tf_op jit(solution)/shard_map/expert_back_core/ppermute | solution.py:292
  (18 other events, 74.7 us)

commit v4 on v3

--- a/solution.py
+++ b/solution.py
@@ -336,7 +336,6 @@
             shape = (2, 2, tensor, layout.width, model)
             self.master, self.moment = master.reshape(shape), moment.reshape(shape)
             self.result = None
-            self.split = False
 
         def start(self):
             change = after(self.change)
@@ -404,22 +403,12 @@
 
         def gather_x(self):
             near = after(self.near)
-            if self.split:
-                half = self.layout.width // 2
-                first, second = near[:half], self.far[half:]
-                mark(first)
-                second = mark(after(second))
-                self.far2 = over_y(self.name + "_gather2", first)
-                self.far2_x = over_x(self.name + "_gather2", second)
-            else:
-                self.far2 = over_y(self.name + "_gather2", near)
-            self.pair = mark(jnp.stack([self.own, after(near)]).astype(jnp.float32))
+            self.far2 = over_y(self.name + "_gather2", near)
+            self.pair = mark(jnp.stack([self.own, near]).astype(jnp.float32))
             self.pair_core = over_core(self.name + "_gather", self.pair)
 
         def gather_y(self):
-            far, *far2 = after(self.far, self.far2, *([self.far2_x] if self.split else []))
-            mark(far2[-1])
-            far2 = jnp.concatenate(far2)
+            far, far2 = after(self.far, self.far2)
             self.far_pair = mark(jnp.stack([far, far2]).astype(jnp.float32))
             self.far_core = over_core(self.name + "_gather2", self.far_pair)
 
@@ -440,24 +429,22 @@
             self.low_near = near
             self.low_far = over_y(self.name + "_back", far)
             self.low_near_x = over_x(self.name + "_back", near)
-            self.low_near_core = over_core(self.name + "_back", near)
 
         def copies_x(self):
-            far = mark(after(self.low_far))
-            self.low_far = far
+            far, near_x = after(self.low_far, self.low_near_x)
+            mark(far)
             self.low_far_x = over_x(self.name + "_back2", far)
-            self.low_far_core = over_core(self.name + "_back2", far)
+            self.parts = [self.low_near, far, near_x]
+            self.parts_core = [over_core(self.name + "_back", part) for part in self.parts]
 
         def copies_core(self):
-            near_x, far_x = after(self.low_near_x, self.low_far_x)
-            mark(far_x)
-            self.parts = [self.low_near, self.low_far, near_x, far_x]
-            self.parts_core = [
-                self.low_near_core,
-                self.low_far_core,
-                over_core(self.name + "_back", near_x),
-                over_core(self.name + "_back2", far_x),
-            ]
+            far_x = mark(after(self.low_far_x))
+            self.parts.append(far_x)
+            self.parts_core.append(over_core(self.name + "_back2", far_x))
+
+        def wait_core(self):
+            self.parts_core = list(after(*self.parts_core))
+            mark(self.parts_core[-1])
 
         def place(self):
             parts = after(*self.parts, *self.parts_core)
@@ -500,6 +487,7 @@
     e.copies_y()
     t.gather()
     t.low_part()
+    t.copies_z()
     e.update("pair_core")
     e.update("far_pair")
     e.update("far_core")
@@ -507,23 +495,26 @@
     t.wait("far")
     e.wait("low_far")
     e.wait("low_near_x")
+    t.wait("low")
     t.gather_x()
     e.copies_x()
-    t.copies_z()
     t.update("pair")
     t.update("pair_core")
     t.wait("far2")
+    e.wait_core()
     e.wait("low_far_x")
     t.gather_y()
+    e.copies_core()
     t.copies_y()
     t.update("far_pair")
     t.wait("low_near_x")
     t.wait("low_far")
     t.copies_x()
-    e.copies_core()
     t.update("far_core")
+    e.place()
+    t.wait_core()
+    t.wait("low_far_x")
     t.copies_core()
-    e.place()
     t.place()
     return (
         e.result[0].reshape(expert_master.shape),

time: 172 us -> 168 us (0.977)
  other arithmetic: 20.8 us -> 19 us
    all_to_all x2, waiting for transfers between devices: 6.46 us -> 3.67 us  [over_z(): lax.all_to_all(value, 'shard', split_axis=0, concat_axis=0, tiled=True)]
  transfers between devices with their start and end apart: 40 -> 40, of which waited for: 13 -> 11; matrix products, arithmetic and copies ran while one was open for 12% -> 11% of each run, Pallas kernels for 39% -> 40%
where the time goes in v4:
time: 168 us; the launch traced here: 167 us
  Pallas kernels  71.1 us (42%)
  starting transfers between devices  48.8 us (29%)
  waiting for transfers between devices  20.1 us (12%)
  other arithmetic  19 us (11%)
  local copies, waits for them, and re-layouts  7.4 us (4%)
    pallas_call x15, Pallas kernels, call(): pl.pallas_call(kernel, grid_spec=grid_spec, out_shape=[jax.ShapeDtypeStru...  71.1 us
    ppermute x38, starting transfers between devices, send(): return lax.ppermute(value, axes, pairs(sizes, move))  40.9 us
    ppermute x38, waiting for transfers between devices, send(): return lax.ppermute(value, axes, pairs(sizes, move))  16.5 us
    all_to_all x2, starting transfers between devices, over_z(): lax.all_to_all(value, 'shard', split_axis=0, concat_axis=0, tiled=True)  7.9 us
    convert_element_type x2, other arithmetic, gather_x(): self.pair = mark(jnp.stack([self.own, near]).astype(jnp.float32))  4.43 us
    convert_element_type x2, other arithmetic, gather_y(): self.far_pair = mark(jnp.stack([far, far2]).astype(jnp.float32))  4.28 us
    all_to_all x2, waiting for transfers between devices, over_z(): lax.all_to_all(value, 'shard', split_axis=0, concat_axis=0, tiled=True)  3.67 us
  transfers between devices with their start and end apart: 40, of which 11 were waited for; matrix products, arithmetic and copies ran while one was open for 11% of the time, Pallas kernels for 40%

profile of v4, /device:TPU:0, one launch (start us, length us, event | category | flops | bytes accessed | tf_op | source)
XLA Modules:
  0.0 167.4 jit_solution(12143320541232288818)
XLA Ops:
  3.1 3.7 %pick.1 = f32[2,192,2048]{2,1,0:T(8,128)} custom-call(s32[3]{0:T(128)S(1)} %pad_add_fusion.4.here, f32[192,8192]{1,0:T(8,128)} %bitcast.96), custom_call_target="tpu_custom_call" | custom-call | flops 20000000000 | bytes 1000000 | tf_op jit(solution)/shard_map/pick/pallas_call | solution.py:76
  7.3 3.7 %add_split.2 = (f32[2,192,384]{2,1,0:T(8,128)S(1)}, f32[2,192,384]{2,1,0:T(8,128)S(1)}, f32[2,192,384]{2,1,0:T(8,128)S(1)}, f32[2,192,384]{2,1,0:T(8,128)}) custom-call(s32[3]{0:T(128)S(1)} %pad_add_fusion.5.here, f32[2,2,192,1536]{3,2,1,0:T(8,128)} %bitcast.72, f32[2,2,192,1536]{3,2,1,0:T(8,128)} %bitcast.73, ...), custom_call_target="tpu_custom_call" | custom-call | flops 20000000000 | bytes 1000000 | tf_op jit(solution)/shard_map/add_split/pallas_call | solution.py:76
  11.1 2.9 %collective-permute-start.3 = (f16[2,192,384]{2,1,0:T(8,128)(2,1)S(1)}, f16[2,192,384]{2,1,0:T(8,128)(2,1)S(1)}, u32[]{:S(2)}, u32[]{:S(2)}) collective-permute-start(f16[2,192,384]{2,1,0:T(8,128)(2,1)S(1)} %multiply_convert_fusion.3), channel_id=1, source_target_pairs={{0,16},{1,17},{2,18},{3,19},{4,20},{5,21},{6,22},{7,23},{8,24},{9,... | collective-permute-start | bytes 884744 | tf_op jit(solution)/shard_map/expert_far_x/ppermute | solution.py:292
  14.2 4.4 %add_split.3 = (f32[2,192,512]{2,1,0:T(8,128)S(1)}, f32[2,192,512]{2,1,0:T(8,128)S(1)}, f32[2,192,512]{2,1,0:T(8,128)}, f32[2,192,512]{2,1,0:T(8,128)}) custom-call(s32[3]{0:T(128)S(1)} %pad_add_fusion.5.here, f32[192,8192]{1,0:T(8,128)} %bitcast.97, f32[192,8192]{1,0:T(8,128)} %bitcast.98, f32[2,192,2048]{2,1,0:T(8,128)} %collective-permute-done.2.got_sent.got_kept, ...), custom_call_target="tpu_custom_call" | custom-call | flops 20000000000 | bytes 1000000 | tf_op jit(solution)/shard_map/add_split/pallas_call | solution.py:76
  18.7 2.1 %collective-permute-start.8 = (f16[2,192,512]{2,1,0:T(8,128)(2,1)S(1)}, f16[2,192,512]{2,1,0:T(8,128)(2,1)S(1)}, u32[]{:S(2)}, u32[]{:S(2)}) collective-permute-start(f16[2,192,512]{2,1,0:T(8,128)(2,1)S(1)} %multiply_convert_fusion.1), channel_id=1, source_target_pairs={{0,16},{1,17},{2,18},{3,19},{4,20},{5,21},{6,22},{7,23},{8,24},{9,... | collective-permute-start | bytes 1179656 | tf_op jit(solution)/shard_map/table_far_x/ppermute | solution.py:292
  21.9 2.1 %collective-permute-start.4 = (f16[2,192,384]{2,1,0:T(8,128)(2,1)S(1)}, f16[2,192,384]{2,1,0:T(8,128)(2,1)S(1)}, u32[]{:S(2)}, u32[]{:S(2)}) collective-permute-start(f16[2,192,384]{2,1,0:T(8,128)(2,1)S(1)} %add_convert_fusion.3), channel_id=1, source_target_pairs={{0,1},{1,0},{2,3},{3,2},{4,5},{5,4},{6,7},{7,6},{8,9},{9,8},{10,11... | collective-permute-start | bytes 884744 | tf_op jit(solution)/shard_map/expert_y/ppermute | solution.py:292
  26.3 2.5 %transposed_base.2 = f32[768,384]{1,0:T(8,128)S(1)} custom-call(s32[3]{0:T(128)S(1)} %pad_add_fusion.5.here, f32[2,2,2,384,768]{4,3,2,1,0:T(8,128)} %bitcast.86, f32[2,2,2,384,768]{4,3,2,1,0:T(8,128)} %bitcast.91), custom_call_target="tpu_custom_call" | custom-call | flops 20000000000 | bytes 1000000 | tf_op jit(solution)/shard_map/transposed_base/pallas_call | solution.py:76
  31.8 2.6 %collective-permute-start.6 = (f16[192,384]{1,0:T(8,128)(2,1)S(1)}, f16[192,384]{1,0:T(8,128)(2,1)S(1)}, u32[]{:S(2)}, u32[]{:S(2)}) collective-permute-start(f16[192,384]{1,0:T(8,128)(2,1)S(1)} %get-tuple-element.249), channel_id=1, source_target_pairs={{0,4},{1,5},{2,6},{3,7},{4,0},{5,1},{6,2},{7,3},{8,12},{9,13},{10,... | collective-permute-start | bytes 442376 | tf_op jit(solution)/shard_map/expert_z2/ppermute | solution.py:292
  37.4 2.1 %collective-permute-start.12 = (f16[2,192,512]{2,1,0:T(8,128)(2,1)}, f16[2,192,512]{2,1,0:T(8,128)(2,1)}, u32[]{:S(2)}, u32[]{:S(2)}) collective-permute-start(f16[2,192,512]{2,1,0:T(8,128)(2,1)} %add_convert_fusion.1), channel_id=1, source_target_pairs={{0,1},{1,0},{2,3},{3,2},{4,5},{5,4},{6,7},{7,6},{8,9},{9,8},{10,11... | collective-permute-start | bytes 1179656 | tf_op jit(solution)/shard_map/table_y/ppermute | solution.py:292
  39.5 2.7 %transposed_base.3 = f32[768,512]{1,0:T(8,128)S(1)} custom-call(s32[3]{0:T(128)S(1)} %pad_add_fusion.5.here, f32[2,2,2,512,768]{4,3,2,1,0:T(8,128)} %bitcast.76, f32[2,2,2,512,768]{4,3,2,1,0:T(8,128)} %bitcast.81), custom_call_target="tpu_custom_call" | custom-call | flops 20000000000 | bytes 1000000 | tf_op jit(solution)/shard_map/transposed_base/pallas_call | solution.py:76
  49.6 2.4 %select_bitcast_fusion.4 = (f16[192,512]{1,0:T(8,128)(2,1)}, f16[192,512]{1,0:T(8,128)(2,1)}, f16[192,512]{1,0:T(8,128)(2,1)S(1)}, f16[192,512]{1,0:T(8,128)(2,1)}) fusion(f16[2,192,512]{2,1,0:T(8,128)(2,1)} %collective-permute-done.12, s32[]{:T(128)S(6)} %select_n.257, f16[2,192,512]{2,1,0:T(8,128)(2,1)S(1)} %add_convert_fusion, pred[]{:T(512)S(6)} %eq.28, ...), kind=kLoop, calls=%fused_computation.21 | loop fusion | flops 393216 | bytes 2359316 | tf_op jit(solution)/shard_map/jit(_where)/select_n | solution.py:379
  52.0 3.4 %collective-permute-start.18 = (f16[192,512]{1,0:T(8,128)(2,1)}, f16[192,512]{1,0:T(8,128)(2,1)}, u32[]{:S(2)}, u32[]{:S(2)}) collective-permute-start(f16[192,512]{1,0:T(8,128)(2,1)} %get-tuple-element.241), channel_id=1, source_target_pairs={{0,6},{1,7},{2,4},{3,5},{4,2},{5,3},{6,0},{7,1},{8,14},{9,15},{10,... | collective-permute-start | bytes 589832 | tf_op jit(solution)/shard_map/table_z3/ppermute | solution.py:292
  56.4 3.5 %all-to-all-start = ((bf16[4,192,384]{2,1,0:T(8,128)(2,1)}), bf16[4,192,384]{2,1,0:T(8,128)(2,1)S(1)}, u32[]{:S(2)}, u32[]{:S(2)}) async-start(bf16[4,192,384]{2,1,0:T(8,128)(2,1)} %subtract_convert_fusion.1), calls=%async_computation | async-start | bytes 1179648 | tf_op jit(solution)/shard_map/expert_back_z/all_to_all | solution.py:305
  59.8 2.0 %collective-permute-start.16 = (f16[192,512]{1,0:T(8,128)(2,1)}, f16[192,512]{1,0:T(8,128)(2,1)S(1)}, u32[]{:S(2)}, u32[]{:S(2)}) collective-permute-start(f16[192,512]{1,0:T(8,128)(2,1)} %get-tuple-element.239), channel_id=1, source_target_pairs={{0,2},{1,3},{2,0},{3,1},{4,6},{5,7},{6,4},{7,5},{8,10},{9,11},{10,... | collective-permute-start | bytes 589832 | tf_op jit(solution)/shard_map/table_z1/ppermute | solution.py:292
  61.8 2.4 %collective-permute-start.17 = (f16[192,512]{1,0:T(8,128)(2,1)}, f16[192,512]{1,0:T(8,128)(2,1)S(1)}, u32[]{:S(2)}, u32[]{:S(2)}) collective-permute-start(f16[192,512]{1,0:T(8,128)(2,1)} %get-tuple-element.238), channel_id=1, source_target_pairs={{0,4},{1,5},{2,6},{3,7},{4,0},{5,1},{6,2},{7,3},{8,12},{9,13},{10,... | collective-permute-start | bytes 589832 | tf_op jit(solution)/shard_map/table_z2/ppermute | solution.py:292
  64.2 2.5 %collective-permute-start.13 = (f16[384,768]{1,0:T(8,128)(2,1)}, f16[384,768]{1,0:T(8,128)(2,1)S(1)}, u32[]{:S(2)}, u32[]{:S(2)}) collective-permute-start(f16[384,768]{1,0:T(8,128)(2,1)} %collective-permute-done.10), channel_id=1, source_target_pairs={{0,1},{1,0},{2,3},{3,2},{4,5},{5,4},{6,7},{7,6},{8,9},{9,8},{10,11... | collective-permute-start | bytes 1769480 | tf_op jit(solution)/shard_map/expert_gather2_y/ppermute | solution.py:292
  66.7 2.8 %maximum_convert_fusion.2.refs_0_ = f32[2,384,768]{2,1,0:T(8,128)} fusion(f16[1,384,768]{2,1,0:T(8,128)(2,1)} %bitcast.25, f16[1,384,768]{2,1,0:T(8,128)(2,1)} %bitcast.70), kind=kLoop, calls=%fused_computation.4 | loop fusion | flops 1179648 | bytes 3538944 | tf_op jit(solution)/shard_map/convert_element_type | solution.py:407
  69.5 5.3 %update.8 = (f32[2,2,2,384,768]{4,3,2,1,0:T(8,128)}, f32[2,2,2,384,768]{4,3,2,1,0:T(8,128)}) custom-call(s32[3]{0:T(128)S(1)} %pad_add_fusion.5.here, f32[2,384,768]{2,1,0:T(8,128)} %maximum_convert_fusion.2.refs_0_, f32[2,2,2,384,768]{4,3,2,1,0:T(8,128)} %bitcast.87, f32[2,2,2,384,768]{4,3,2,1,0:T(8,128)} %bitcast.92), custom_call_target="tpu_custom_call" | custom-call | flops 20000000000 | bytes 1000000 | tf_op jit(solution)/shard_map/update/pallas_call | solution.py:76
  74.8 2.6 %maximum_convert_fusion.3.refs_0_ = f32[2,384,768]{2,1,0:T(8,128)} fusion(f16[1,384,768]{2,1,0:T(8,128)(2,1)S(1)} %bitcast.75, f16[1,384,768]{2,1,0:T(8,128)(2,1)} %bitcast.26), kind=kLoop, calls=%fused_computation.5 | loop fusion | flops 1179648 | bytes 3538944 | tf_op jit(solution)/shard_map/convert_element_type | solution.py:412
  78.0 2.2 %all-to-all-done = bf16[4,192,384]{2,1,0:T(8,128)(2,1)S(1)} async-done(((bf16[4,192,384]{2,1,0:T(8,128)(2,1)}), bf16[4,192,384]{2,1,0:T(8,128)(2,1)S(1)}, u32[]{:S(2)}, u32[]{:S(2)}) %all-to-all-start) | async-done | bytes 589856 | tf_op jit(solution)/shard_map/expert_back_z/all_to_all | solution.py:305
  90.3 4.4 %all-to-all-start.1 = ((bf16[4,192,512]{2,1,0:T(8,128)(2,1)}), bf16[4,192,512]{2,1,0:T(8,128)(2,1)S(1)}, u32[]{:S(2)}, u32[]{:S(2)}) async-start(bf16[4,192,512]{2,1,0:T(8,128)(2,1)} %subtract_convert_fusion), calls=%async_computation.1 | async-start | bytes 1572864 | tf_op jit(solution)/shard_map/table_back_z/all_to_all | solution.py:305
  95.7 5.3 %update.9 = (f32[2,2,2,384,768]{4,3,2,1,0:T(8,128)}, f32[2,2,2,384,768]{4,3,2,1,0:T(8,128)}) custom-call(s32[3]{0:T(128)S(1)} %pad_add_fusion.4.here, f32[2,384,768]{2,1,0:T(8,128)} %collective-permute-done.15.refs_0_, f32[2,2,2,384,768]{4,3,2,1,0:T(8,128)} %bitcast.88, ...), custom_call_target="tpu_custom_call", output_to_operand_aliasing={{0}: (4, {}), {1}: (5, {})} | custom-call | flops 20000000000 | bytes 1000000 | tf_op jit(solution)/shard_map/update/pallas_call | solution.py:76
  101.0 5.3 %update.10 = (f32[2,2,2,384,768]{4,3,2,1,0:T(8,128)}, f32[2,2,2,384,768]{4,3,2,1,0:T(8,128)}) custom-call(s32[3]{0:T(128)S(1)} %get-tuple-element.252.here, f32[2,384,768]{2,1,0:T(8,128)} %maximum_convert_fusion.3.refs_0_, f32[2,2,2,384,768]{4,3,2,1,0:T(8,128)} %bitcast.89, ...), custom_call_target="tpu_custom_call", output_to_operand_aliasing={{0}: (4, {}), {1}: (5, {})} | custom-call | flops 20000000000 | bytes 1000000 | tf_op jit(solution)/shard_map/update/pallas_call | solution.py:76
  106.3 5.3 %update.11 = (f32[2,2,2,384,768]{4,3,2,1,0:T(8,128)}, f32[2,2,2,384,768]{4,3,2,1,0:T(8,128)}) custom-call(s32[3]{0:T(128)S(1)} %get-tuple-element.253.here, f32[2,384,768]{2,1,0:T(8,128)} %collective-permute-done.14.refs_0_, f32[2,2,2,384,768]{4,3,2,1,0:T(8,128)} %bitcast.90, ...), custom_call_target="tpu_custom_call", output_to_operand_aliasing={{0}: (4, {}), {1}: (5, {})} | custom-call | flops 20000000000 | bytes 1000000 | tf_op jit(solution)/shard_map/update/pallas_call | solution.py:76
  117.4 6.4 %update.12 = (f32[2,2,2,512,768]{4,3,2,1,0:T(8,128)}, f32[2,2,2,512,768]{4,3,2,1,0:T(8,128)}) custom-call(s32[3]{0:T(128)S(1)} %pad_add_fusion.5.here, f32[2,512,768]{2,1,0:T(8,128)} %copy-done.1, f32[2,2,2,512,768]{4,3,2,1,0:T(8,128)} %bitcast.77, f32[2,2,2,512,768]{4,3,2,1,0:T(8,128)} %bitcast.82), custom_call_target="tpu_custom_call" | custom-call | flops 20000000000 | bytes 1000000 | tf_op jit(solution)/shard_map/update/pallas_call | solution.py:76
  124.1 6.4 %update.13 = (f32[2,2,2,512,768]{4,3,2,1,0:T(8,128)}, f32[2,2,2,512,768]{4,3,2,1,0:T(8,128)}) custom-call(s32[3]{0:T(128)S(1)} %pad_add_fusion.4.here, f32[2,512,768]{2,1,0:T(8,128)} %collective-permute-done.28.refs_0_, f32[2,2,2,512,768]{4,3,2,1,0:T(8,128)} %bitcast.78, ...), custom_call_target="tpu_custom_call", output_to_operand_aliasing={{0}: (4, {}), {1}: (5, {})} | custom-call | flops 20000000000 | bytes 1000000 | tf_op jit(solution)/shard_map/update/pallas_call | solution.py:76
  130.5 4.6 %collective-permute-done.27 = f16[512,768]{1,0:T(8,128)(2,1)S(1)} collective-permute-done((f16[512,768]{1,0:T(8,128)(2,1)}, f16[512,768]{1,0:T(8,128)(2,1)S(1)}, u32[]{:S(2)}, u32[]{:S(2)}) %collective-permute-start.27) | collective-permute-done | bytes 786464 | tf_op jit(solution)/shard_map/table_gather2_y/ppermute | solution.py:292
  139.2 6.4 %update.14 = (f32[2,2,2,512,768]{4,3,2,1,0:T(8,128)}, f32[2,2,2,512,768]{4,3,2,1,0:T(8,128)}) custom-call(s32[3]{0:T(128)S(1)} %get-tuple-element.252.here, f32[2,512,768]{2,1,0:T(8,128)} %copy-done, f32[2,2,2,512,768]{4,3,2,1,0:T(8,128)} %bitcast.79, f32[2,2,2,512,768]{4,3,2,1,0:T(8,128)} %bitcast.84, ...), custom_call_target="tpu_custom_call", output_to_operand_aliasing={{0}: (4, {}), {1}: (5, {})} | custom-call | flops 20000000000 | bytes 1000000 | tf_op jit(solution)/shard_map/update/pallas_call | solution.py:76
  145.7 3.2 %collective-permute-done.32.refs_2_ = bf16[2,192,512]{2,1,0:T(8,128)(2,1)S(1)} collective-permute-done((bf16[2,192,512]{2,1,0:T(8,128)(2,1)S(1)}, bf16[2,192,512]{2,1,0:T(8,128)(2,1)S(1)}, u32[]{:S(2)}, u32[]{:S(2)}) %collective-permute-start.32) | collective-permute-done | bytes 393248 | tf_op jit(solution)/shard_map/table_back_x/ppermute | solution.py:292
  150.8 6.4 %update.15 = (f32[2,2,2,512,768]{4,3,2,1,0:T(8,128)}, f32[2,2,2,512,768]{4,3,2,1,0:T(8,128)}) custom-call(s32[3]{0:T(128)S(1)} %get-tuple-element.253.here, f32[2,512,768]{2,1,0:T(8,128)} %collective-permute-done.30.refs_0_, f32[2,2,2,512,768]{4,3,2,1,0:T(8,128)} %bitcast.80, ...), custom_call_target="tpu_custom_call", output_to_operand_aliasing={{0}: (4, {}), {1}: (5, {})} | custom-call | flops 20000000000 | bytes 1000000 | tf_op jit(solution)/shard_map/update/pallas_call | solution.py:76
  157.9 3.2 %place.2 = bf16[2,2,192,1536]{3,2,1,0:T(8,128)(2,1)} custom-call(s32[3]{0:T(128)S(1)} %pad_add_fusion.5.here, bf16[2,192,384]{2,1,0:T(8,128)(2,1)S(1)} %get-tuple-element.210.refs_0_, bf16[2,192,384]{2,1,0:T(8,128)(2,1)S(1)} %collective-permute-done.19.refs_1_, bf16[2,192,384]{2,1,0:T(8,128)(2,1)S(1)} %collective-permute-done.22.refs_2_, ...), custom_call_target="tpu_custom_call" | custom-call | flops 20000000000 | bytes 1000000 | tf_op jit(solution)/shard_map/place/pallas_call | solution.py:76
  163.7 3.7 %place.3 = bf16[192,8192]{1,0:T(8,128)(2,1)} custom-call(s32[3]{0:T(128)S(1)} %pad_add_fusion.5.here, bf16[2,192,512]{2,1,0:T(8,128)(2,1)S(1)} %get-tuple-element.224.refs_0_, bf16[2,192,512]{2,1,0:T(8,128)(2,1)S(1)} %collective-permute-done.31.refs_1_, bf16[2,192,512]{2,1,0:T(8,128)(2,1)S(1)} %collective-permute-done.32.refs_2_, ...), custom_call_target="tpu_custom_call" | custom-call | flops 20000000000 | bytes 1000000 | tf_op jit(solution)/shard_map/place/pallas_call | solution.py:76
  (111 shorter events, 47.7 us)
Async XLA Ops:
  11.1 10.7 %collective-permute-start.3 = (f16[2,192,384]{2,1,0:T(8,128)(2,1)S(1)}, f16[2,192,384]{2,1,0:T(8,128)(2,1)S(1)}, u32[]{:S(2)}, u32[]{:S(2)}) collective-permute-start(f16[2,192,384]{2,1,0:T(8,128)(2,1)S(1)} %multiply_convert_fusion.3), channel_id=1, source_target_pairs={{0,16},{1,17},{2,18},{3,19},{4,20},{5,21},{6,22},{7,23},{8,24},{9,... | collective-permute-start | bytes 884744 | tf_op jit(solution)/shard_map/expert_far_x/ppermute | solution.py:292
  14.1 14.8 %collective-permute-start.1 = (f16[2,192,384]{2,1,0:T(8,128)(2,1)S(1)}, f16[2,192,384]{2,1,0:T(8,128)(2,1)S(1)}, u32[]{:S(2)}, u32[]{:S(2)}) collective-permute-start(f16[2,192,384]{2,1,0:T(8,128)(2,1)S(1)} %multiply_convert_fusion.2), channel_id=1, source_target_pairs={{0,16},{1,17},{2,18},{3,19},{4,20},{5,21},{6,22},{7,23},{8,24},{9,... | collective-permute-start | bytes 884744 | tf_op jit(solution)/shard_map/expert_near_x/ppermute | solution.py:292
  18.7 17.9 %collective-permute-start.8 = (f16[2,192,512]{2,1,0:T(8,128)(2,1)S(1)}, f16[2,192,512]{2,1,0:T(8,128)(2,1)S(1)}, u32[]{:S(2)}, u32[]{:S(2)}) collective-permute-start(f16[2,192,512]{2,1,0:T(8,128)(2,1)S(1)} %multiply_convert_fusion.1), channel_id=1, source_target_pairs={{0,16},{1,17},{2,18},{3,19},{4,20},{5,21},{6,22},{7,23},{8,24},{9,... | collective-permute-start | bytes 1179656 | tf_op jit(solution)/shard_map/table_far_x/ppermute | solution.py:292
  24.9 23.4 %collective-permute-start.11 = (f16[2,192,512]{2,1,0:T(8,128)(2,1)}, f16[2,192,512]{2,1,0:T(8,128)(2,1)}, u32[]{:S(2)}, u32[]{:S(2)}) collective-permute-start(f16[2,192,512]{2,1,0:T(8,128)(2,1)} %multiply_convert_fusion), channel_id=1, source_target_pairs={{0,16},{1,17},{2,18},{3,19},{4,20},{5,21},{6,22},{7,23},{8,24},{9,... | collective-permute-start | bytes 1179656 | tf_op jit(solution)/shard_map/table_near_x/ppermute | solution.py:292
  30.2 12.1 %collective-permute-start.5 = (f16[192,384]{1,0:T(8,128)(2,1)S(1)}, f16[192,384]{1,0:T(8,128)(2,1)S(1)}, u32[]{:S(2)}, u32[]{:S(2)}) collective-permute-start(f16[192,384]{1,0:T(8,128)(2,1)S(1)} %get-tuple-element.250), channel_id=1, source_target_pairs={{0,2},{1,3},{2,0},{3,1},{4,6},{5,7},{6,4},{7,5},{8,10},{9,11},{10,... | collective-permute-start | bytes 442376 | tf_op jit(solution)/shard_map/expert_z1/ppermute | solution.py:292
  31.8 11.9 %collective-permute-start.6 = (f16[192,384]{1,0:T(8,128)(2,1)S(1)}, f16[192,384]{1,0:T(8,128)(2,1)S(1)}, u32[]{:S(2)}, u32[]{:S(2)}) collective-permute-start(f16[192,384]{1,0:T(8,128)(2,1)S(1)} %get-tuple-element.249), channel_id=1, source_target_pairs={{0,4},{1,5},{2,6},{3,7},{4,0},{5,1},{6,2},{7,3},{8,12},{9,13},{10,... | collective-permute-start | bytes 442376 | tf_op jit(solution)/shard_map/expert_z2/ppermute | solution.py:292
  37.4 12.2 %collective-permute-start.12 = (f16[2,192,512]{2,1,0:T(8,128)(2,1)}, f16[2,192,512]{2,1,0:T(8,128)(2,1)}, u32[]{:S(2)}, u32[]{:S(2)}) collective-permute-start(f16[2,192,512]{2,1,0:T(8,128)(2,1)} %add_convert_fusion.1), channel_id=1, source_target_pairs={{0,1},{1,0},{2,3},{3,2},{4,5},{5,4},{6,7},{7,6},{8,9},{9,8},{10,11... | collective-permute-start | bytes 1179656 | tf_op jit(solution)/shard_map/table_y/ppermute | solution.py:292
  45.2 19.0 %collective-permute-start.10 = (f16[384,768]{1,0:T(8,128)(2,1)}, f16[384,768]{1,0:T(8,128)(2,1)}, u32[]{:S(2)}, u32[]{:S(2)}) collective-permute-start(f16[384,768]{1,0:T(8,128)(2,1)} %copy.24), channel_id=1, source_target_pairs={{0,16},{1,17},{2,18},{3,19},{4,20},{5,21},{6,22},{7,23},{8,24},{9,... | collective-permute-start | bytes 1769480 | tf_op jit(solution)/shard_map/expert_gather_x/ppermute | solution.py:292
  46.7 17.5 %collective-permute-start.9 = (f16[384,768]{1,0:T(8,128)(2,1)}, f16[384,768]{1,0:T(8,128)(2,1)}, u32[]{:S(2)}, u32[]{:S(2)}) collective-permute-start(f16[384,768]{1,0:T(8,128)(2,1)} %copy.24), channel_id=1, source_target_pairs={{0,1},{1,0},{2,3},{3,2},{4,5},{5,4},{6,7},{7,6},{8,9},{9,8},{10,11... | collective-permute-start | bytes 1769480 | tf_op jit(solution)/shard_map/expert_gather_y/ppermute | solution.py:292
  52.0 30.6 %collective-permute-start.18 = (f16[192,512]{1,0:T(8,128)(2,1)}, f16[192,512]{1,0:T(8,128)(2,1)}, u32[]{:S(2)}, u32[]{:S(2)}) collective-permute-start(f16[192,512]{1,0:T(8,128)(2,1)} %get-tuple-element.241), channel_id=1, source_target_pairs={{0,6},{1,7},{2,4},{3,5},{4,2},{5,3},{6,0},{7,1},{8,14},{9,15},{10,... | collective-permute-start | bytes 589832 | tf_op jit(solution)/shard_map/table_z3/ppermute | solution.py:292
  56.4 23.8 %all-to-all-start = ((bf16[4,192,384]{2,1,0:T(8,128)(2,1)}), bf16[4,192,384]{2,1,0:T(8,128)(2,1)S(1)}, u32[]{:S(2)}, u32[]{:S(2)}) async-start(bf16[4,192,384]{2,1,0:T(8,128)(2,1)} %subtract_convert_fusion.1), calls=%async_computation | async-start | bytes 1179648 | tf_op jit(solution)/shard_map/expert_back_z/all_to_all | solution.py:305
  59.8 21.1 %collective-permute-start.16 = (f16[192,512]{1,0:T(8,128)(2,1)}, f16[192,512]{1,0:T(8,128)(2,1)S(1)}, u32[]{:S(2)}, u32[]{:S(2)}) collective-permute-start(f16[192,512]{1,0:T(8,128)(2,1)} %get-tuple-element.239), channel_id=1, source_target_pairs={{0,2},{1,3},{2,0},{3,1},{4,6},{5,7},{6,4},{7,5},{8,10},{9,11},{10,... | collective-permute-start | bytes 589832 | tf_op jit(solution)/shard_map/table_z1/ppermute | solution.py:292
  61.8 20.8 %collective-permute-start.17 = (f16[192,512]{1,0:T(8,128)(2,1)}, f16[192,512]{1,0:T(8,128)(2,1)S(1)}, u32[]{:S(2)}, u32[]{:S(2)}) collective-permute-start(f16[192,512]{1,0:T(8,128)(2,1)} %get-tuple-element.238), channel_id=1, source_target_pairs={{0,4},{1,5},{2,6},{3,7},{4,0},{5,1},{6,2},{7,3},{8,12},{9,13},{10,... | collective-permute-start | bytes 589832 | tf_op jit(solution)/shard_map/table_z2/ppermute | solution.py:292
  69.5 25.2 %collective-permute-start.15 = (f32[2,384,768]{2,1,0:T(8,128)}, f32[2,384,768]{2,1,0:T(8,128)}, u32[]{:S(2)}, u32[]{:S(2)}) collective-permute-start(f32[2,384,768]{2,1,0:T(8,128)} %maximum_convert_fusion.2.refs_0_), channel_id=1, source_target_pairs={{0,8},{1,9},{2,10},{3,11},{4,12},{5,13},{6,14},{7,15},{8,0},{9,1},... | collective-permute-start | bytes 7077896 | tf_op jit(solution)/shard_map/expert_gather_core/ppermute | solution.py:292
  77.5 28.8 %collective-permute-start.14 = (f32[2,384,768]{2,1,0:T(8,128)}, f32[2,384,768]{2,1,0:T(8,128)}, u32[]{:S(2)}, u32[]{:S(2)}) collective-permute-start(f32[2,384,768]{2,1,0:T(8,128)} %maximum_convert_fusion.3.refs_0_), channel_id=1, source_target_pairs={{0,8},{1,9},{2,10},{3,11},{4,12},{5,13},{6,14},{7,15},{8,0},{9,1},... | collective-permute-start | bytes 7077896 | tf_op jit(solution)/shard_map/expert_gather2_core/ppermute | solution.py:292
  86.2 25.5 %collective-permute-start.21 = (f16[512,768]{1,0:T(8,128)(2,1)}, f16[512,768]{1,0:T(8,128)(2,1)}, u32[]{:S(2)}, u32[]{:S(2)}) collective-permute-start(f16[512,768]{1,0:T(8,128)(2,1)} %copy.25), channel_id=1, source_target_pairs={{0,16},{1,17},{2,18},{3,19},{4,20},{5,21},{6,22},{7,23},{8,24},{9,... | collective-permute-start | bytes 2359304 | tf_op jit(solution)/shard_map/table_gather_x/ppermute | solution.py:292
  87.1 24.5 %collective-permute-start.20 = (f16[512,768]{1,0:T(8,128)(2,1)}, f16[512,768]{1,0:T(8,128)(2,1)}, u32[]{:S(2)}, u32[]{:S(2)}) collective-permute-start(f16[512,768]{1,0:T(8,128)(2,1)} %copy.25), channel_id=1, source_target_pairs={{0,1},{1,0},{2,3},{3,2},{4,5},{5,4},{6,7},{7,6},{8,9},{9,8},{10,11... | collective-permute-start | bytes 2359304 | tf_op jit(solution)/shard_map/table_gather_y/ppermute | solution.py:292
  88.2 23.5 %collective-permute-start.19 = (bf16[2,192,384]{2,1,0:T(8,128)(2,1)}, bf16[2,192,384]{2,1,0:T(8,128)(2,1)S(1)}, u32[]{:S(2)}, u32[]{:S(2)}) collective-permute-start(bf16[2,192,384]{2,1,0:T(8,128)(2,1)} %get-tuple-element.243), channel_id=1, source_target_pairs={{0,1},{1,0},{2,3},{3,2},{4,5},{5,4},{6,7},{7,6},{8,9},{9,8},{10,11... | collective-permute-start | bytes 884744 | tf_op jit(solution)/shard_map/expert_back_y/ppermute | solution.py:292
  90.3 22.8 %all-to-all-start.1 = ((bf16[4,192,512]{2,1,0:T(8,128)(2,1)}), bf16[4,192,512]{2,1,0:T(8,128)(2,1)S(1)}, u32[]{:S(2)}, u32[]{:S(2)}) async-start(bf16[4,192,512]{2,1,0:T(8,128)(2,1)} %subtract_convert_fusion), calls=%async_computation.1 | async-start | bytes 1572864 | tf_op jit(solution)/shard_map/table_back_z/all_to_all | solution.py:305
  94.7 16.9 %collective-permute-start.22 = (bf16[2,192,384]{2,1,0:T(8,128)(2,1)S(1)}, bf16[2,192,384]{2,1,0:T(8,128)(2,1)S(1)}, u32[]{:S(2)}, u32[]{:S(2)}) collective-permute-start(bf16[2,192,384]{2,1,0:T(8,128)(2,1)S(1)} %get-tuple-element.210.refs_0_), channel_id=1, source_target_pairs={{0,16},{1,17},{2,18},{3,19},{4,20},{5,21},{6,22},{7,23},{8,24},{9,... | collective-permute-start | bytes 884744 | tf_op jit(solution)/shard_map/expert_back_x/ppermute | solution.py:292
  114.8 20.2 %collective-permute-start.24 = (bf16[2,192,384]{2,1,0:T(8,128)(2,1)S(1)}, bf16[2,192,384]{2,1,0:T(8,128)(2,1)S(1)}, u32[]{:S(2)}, u32[]{:S(2)}) collective-permute-start(bf16[2,192,384]{2,1,0:T(8,128)(2,1)S(1)} %get-tuple-element.210.refs_0_), channel_id=1, source_target_pairs={{0,8},{1,9},{2,10},{3,11},{4,12},{5,13},{6,14},{7,15},{8,0},{9,1},... | collective-permute-start | bytes 884744 | tf_op jit(solution)/shard_map/expert_back_core/ppermute | solution.py:292
  115.3 19.7 %collective-permute-start.27 = (f16[512,768]{1,0:T(8,128)(2,1)}, f16[512,768]{1,0:T(8,128)(2,1)S(1)}, u32[]{:S(2)}, u32[]{:S(2)}) collective-permute-start(f16[512,768]{1,0:T(8,128)(2,1)} %collective-permute-done.21), channel_id=1, source_target_pairs={{0,1},{1,0},{2,3},{3,2},{4,5},{5,4},{6,7},{7,6},{8,9},{9,8},{10,11... | collective-permute-start | bytes 2359304 | tf_op jit(solution)/shard_map/table_gather2_y/ppermute | solution.py:292
  115.7 19.4 %collective-permute-start.25 = (bf16[2,192,384]{2,1,0:T(8,128)(2,1)S(1)}, bf16[2,192,384]{2,1,0:T(8,128)(2,1)S(1)}, u32[]{:S(2)}, u32[]{:S(2)}) collective-permute-start(bf16[2,192,384]{2,1,0:T(8,128)(2,1)S(1)} %collective-permute-done.19.refs_1_), channel_id=1, source_target_pairs={{0,8},{1,9},{2,10},{3,11},{4,12},{5,13},{6,14},{7,15},{8,0},{9,1},... | collective-permute-start | bytes 884744 | tf_op jit(solution)/shard_map/expert_back_core/ppermute | solution.py:292
  115.7 19.4 %collective-permute-start.23 = (bf16[2,192,384]{2,1,0:T(8,128)(2,1)S(1)}, bf16[2,192,384]{2,1,0:T(8,128)(2,1)S(1)}, u32[]{:S(2)}, u32[]{:S(2)}) collective-permute-start(bf16[2,192,384]{2,1,0:T(8,128)(2,1)S(1)} %collective-permute-done.19.refs_1_), channel_id=1, source_target_pairs={{0,16},{1,17},{2,18},{3,19},{4,20},{5,21},{6,22},{7,23},{8,24},{9,... | collective-permute-start | bytes 884744 | tf_op jit(solution)/shard_map/expert_back2_x/ppermute | solution.py:292
  123.8 11.3 %collective-permute-start.26 = (bf16[2,192,384]{2,1,0:T(8,128)(2,1)S(1)}, bf16[2,192,384]{2,1,0:T(8,128)(2,1)S(1)}, u32[]{:S(2)}, u32[]{:S(2)}) collective-permute-start(bf16[2,192,384]{2,1,0:T(8,128)(2,1)S(1)} %collective-permute-done.22.refs_2_), channel_id=1, source_target_pairs={{0,8},{1,9},{2,10},{3,11},{4,12},{5,13},{6,14},{7,15},{8,0},{9,1},... | collective-permute-start | bytes 884744 | tf_op jit(solution)/shard_map/expert_back_core/ppermute | solution.py:292
  136.8 13.8 %collective-permute-start.30 = (f32[2,512,768]{2,1,0:T(8,128)S(1)}, f32[2,512,768]{2,1,0:T(8,128)}, u32[]{:S(2)}, u32[]{:S(2)}) collective-permute-start(f32[2,512,768]{2,1,0:T(8,128)S(1)} %maximum_convert_fusion.1.refs_0_), channel_id=1, source_target_pairs={{0,8},{1,9},{2,10},{3,11},{4,12},{5,13},{6,14},{7,15},{8,0},{9,1},... | collective-permute-start | bytes 9437192 | tf_op jit(solution)/shard_map/table_gather2_core/ppermute | solution.py:292
  136.9 11.9 %collective-permute-start.31 = (bf16[2,192,512]{2,1,0:T(8,128)(2,1)S(1)}, bf16[2,192,512]{2,1,0:T(8,128)(2,1)S(1)}, u32[]{:S(2)}, u32[]{:S(2)}) collective-permute-start(bf16[2,192,512]{2,1,0:T(8,128)(2,1)S(1)} %get-tuple-element.233), channel_id=1, source_target_pairs={{0,1},{1,0},{2,3},{3,2},{4,5},{5,4},{6,7},{7,6},{8,9},{9,8},{10,11... | collective-permute-start | bytes 1179656 | tf_op jit(solution)/shard_map/table_back_y/ppermute | solution.py:292
  137.3 19.9 %collective-permute-start.29 = (bf16[2,192,384]{2,1,0:T(8,128)(2,1)S(1)}, bf16[2,192,384]{2,1,0:T(8,128)(2,1)S(1)}, u32[]{:S(2)}, u32[]{:S(2)}) collective-permute-start(bf16[2,192,384]{2,1,0:T(8,128)(2,1)S(1)} %collective-permute-done.23.refs_3_), channel_id=1, source_target_pairs={{0,8},{1,9},{2,10},{3,11},{4,12},{5,13},{6,14},{7,15},{8,0},{9,1},... | collective-permute-start | bytes 884744 | tf_op jit(solution)/shard_map/expert_back2_core/ppermute | solution.py:292
  137.6 11.3 %collective-permute-start.32 = (bf16[2,192,512]{2,1,0:T(8,128)(2,1)S(1)}, bf16[2,192,512]{2,1,0:T(8,128)(2,1)S(1)}, u32[]{:S(2)}, u32[]{:S(2)}) collective-permute-start(bf16[2,192,512]{2,1,0:T(8,128)(2,1)S(1)} %get-tuple-element.224.refs_0_), channel_id=1, source_target_pairs={{0,16},{1,17},{2,18},{3,19},{4,20},{5,21},{6,22},{7,23},{8,24},{9,... | collective-permute-start | bytes 1179656 | tf_op jit(solution)/shard_map/table_back_x/ppermute | solution.py:292
  139.2 21.9 %collective-permute-start.34 = (bf16[2,192,512]{2,1,0:T(8,128)(2,1)S(1)}, bf16[2,192,512]{2,1,0:T(8,128)(2,1)S(1)}, u32[]{:S(2)}, u32[]{:S(2)}) collective-permute-start(bf16[2,192,512]{2,1,0:T(8,128)(2,1)S(1)} %get-tuple-element.224.refs_0_), channel_id=1, source_target_pairs={{0,8},{1,9},{2,10},{3,11},{4,12},{5,13},{6,14},{7,15},{8,0},{9,1},... | collective-permute-start | bytes 1179656 | tf_op jit(solution)/shard_map/table_back_core/ppermute | solution.py:292
  148.8 12.3 %collective-permute-start.35 = (bf16[2,192,512]{2,1,0:T(8,128)(2,1)S(1)}, bf16[2,192,512]{2,1,0:T(8,128)(2,1)S(1)}, u32[]{:S(2)}, u32[]{:S(2)}) collective-permute-start(bf16[2,192,512]{2,1,0:T(8,128)(2,1)S(1)} %collective-permute-done.31.refs_1_), channel_id=1, source_target_pairs={{0,8},{1,9},{2,10},{3,11},{4,12},{5,13},{6,14},{7,15},{8,0},{9,1},... | collective-permute-start | bytes 1179656 | tf_op jit(solution)/shard_map/table_back_core/ppermute | solution.py:292
  148.8 12.3 %collective-permute-start.33 = (bf16[2,192,512]{2,1,0:T(8,128)(2,1)S(1)}, bf16[2,192,512]{2,1,0:T(8,128)(2,1)S(1)}, u32[]{:S(2)}, u32[]{:S(2)}) collective-permute-start(bf16[2,192,512]{2,1,0:T(8,128)(2,1)S(1)} %collective-permute-done.31.refs_1_), channel_id=1, source_target_pairs={{0,16},{1,17},{2,18},{3,19},{4,20},{5,21},{6,22},{7,23},{8,24},{9,... | collective-permute-start | bytes 1179656 | tf_op jit(solution)/shard_map/table_back2_x/ppermute | solution.py:292
  (18 other events, 84.4 us)

commit v5 on v4

--- a/solution.py
+++ b/solution.py
@@ -484,8 +484,8 @@
     e.update("pair")
     e.wait("far2")
     e.gather_y()
+    t.gather()
     e.copies_y()
-    t.gather()
     t.low_part()
     t.copies_z()
     e.update("pair_core")

time: 168 us -> 164 us (0.976)
  starting transfers between devices: 48.8 us -> 44.5 us
    ppermute x38, starting transfers between devices: 40.9 us -> 35.8 us  [send(): return lax.ppermute(value, axes, pairs(sizes, move))]
    ppermute x38, waiting for transfers between devices: 16.5 us -> 19.3 us  [send(): return lax.ppermute(value, axes, pairs(sizes, move))]
  transfers between devices with their start and end apart: 40 -> 40, of which waited for: 11 -> 13; matrix products, arithmetic and copies ran while one was open for 11% -> 12% of each run, Pallas kernels for 40% -> 41%
where the time goes in v5:
time: 164 us
  Pallas kernels  71.1 us (43%)
  starting transfers between devices  44.5 us (27%)
  waiting for transfers between devices  21.6 us (13%)
  other arithmetic  18.9 us (12%)
  local copies, waits for them, and re-layouts  6.71 us (4%)
    pallas_call x15, Pallas kernels, call(): pl.pallas_call(kernel, grid_spec=grid_spec, out_shape=[jax.ShapeDtypeStru...  71.1 us
    ppermute x38, starting transfers between devices, send(): return lax.ppermute(value, axes, pairs(sizes, move))  35.8 us
    ppermute x38, waiting for transfers between devices, send(): return lax.ppermute(value, axes, pairs(sizes, move))  19.3 us
    all_to_all x2, starting transfers between devices, over_z(): lax.all_to_all(value, 'shard', split_axis=0, concat_axis=0, tiled=True)  8.74 us
    convert_element_type x2, other arithmetic, gather_x(): self.pair = mark(jnp.stack([self.own, near]).astype(jnp.float32))  4.43 us
    convert_element_type x2, other arithmetic, gather_y(): self.far_pair = mark(jnp.stack([far, far2]).astype(jnp.float32))  4.28 us
  transfers between devices with their start and end apart: 40, of which 13 were waited for; matrix products, arithmetic and copies ran while one was open for 12% of the time, Pallas kernels for 41%

profile of v5, /device:TPU:0, one launch (start us, length us, event | category | flops | bytes accessed | tf_op | source)
XLA Modules:
  0.0 163.8 jit_solution(5898444327236400713)
XLA Ops:
  3.1 3.7 %pick.1 = f32[2,192,2048]{2,1,0:T(8,128)} custom-call(s32[3]{0:T(128)S(1)} %pad_add_fusion.4.here, f32[192,8192]{1,0:T(8,128)} %bitcast.96), custom_call_target="tpu_custom_call" | custom-call | flops 20000000000 | bytes 1000000 | tf_op jit(solution)/shard_map/pick/pallas_call | solution.py:76
  7.3 3.7 %add_split.2 = (f32[2,192,384]{2,1,0:T(8,128)S(1)}, f32[2,192,384]{2,1,0:T(8,128)S(1)}, f32[2,192,384]{2,1,0:T(8,128)S(1)}, f32[2,192,384]{2,1,0:T(8,128)}) custom-call(s32[3]{0:T(128)S(1)} %pad_add_fusion.5.here, f32[2,2,192,1536]{3,2,1,0:T(8,128)} %bitcast.72, f32[2,2,192,1536]{3,2,1,0:T(8,128)} %bitcast.73, ...), custom_call_target="tpu_custom_call" | custom-call | flops 20000000000 | bytes 1000000 | tf_op jit(solution)/shard_map/add_split/pallas_call | solution.py:76
  11.1 2.9 %collective-permute-start.3 = (f16[2,192,384]{2,1,0:T(8,128)(2,1)S(1)}, f16[2,192,384]{2,1,0:T(8,128)(2,1)S(1)}, u32[]{:S(2)}, u32[]{:S(2)}) collective-permute-start(f16[2,192,384]{2,1,0:T(8,128)(2,1)S(1)} %multiply_convert_fusion.3), channel_id=1, source_target_pairs={{0,16},{1,17},{2,18},{3,19},{4,20},{5,21},{6,22},{7,23},{8,24},{9,... | collective-permute-start | bytes 884744 | tf_op jit(solution)/shard_map/expert_far_x/ppermute | solution.py:292
  14.2 4.4 %add_split.3 = (f32[2,192,512]{2,1,0:T(8,128)S(1)}, f32[2,192,512]{2,1,0:T(8,128)S(1)}, f32[2,192,512]{2,1,0:T(8,128)}, f32[2,192,512]{2,1,0:T(8,128)}) custom-call(s32[3]{0:T(128)S(1)} %pad_add_fusion.5.here, f32[192,8192]{1,0:T(8,128)} %bitcast.97, f32[192,8192]{1,0:T(8,128)} %bitcast.98, f32[2,192,2048]{2,1,0:T(8,128)} %collective-permute-done.2.got_sent.got_kept, ...), custom_call_target="tpu_custom_call" | custom-call | flops 20000000000 | bytes 1000000 | tf_op jit(solution)/shard_map/add_split/pallas_call | solution.py:76
  18.7 2.1 %collective-permute-start.8 = (f16[2,192,512]{2,1,0:T(8,128)(2,1)S(1)}, f16[2,192,512]{2,1,0:T(8,128)(2,1)S(1)}, u32[]{:S(2)}, u32[]{:S(2)}) collective-permute-start(f16[2,192,512]{2,1,0:T(8,128)(2,1)S(1)} %multiply_convert_fusion.1), channel_id=1, source_target_pairs={{0,16},{1,17},{2,18},{3,19},{4,20},{5,21},{6,22},{7,23},{8,24},{9,... | collective-permute-start | bytes 1179656 | tf_op jit(solution)/shard_map/table_far_x/ppermute | solution.py:292
  21.9 2.1 %collective-permute-start.4 = (f16[2,192,384]{2,1,0:T(8,128)(2,1)S(1)}, f16[2,192,384]{2,1,0:T(8,128)(2,1)S(1)}, u32[]{:S(2)}, u32[]{:S(2)}) collective-permute-start(f16[2,192,384]{2,1,0:T(8,128)(2,1)S(1)} %add_convert_fusion.3), channel_id=1, source_target_pairs={{0,1},{1,0},{2,3},{3,2},{4,5},{5,4},{6,7},{7,6},{8,9},{9,8},{10,11... | collective-permute-start | bytes 884744 | tf_op jit(solution)/shard_map/expert_y/ppermute | solution.py:292
  26.3 2.5 %transposed_base.2 = f32[768,384]{1,0:T(8,128)S(1)} custom-call(s32[3]{0:T(128)S(1)} %pad_add_fusion.5.here, f32[2,2,2,384,768]{4,3,2,1,0:T(8,128)} %bitcast.86, f32[2,2,2,384,768]{4,3,2,1,0:T(8,128)} %bitcast.91), custom_call_target="tpu_custom_call" | custom-call | flops 20000000000 | bytes 1000000 | tf_op jit(solution)/shard_map/transposed_base/pallas_call | solution.py:76
  31.8 2.6 %collective-permute-start.6 = (f16[192,384]{1,0:T(8,128)(2,1)S(1)}, f16[192,384]{1,0:T(8,128)(2,1)S(1)}, u32[]{:S(2)}, u32[]{:S(2)}) collective-permute-start(f16[192,384]{1,0:T(8,128)(2,1)S(1)} %get-tuple-element.249), channel_id=1, source_target_pairs={{0,4},{1,5},{2,6},{3,7},{4,0},{5,1},{6,2},{7,3},{8,12},{9,13},{10,... | collective-permute-start | bytes 442376 | tf_op jit(solution)/shard_map/expert_z2/ppermute | solution.py:292
  34.7 1.9 %collective-permute-done.8 = f16[2,192,512]{2,1,0:T(8,128)(2,1)S(1)} collective-permute-done((f16[2,192,512]{2,1,0:T(8,128)(2,1)S(1)}, f16[2,192,512]{2,1,0:T(8,128)(2,1)S(1)}, u32[]{:S(2)}, u32[]{:S(2)}) %collective-permute-start.8) | collective-permute-done | bytes 393248 | tf_op jit(solution)/shard_map/table_far_x/ppermute | solution.py:292
  37.4 2.1 %collective-permute-start.12 = (f16[2,192,512]{2,1,0:T(8,128)(2,1)}, f16[2,192,512]{2,1,0:T(8,128)(2,1)}, u32[]{:S(2)}, u32[]{:S(2)}) collective-permute-start(f16[2,192,512]{2,1,0:T(8,128)(2,1)} %add_convert_fusion.1), channel_id=1, source_target_pairs={{0,1},{1,0},{2,3},{3,2},{4,5},{5,4},{6,7},{7,6},{8,9},{9,8},{10,11... | collective-permute-start | bytes 1179656 | tf_op jit(solution)/shard_map/table_y/ppermute | solution.py:292
  39.5 2.7 %transposed_base.3 = f32[768,512]{1,0:T(8,128)S(1)} custom-call(s32[3]{0:T(128)S(1)} %pad_add_fusion.5.here, f32[2,2,2,512,768]{4,3,2,1,0:T(8,128)} %bitcast.76, f32[2,2,2,512,768]{4,3,2,1,0:T(8,128)} %bitcast.81), custom_call_target="tpu_custom_call" | custom-call | flops 20000000000 | bytes 1000000 | tf_op jit(solution)/shard_map/transposed_base/pallas_call | solution.py:76
  49.6 2.4 %select_bitcast_fusion.4 = (f16[192,512]{1,0:T(8,128)(2,1)}, f16[192,512]{1,0:T(8,128)(2,1)}, f16[192,512]{1,0:T(8,128)(2,1)S(1)}, f16[192,512]{1,0:T(8,128)(2,1)}) fusion(f16[2,192,512]{2,1,0:T(8,128)(2,1)} %collective-permute-done.12, s32[]{:T(128)S(6)} %select_n.257, f16[2,192,512]{2,1,0:T(8,128)(2,1)S(1)} %add_convert_fusion, pred[]{:T(512)S(6)} %eq.28, ...), kind=kLoop, calls=%fused_computation.21 | loop fusion | flops 393216 | bytes 2359316 | tf_op jit(solution)/shard_map/jit(_where)/select_n | solution.py:379
  52.0 3.4 %collective-permute-start.18 = (f16[192,512]{1,0:T(8,128)(2,1)}, f16[192,512]{1,0:T(8,128)(2,1)}, u32[]{:S(2)}, u32[]{:S(2)}) collective-permute-start(f16[192,512]{1,0:T(8,128)(2,1)} %get-tuple-element.241), channel_id=1, source_target_pairs={{0,6},{1,7},{2,4},{3,5},{4,2},{5,3},{6,0},{7,1},{8,14},{9,15},{10,... | collective-permute-start | bytes 589832 | tf_op jit(solution)/shard_map/table_z3/ppermute | solution.py:292
  57.4 4.6 %all-to-all-start = ((bf16[4,192,384]{2,1,0:T(8,128)(2,1)}), bf16[4,192,384]{2,1,0:T(8,128)(2,1)S(1)}, u32[]{:S(2)}, u32[]{:S(2)}) async-start(bf16[4,192,384]{2,1,0:T(8,128)(2,1)} %subtract_convert_fusion.1), calls=%async_computation | async-start | bytes 1179648 | tf_op jit(solution)/shard_map/expert_back_z/all_to_all | solution.py:305
  62.0 2.5 %collective-permute-start.13 = (f16[384,768]{1,0:T(8,128)(2,1)}, f16[384,768]{1,0:T(8,128)(2,1)S(1)}, u32[]{:S(2)}, u32[]{:S(2)}) collective-permute-start(f16[384,768]{1,0:T(8,128)(2,1)} %collective-permute-done.10), channel_id=1, source_target_pairs={{0,1},{1,0},{2,3},{3,2},{4,5},{5,4},{6,7},{7,6},{8,9},{9,8},{10,11... | collective-permute-start | bytes 1769480 | tf_op jit(solution)/shard_map/expert_gather2_y/ppermute | solution.py:292
  64.6 2.8 %maximum_convert_fusion.2.refs_0_ = f32[2,384,768]{2,1,0:T(8,128)} fusion(f16[1,384,768]{2,1,0:T(8,128)(2,1)} %bitcast.25, f16[1,384,768]{2,1,0:T(8,128)(2,1)} %bitcast.70), kind=kLoop, calls=%fused_computation.4 | loop fusion | flops 1179648 | bytes 3538944 | tf_op jit(solution)/shard_map/convert_element_type | solution.py:407
  67.4 5.3 %update.8 = (f32[2,2,2,384,768]{4,3,2,1,0:T(8,128)}, f32[2,2,2,384,768]{4,3,2,1,0:T(8,128)}) custom-call(s32[3]{0:T(128)S(1)} %pad_add_fusion.5.here, f32[2,384,768]{2,1,0:T(8,128)} %maximum_convert_fusion.2.refs_0_, f32[2,2,2,384,768]{4,3,2,1,0:T(8,128)} %bitcast.87, f32[2,2,2,384,768]{4,3,2,1,0:T(8,128)} %bitcast.92), custom_call_target="tpu_custom_call" | custom-call | flops 20000000000 | bytes 1000000 | tf_op jit(solution)/shard_map/update/pallas_call | solution.py:76
  73.4 2.6 %maximum_convert_fusion.3.refs_0_ = f32[2,384,768]{2,1,0:T(8,128)} fusion(f16[1,384,768]{2,1,0:T(8,128)(2,1)S(1)} %bitcast.75, f16[1,384,768]{2,1,0:T(8,128)(2,1)} %bitcast.26), kind=kLoop, calls=%fused_computation.5 | loop fusion | flops 1179648 | bytes 3538944 | tf_op jit(solution)/shard_map/convert_element_type | solution.py:412
  76.0 2.1 %collective-permute-done.17 = f16[192,512]{1,0:T(8,128)(2,1)S(1)} collective-permute-done((f16[192,512]{1,0:T(8,128)(2,1)}, f16[192,512]{1,0:T(8,128)(2,1)S(1)}, u32[]{:S(2)}, u32[]{:S(2)}) %collective-permute-start.17) | collective-permute-done | bytes 196640 | tf_op jit(solution)/shard_map/table_z2/ppermute | solution.py:292
  85.8 4.1 %all-to-all-start.1 = ((bf16[4,192,512]{2,1,0:T(8,128)(2,1)}), bf16[4,192,512]{2,1,0:T(8,128)(2,1)S(1)}, u32[]{:S(2)}, u32[]{:S(2)}) async-start(bf16[4,192,512]{2,1,0:T(8,128)(2,1)} %subtract_convert_fusion), calls=%async_computation.1 | async-start | bytes 1572864 | tf_op jit(solution)/shard_map/table_back_z/all_to_all | solution.py:305
  91.0 5.3 %update.9 = (f32[2,2,2,384,768]{4,3,2,1,0:T(8,128)}, f32[2,2,2,384,768]{4,3,2,1,0:T(8,128)}) custom-call(s32[3]{0:T(128)S(1)} %pad_add_fusion.4.here, f32[2,384,768]{2,1,0:T(8,128)} %collective-permute-done.15.refs_0_, f32[2,2,2,384,768]{4,3,2,1,0:T(8,128)} %bitcast.88, ...), custom_call_target="tpu_custom_call", output_to_operand_aliasing={{0}: (4, {}), {1}: (5, {})} | custom-call | flops 20000000000 | bytes 1000000 | tf_op jit(solution)/shard_map/update/pallas_call | solution.py:76
  96.4 5.3 %update.10 = (f32[2,2,2,384,768]{4,3,2,1,0:T(8,128)}, f32[2,2,2,384,768]{4,3,2,1,0:T(8,128)}) custom-call(s32[3]{0:T(128)S(1)} %get-tuple-element.252.here, f32[2,384,768]{2,1,0:T(8,128)} %maximum_convert_fusion.3.refs_0_, f32[2,2,2,384,768]{4,3,2,1,0:T(8,128)} %bitcast.89, ...), custom_call_target="tpu_custom_call", output_to_operand_aliasing={{0}: (4, {}), {1}: (5, {})} | custom-call | flops 20000000000 | bytes 1000000 | tf_op jit(solution)/shard_map/update/pallas_call | solution.py:76
  101.7 5.3 %update.11 = (f32[2,2,2,384,768]{4,3,2,1,0:T(8,128)}, f32[2,2,2,384,768]{4,3,2,1,0:T(8,128)}) custom-call(s32[3]{0:T(128)S(1)} %get-tuple-element.253.here, f32[2,384,768]{2,1,0:T(8,128)} %collective-permute-done.14.refs_0_, f32[2,2,2,384,768]{4,3,2,1,0:T(8,128)} %bitcast.90, ...), custom_call_target="tpu_custom_call", output_to_operand_aliasing={{0}: (4, {}), {1}: (5, {})} | custom-call | flops 20000000000 | bytes 1000000 | tf_op jit(solution)/shard_map/update/pallas_call | solution.py:76
  107.1 2.2 %all-to-all-done.1 = bf16[4,192,512]{2,1,0:T(8,128)(2,1)S(1)} async-done(((bf16[4,192,512]{2,1,0:T(8,128)(2,1)}), bf16[4,192,512]{2,1,0:T(8,128)(2,1)S(1)}, u32[]{:S(2)}, u32[]{:S(2)}) %all-to-all-start.1) | async-done | bytes 786464 | tf_op jit(solution)/shard_map/table_back_z/all_to_all | solution.py:305
  113.5 6.4 %update.12 = (f32[2,2,2,512,768]{4,3,2,1,0:T(8,128)}, f32[2,2,2,512,768]{4,3,2,1,0:T(8,128)}) custom-call(s32[3]{0:T(128)S(1)} %pad_add_fusion.5.here, f32[2,512,768]{2,1,0:T(8,128)} %copy-done.1, f32[2,2,2,512,768]{4,3,2,1,0:T(8,128)} %bitcast.77, f32[2,2,2,512,768]{4,3,2,1,0:T(8,128)} %bitcast.82), custom_call_target="tpu_custom_call" | custom-call | flops 20000000000 | bytes 1000000 | tf_op jit(solution)/shard_map/update/pallas_call | solution.py:76
  120.2 6.4 %update.13 = (f32[2,2,2,512,768]{4,3,2,1,0:T(8,128)}, f32[2,2,2,512,768]{4,3,2,1,0:T(8,128)}) custom-call(s32[3]{0:T(128)S(1)} %pad_add_fusion.4.here, f32[2,512,768]{2,1,0:T(8,128)} %collective-permute-done.28.refs_0_, f32[2,2,2,512,768]{4,3,2,1,0:T(8,128)} %bitcast.78, ...), custom_call_target="tpu_custom_call", output_to_operand_aliasing={{0}: (4, {}), {1}: (5, {})} | custom-call | flops 20000000000 | bytes 1000000 | tf_op jit(solution)/shard_map/update/pallas_call | solution.py:76
  126.7 4.5 %collective-permute-done.27 = f16[512,768]{1,0:T(8,128)(2,1)S(1)} collective-permute-done((f16[512,768]{1,0:T(8,128)(2,1)}, f16[512,768]{1,0:T(8,128)(2,1)S(1)}, u32[]{:S(2)}, u32[]{:S(2)}) %collective-permute-start.27) | collective-permute-done | bytes 786464 | tf_op jit(solution)/shard_map/table_gather2_y/ppermute | solution.py:292
  135.4 6.4 %update.14 = (f32[2,2,2,512,768]{4,3,2,1,0:T(8,128)}, f32[2,2,2,512,768]{4,3,2,1,0:T(8,128)}) custom-call(s32[3]{0:T(128)S(1)} %get-tuple-element.252.here, f32[2,512,768]{2,1,0:T(8,128)} %copy-done, f32[2,2,2,512,768]{4,3,2,1,0:T(8,128)} %bitcast.79, f32[2,2,2,512,768]{4,3,2,1,0:T(8,128)} %bitcast.84, ...), custom_call_target="tpu_custom_call", output_to_operand_aliasing={{0}: (4, {}), {1}: (5, {})} | custom-call | flops 20000000000 | bytes 1000000 | tf_op jit(solution)/shard_map/update/pallas_call | solution.py:76
  141.8 4.3 %collective-permute-done.32.refs_2_ = bf16[2,192,512]{2,1,0:T(8,128)(2,1)S(1)} collective-permute-done((bf16[2,192,512]{2,1,0:T(8,128)(2,1)S(1)}, bf16[2,192,512]{2,1,0:T(8,128)(2,1)S(1)}, u32[]{:S(2)}, u32[]{:S(2)}) %collective-permute-start.32) | collective-permute-done | bytes 393248 | tf_op jit(solution)/shard_map/table_back_x/ppermute | solution.py:292
  146.9 6.4 %update.15 = (f32[2,2,2,512,768]{4,3,2,1,0:T(8,128)}, f32[2,2,2,512,768]{4,3,2,1,0:T(8,128)}) custom-call(s32[3]{0:T(128)S(1)} %get-tuple-element.253.here, f32[2,512,768]{2,1,0:T(8,128)} %collective-permute-done.30.refs_0_, f32[2,2,2,512,768]{4,3,2,1,0:T(8,128)} %bitcast.80, ...), custom_call_target="tpu_custom_call", output_to_operand_aliasing={{0}: (4, {}), {1}: (5, {})} | custom-call | flops 20000000000 | bytes 1000000 | tf_op jit(solution)/shard_map/update/pallas_call | solution.py:76
  154.1 3.2 %place.2 = bf16[2,2,192,1536]{3,2,1,0:T(8,128)(2,1)} custom-call(s32[3]{0:T(128)S(1)} %pad_add_fusion.5.here, bf16[2,192,384]{2,1,0:T(8,128)(2,1)S(1)} %get-tuple-element.210.refs_0_, bf16[2,192,384]{2,1,0:T(8,128)(2,1)S(1)} %collective-permute-done.19.refs_1_, bf16[2,192,384]{2,1,0:T(8,128)(2,1)S(1)} %collective-permute-done.22.refs_2_, ...), custom_call_target="tpu_custom_call" | custom-call | flops 20000000000 | bytes 1000000 | tf_op jit(solution)/shard_map/place/pallas_call | solution.py:76
  160.2 3.7 %place.3 = bf16[192,8192]{1,0:T(8,128)(2,1)} custom-call(s32[3]{0:T(128)S(1)} %pad_add_fusion.5.here, bf16[2,192,512]{2,1,0:T(8,128)(2,1)S(1)} %get-tuple-element.224.refs_0_, bf16[2,192,512]{2,1,0:T(8,128)(2,1)S(1)} %collective-permute-done.31.refs_1_, bf16[2,192,512]{2,1,0:T(8,128)(2,1)S(1)} %collective-permute-done.32.refs_2_, ...), custom_call_target="tpu_custom_call" | custom-call | flops 20000000000 | bytes 1000000 | tf_op jit(solution)/shard_map/place/pallas_call | solution.py:76
  (109 shorter events, 42.6 us)
Async XLA Ops:
  14.1 14.8 %collective-permute-start.1 = (f16[2,192,384]{2,1,0:T(8,128)(2,1)S(1)}, f16[2,192,384]{2,1,0:T(8,128)(2,1)S(1)}, u32[]{:S(2)}, u32[]{:S(2)}) collective-permute-start(f16[2,192,384]{2,1,0:T(8,128)(2,1)S(1)} %multiply_convert_fusion.2), channel_id=1, source_target_pairs={{0,16},{1,17},{2,18},{3,19},{4,20},{5,21},{6,22},{7,23},{8,24},{9,... | collective-permute-start | bytes 884744 | tf_op jit(solution)/shard_map/expert_near_x/ppermute | solution.py:292
  18.7 17.9 %collective-permute-start.8 = (f16[2,192,512]{2,1,0:T(8,128)(2,1)S(1)}, f16[2,192,512]{2,1,0:T(8,128)(2,1)S(1)}, u32[]{:S(2)}, u32[]{:S(2)}) collective-permute-start(f16[2,192,512]{2,1,0:T(8,128)(2,1)S(1)} %multiply_convert_fusion.1), channel_id=1, source_target_pairs={{0,16},{1,17},{2,18},{3,19},{4,20},{5,21},{6,22},{7,23},{8,24},{9,... | collective-permute-start | bytes 1179656 | tf_op jit(solution)/shard_map/table_far_x/ppermute | solution.py:292
  24.9 23.4 %collective-permute-start.11 = (f16[2,192,512]{2,1,0:T(8,128)(2,1)}, f16[2,192,512]{2,1,0:T(8,128)(2,1)}, u32[]{:S(2)}, u32[]{:S(2)}) collective-permute-start(f16[2,192,512]{2,1,0:T(8,128)(2,1)} %multiply_convert_fusion), channel_id=1, source_target_pairs={{0,16},{1,17},{2,18},{3,19},{4,20},{5,21},{6,22},{7,23},{8,24},{9,... | collective-permute-start | bytes 1179656 | tf_op jit(solution)/shard_map/table_near_x/ppermute | solution.py:292
  30.2 12.1 %collective-permute-start.5 = (f16[192,384]{1,0:T(8,128)(2,1)S(1)}, f16[192,384]{1,0:T(8,128)(2,1)S(1)}, u32[]{:S(2)}, u32[]{:S(2)}) collective-permute-start(f16[192,384]{1,0:T(8,128)(2,1)S(1)} %get-tuple-element.250), channel_id=1, source_target_pairs={{0,2},{1,3},{2,0},{3,1},{4,6},{5,7},{6,4},{7,5},{8,10},{9,11},{10,... | collective-permute-start | bytes 442376 | tf_op jit(solution)/shard_map/expert_z1/ppermute | solution.py:292
  31.8 11.9 %collective-permute-start.6 = (f16[192,384]{1,0:T(8,128)(2,1)S(1)}, f16[192,384]{1,0:T(8,128)(2,1)S(1)}, u32[]{:S(2)}, u32[]{:S(2)}) collective-permute-start(f16[192,384]{1,0:T(8,128)(2,1)S(1)} %get-tuple-element.249), channel_id=1, source_target_pairs={{0,4},{1,5},{2,6},{3,7},{4,0},{5,1},{6,2},{7,3},{8,12},{9,13},{10,... | collective-permute-start | bytes 442376 | tf_op jit(solution)/shard_map/expert_z2/ppermute | solution.py:292
  37.4 12.2 %collective-permute-start.12 = (f16[2,192,512]{2,1,0:T(8,128)(2,1)}, f16[2,192,512]{2,1,0:T(8,128)(2,1)}, u32[]{:S(2)}, u32[]{:S(2)}) collective-permute-start(f16[2,192,512]{2,1,0:T(8,128)(2,1)} %add_convert_fusion.1), channel_id=1, source_target_pairs={{0,1},{1,0},{2,3},{3,2},{4,5},{5,4},{6,7},{7,6},{8,9},{9,8},{10,11... | collective-permute-start | bytes 1179656 | tf_op jit(solution)/shard_map/table_y/ppermute | solution.py:292
  45.2 16.8 %collective-permute-start.10 = (f16[384,768]{1,0:T(8,128)(2,1)}, f16[384,768]{1,0:T(8,128)(2,1)}, u32[]{:S(2)}, u32[]{:S(2)}) collective-permute-start(f16[384,768]{1,0:T(8,128)(2,1)} %copy.24), channel_id=1, source_target_pairs={{0,16},{1,17},{2,18},{3,19},{4,20},{5,21},{6,22},{7,23},{8,24},{9,... | collective-permute-start | bytes 1769480 | tf_op jit(solution)/shard_map/expert_gather_x/ppermute | solution.py:292
  46.7 15.3 %collective-permute-start.9 = (f16[384,768]{1,0:T(8,128)(2,1)}, f16[384,768]{1,0:T(8,128)(2,1)}, u32[]{:S(2)}, u32[]{:S(2)}) collective-permute-start(f16[384,768]{1,0:T(8,128)(2,1)} %copy.24), channel_id=1, source_target_pairs={{0,1},{1,0},{2,3},{3,2},{4,5},{5,4},{6,7},{7,6},{8,9},{9,8},{10,11... | collective-permute-start | bytes 1769480 | tf_op jit(solution)/shard_map/expert_gather_y/ppermute | solution.py:292
  52.0 26.1 %collective-permute-start.18 = (f16[192,512]{1,0:T(8,128)(2,1)}, f16[192,512]{1,0:T(8,128)(2,1)}, u32[]{:S(2)}, u32[]{:S(2)}) collective-permute-start(f16[192,512]{1,0:T(8,128)(2,1)} %get-tuple-element.241), channel_id=1, source_target_pairs={{0,6},{1,7},{2,4},{3,5},{4,2},{5,3},{6,0},{7,1},{8,14},{9,15},{10,... | collective-permute-start | bytes 589832 | tf_op jit(solution)/shard_map/table_z3/ppermute | solution.py:292
  56.4 19.7 %collective-permute-start.16 = (f16[192,512]{1,0:T(8,128)(2,1)}, f16[192,512]{1,0:T(8,128)(2,1)S(1)}, u32[]{:S(2)}, u32[]{:S(2)}) collective-permute-start(f16[192,512]{1,0:T(8,128)(2,1)} %get-tuple-element.239), channel_id=1, source_target_pairs={{0,2},{1,3},{2,0},{3,1},{4,6},{5,7},{6,4},{7,5},{8,10},{9,11},{10,... | collective-permute-start | bytes 589832 | tf_op jit(solution)/shard_map/table_z1/ppermute | solution.py:292
  56.7 21.3 %collective-permute-start.17 = (f16[192,512]{1,0:T(8,128)(2,1)}, f16[192,512]{1,0:T(8,128)(2,1)S(1)}, u32[]{:S(2)}, u32[]{:S(2)}) collective-permute-start(f16[192,512]{1,0:T(8,128)(2,1)} %get-tuple-element.238), channel_id=1, source_target_pairs={{0,4},{1,5},{2,6},{3,7},{4,0},{5,1},{6,2},{7,3},{8,12},{9,13},{10,... | collective-permute-start | bytes 589832 | tf_op jit(solution)/shard_map/table_z2/ppermute | solution.py:292
  57.4 25.2 %all-to-all-start = ((bf16[4,192,384]{2,1,0:T(8,128)(2,1)}), bf16[4,192,384]{2,1,0:T(8,128)(2,1)S(1)}, u32[]{:S(2)}, u32[]{:S(2)}) async-start(bf16[4,192,384]{2,1,0:T(8,128)(2,1)} %subtract_convert_fusion.1), calls=%async_computation | async-start | bytes 1179648 | tf_op jit(solution)/shard_map/expert_back_z/all_to_all | solution.py:305
  62.0 11.4 %collective-permute-start.13 = (f16[384,768]{1,0:T(8,128)(2,1)}, f16[384,768]{1,0:T(8,128)(2,1)S(1)}, u32[]{:S(2)}, u32[]{:S(2)}) collective-permute-start(f16[384,768]{1,0:T(8,128)(2,1)} %collective-permute-done.10), channel_id=1, source_target_pairs={{0,1},{1,0},{2,3},{3,2},{4,5},{5,4},{6,7},{7,6},{8,9},{9,8},{10,11... | collective-permute-start | bytes 1769480 | tf_op jit(solution)/shard_map/expert_gather2_y/ppermute | solution.py:292
  67.4 22.5 %collective-permute-start.15 = (f32[2,384,768]{2,1,0:T(8,128)}, f32[2,384,768]{2,1,0:T(8,128)}, u32[]{:S(2)}, u32[]{:S(2)}) collective-permute-start(f32[2,384,768]{2,1,0:T(8,128)} %maximum_convert_fusion.2.refs_0_), channel_id=1, source_target_pairs={{0,8},{1,9},{2,10},{3,11},{4,12},{5,13},{6,14},{7,15},{8,0},{9,1},... | collective-permute-start | bytes 7077896 | tf_op jit(solution)/shard_map/expert_gather_core/ppermute | solution.py:292
  76.0 25.7 %collective-permute-start.14 = (f32[2,384,768]{2,1,0:T(8,128)}, f32[2,384,768]{2,1,0:T(8,128)}, u32[]{:S(2)}, u32[]{:S(2)}) collective-permute-start(f32[2,384,768]{2,1,0:T(8,128)} %maximum_convert_fusion.3.refs_0_), channel_id=1, source_target_pairs={{0,8},{1,9},{2,10},{3,11},{4,12},{5,13},{6,14},{7,15},{8,0},{9,1},... | collective-permute-start | bytes 7077896 | tf_op jit(solution)/shard_map/expert_gather2_core/ppermute | solution.py:292
  80.9 26.1 %collective-permute-start.21 = (f16[512,768]{1,0:T(8,128)(2,1)}, f16[512,768]{1,0:T(8,128)(2,1)}, u32[]{:S(2)}, u32[]{:S(2)}) collective-permute-start(f16[512,768]{1,0:T(8,128)(2,1)} %copy.25), channel_id=1, source_target_pairs={{0,16},{1,17},{2,18},{3,19},{4,20},{5,21},{6,22},{7,23},{8,24},{9,... | collective-permute-start | bytes 2359304 | tf_op jit(solution)/shard_map/table_gather_x/ppermute | solution.py:292
  81.8 25.2 %collective-permute-start.20 = (f16[512,768]{1,0:T(8,128)(2,1)}, f16[512,768]{1,0:T(8,128)(2,1)}, u32[]{:S(2)}, u32[]{:S(2)}) collective-permute-start(f16[512,768]{1,0:T(8,128)(2,1)} %copy.25), channel_id=1, source_target_pairs={{0,1},{1,0},{2,3},{3,2},{4,5},{5,4},{6,7},{7,6},{8,9},{9,8},{10,11... | collective-permute-start | bytes 2359304 | tf_op jit(solution)/shard_map/table_gather_y/ppermute | solution.py:292
  83.4 23.6 %collective-permute-start.19 = (bf16[2,192,384]{2,1,0:T(8,128)(2,1)}, bf16[2,192,384]{2,1,0:T(8,128)(2,1)S(1)}, u32[]{:S(2)}, u32[]{:S(2)}) collective-permute-start(bf16[2,192,384]{2,1,0:T(8,128)(2,1)} %get-tuple-element.243), channel_id=1, source_target_pairs={{0,1},{1,0},{2,3},{3,2},{4,5},{5,4},{6,7},{7,6},{8,9},{9,8},{10,11... | collective-permute-start | bytes 884744 | tf_op jit(solution)/shard_map/expert_back_y/ppermute | solution.py:292
  85.8 23.4 %all-to-all-start.1 = ((bf16[4,192,512]{2,1,0:T(8,128)(2,1)}), bf16[4,192,512]{2,1,0:T(8,128)(2,1)S(1)}, u32[]{:S(2)}, u32[]{:S(2)}) async-start(bf16[4,192,512]{2,1,0:T(8,128)(2,1)} %subtract_convert_fusion), calls=%async_computation.1 | async-start | bytes 1572864 | tf_op jit(solution)/shard_map/table_back_z/all_to_all | solution.py:305
  89.9 17.1 %collective-permute-start.22 = (bf16[2,192,384]{2,1,0:T(8,128)(2,1)S(1)}, bf16[2,192,384]{2,1,0:T(8,128)(2,1)S(1)}, u32[]{:S(2)}, u32[]{:S(2)}) collective-permute-start(bf16[2,192,384]{2,1,0:T(8,128)(2,1)S(1)} %get-tuple-element.210.refs_0_), channel_id=1, source_target_pairs={{0,16},{1,17},{2,18},{3,19},{4,20},{5,21},{6,22},{7,23},{8,24},{9,... | collective-permute-start | bytes 884744 | tf_op jit(solution)/shard_map/expert_back_x/ppermute | solution.py:292
  111.0 20.2 %collective-permute-start.24 = (bf16[2,192,384]{2,1,0:T(8,128)(2,1)S(1)}, bf16[2,192,384]{2,1,0:T(8,128)(2,1)S(1)}, u32[]{:S(2)}, u32[]{:S(2)}) collective-permute-start(bf16[2,192,384]{2,1,0:T(8,128)(2,1)S(1)} %get-tuple-element.210.refs_0_), channel_id=1, source_target_pairs={{0,8},{1,9},{2,10},{3,11},{4,12},{5,13},{6,14},{7,15},{8,0},{9,1},... | collective-permute-start | bytes 884744 | tf_op jit(solution)/shard_map/expert_back_core/ppermute | solution.py:292
  111.4 19.7 %collective-permute-start.27 = (f16[512,768]{1,0:T(8,128)(2,1)}, f16[512,768]{1,0:T(8,128)(2,1)S(1)}, u32[]{:S(2)}, u32[]{:S(2)}) collective-permute-start(f16[512,768]{1,0:T(8,128)(2,1)} %collective-permute-done.21), channel_id=1, source_target_pairs={{0,1},{1,0},{2,3},{3,2},{4,5},{5,4},{6,7},{7,6},{8,9},{9,8},{10,11... | collective-permute-start | bytes 2359304 | tf_op jit(solution)/shard_map/table_gather2_y/ppermute | solution.py:292
  113.0 18.2 %collective-permute-start.25 = (bf16[2,192,384]{2,1,0:T(8,128)(2,1)S(1)}, bf16[2,192,384]{2,1,0:T(8,128)(2,1)S(1)}, u32[]{:S(2)}, u32[]{:S(2)}) collective-permute-start(bf16[2,192,384]{2,1,0:T(8,128)(2,1)S(1)} %collective-permute-done.19.refs_1_), channel_id=1, source_target_pairs={{0,8},{1,9},{2,10},{3,11},{4,12},{5,13},{6,14},{7,15},{8,0},{9,1},... | collective-permute-start | bytes 884744 | tf_op jit(solution)/shard_map/expert_back_core/ppermute | solution.py:292
  113.0 18.2 %collective-permute-start.23 = (bf16[2,192,384]{2,1,0:T(8,128)(2,1)S(1)}, bf16[2,192,384]{2,1,0:T(8,128)(2,1)S(1)}, u32[]{:S(2)}, u32[]{:S(2)}) collective-permute-start(bf16[2,192,384]{2,1,0:T(8,128)(2,1)S(1)} %collective-permute-done.19.refs_1_), channel_id=1, source_target_pairs={{0,16},{1,17},{2,18},{3,19},{4,20},{5,21},{6,22},{7,23},{8,24},{9,... | collective-permute-start | bytes 884744 | tf_op jit(solution)/shard_map/expert_back2_x/ppermute | solution.py:292
  120.0 11.2 %collective-permute-start.26 = (bf16[2,192,384]{2,1,0:T(8,128)(2,1)S(1)}, bf16[2,192,384]{2,1,0:T(8,128)(2,1)S(1)}, u32[]{:S(2)}, u32[]{:S(2)}) collective-permute-start(bf16[2,192,384]{2,1,0:T(8,128)(2,1)S(1)} %collective-permute-done.22.refs_2_), channel_id=1, source_target_pairs={{0,8},{1,9},{2,10},{3,11},{4,12},{5,13},{6,14},{7,15},{8,0},{9,1},... | collective-permute-start | bytes 884744 | tf_op jit(solution)/shard_map/expert_back_core/ppermute | solution.py:292
  132.9 13.8 %collective-permute-start.30 = (f32[2,512,768]{2,1,0:T(8,128)S(1)}, f32[2,512,768]{2,1,0:T(8,128)}, u32[]{:S(2)}, u32[]{:S(2)}) collective-permute-start(f32[2,512,768]{2,1,0:T(8,128)S(1)} %maximum_convert_fusion.1.refs_0_), channel_id=1, source_target_pairs={{0,8},{1,9},{2,10},{3,11},{4,12},{5,13},{6,14},{7,15},{8,0},{9,1},... | collective-permute-start | bytes 9437192 | tf_op jit(solution)/shard_map/table_gather2_core/ppermute | solution.py:292
  133.0 13.1 %collective-permute-start.31 = (bf16[2,192,512]{2,1,0:T(8,128)(2,1)S(1)}, bf16[2,192,512]{2,1,0:T(8,128)(2,1)S(1)}, u32[]{:S(2)}, u32[]{:S(2)}) collective-permute-start(bf16[2,192,512]{2,1,0:T(8,128)(2,1)S(1)} %get-tuple-element.233), channel_id=1, source_target_pairs={{0,1},{1,0},{2,3},{3,2},{4,5},{5,4},{6,7},{7,6},{8,9},{9,8},{10,11... | collective-permute-start | bytes 1179656 | tf_op jit(solution)/shard_map/table_back_y/ppermute | solution.py:292
  134.6 18.8 %collective-permute-start.29 = (bf16[2,192,384]{2,1,0:T(8,128)(2,1)S(1)}, bf16[2,192,384]{2,1,0:T(8,128)(2,1)S(1)}, u32[]{:S(2)}, u32[]{:S(2)}) collective-permute-start(bf16[2,192,384]{2,1,0:T(8,128)(2,1)S(1)} %collective-permute-done.23.refs_3_), channel_id=1, source_target_pairs={{0,8},{1,9},{2,10},{3,11},{4,12},{5,13},{6,14},{7,15},{8,0},{9,1},... | collective-permute-start | bytes 884744 | tf_op jit(solution)/shard_map/expert_back2_core/ppermute | solution.py:292
  134.8 11.3 %collective-permute-start.32 = (bf16[2,192,512]{2,1,0:T(8,128)(2,1)S(1)}, bf16[2,192,512]{2,1,0:T(8,128)(2,1)S(1)}, u32[]{:S(2)}, u32[]{:S(2)}) collective-permute-start(bf16[2,192,512]{2,1,0:T(8,128)(2,1)S(1)} %get-tuple-element.224.refs_0_), channel_id=1, source_target_pairs={{0,16},{1,17},{2,18},{3,19},{4,20},{5,21},{6,22},{7,23},{8,24},{9,... | collective-permute-start | bytes 1179656 | tf_op jit(solution)/shard_map/table_back_x/ppermute | solution.py:292
  135.3 21.9 %collective-permute-start.34 = (bf16[2,192,512]{2,1,0:T(8,128)(2,1)S(1)}, bf16[2,192,512]{2,1,0:T(8,128)(2,1)S(1)}, u32[]{:S(2)}, u32[]{:S(2)}) collective-permute-start(bf16[2,192,512]{2,1,0:T(8,128)(2,1)S(1)} %get-tuple-element.224.refs_0_), channel_id=1, source_target_pairs={{0,8},{1,9},{2,10},{3,11},{4,12},{5,13},{6,14},{7,15},{8,0},{9,1},... | collective-permute-start | bytes 1179656 | tf_op jit(solution)/shard_map/table_back_core/ppermute | solution.py:292
  146.1 11.1 %collective-permute-start.35 = (bf16[2,192,512]{2,1,0:T(8,128)(2,1)S(1)}, bf16[2,192,512]{2,1,0:T(8,128)(2,1)S(1)}, u32[]{:S(2)}, u32[]{:S(2)}) collective-permute-start(bf16[2,192,512]{2,1,0:T(8,128)(2,1)S(1)} %collective-permute-done.31.refs_1_), channel_id=1, source_target_pairs={{0,8},{1,9},{2,10},{3,11},{4,12},{5,13},{6,14},{7,15},{8,0},{9,1},... | collective-permute-start | bytes 1179656 | tf_op jit(solution)/shard_map/table_back_core/ppermute | solution.py:292
  146.1 11.5 %collective-permute-start.33 = (bf16[2,192,512]{2,1,0:T(8,128)(2,1)S(1)}, bf16[2,192,512]{2,1,0:T(8,128)(2,1)S(1)}, u32[]{:S(2)}, u32[]{:S(2)}) collective-permute-start(bf16[2,192,512]{2,1,0:T(8,128)(2,1)S(1)} %collective-permute-done.31.refs_1_), channel_id=1, source_target_pairs={{0,16},{1,17},{2,18},{3,19},{4,20},{5,21},{6,22},{7,23},{8,24},{9,... | collective-permute-start | bytes 1179656 | tf_op jit(solution)/shard_map/table_back2_x/ppermute | solution.py:292
  (17 other events, 84.4 us)

commit v6 on v5

--- a/solution.py
+++ b/solution.py
@@ -485,8 +485,8 @@
     e.wait("far2")
     e.gather_y()
     t.gather()
+    t.low_part()
     e.copies_y()
-    t.low_part()
     t.copies_z()
     e.update("pair_core")
     e.update("far_pair")
@@ -503,9 +503,9 @@
     t.wait("far2")
     e.wait_core()
     e.wait("low_far_x")
+    t.copies_y()
     t.gather_y()
     e.copies_core()
-    t.copies_y()
     t.update("far_pair")
     t.wait("low_near_x")
     t.wait("low_far")

time: 164 us -> 164 us (level)
  transfers between devices with their start and end apart: 40 -> 40, of which waited for: 13 -> 12; matrix products, arithmetic and copies ran while one was open for 12% -> 11% of each run, Pallas kernels for 41% -> 41%
where the time goes in v6:
time: 164 us; the launch traced here: 163 us
  Pallas kernels  71.1 us (43%)
  starting transfers between devices  44.8 us (27%)
  waiting for transfers between devices  21.5 us (13%)
  other arithmetic  18.6 us (11%)
  local copies, waits for them, and re-layouts  6.33 us (4%)
    pallas_call x15, Pallas kernels, call(): pl.pallas_call(kernel, grid_spec=grid_spec, out_shape=[jax.ShapeDtypeStru...  71.1 us
    ppermute x38, starting transfers between devices, send(): return lax.ppermute(value, axes, pairs(sizes, move))  36.4 us
    ppermute x38, waiting for transfers between devices, send(): return lax.ppermute(value, axes, pairs(sizes, move))  19.3 us
    all_to_all x2, starting transfers between devices, over_z(): lax.all_to_all(value, 'shard', split_axis=0, concat_axis=0, tiled=True)  8.41 us
    convert_element_type x2, other arithmetic, gather_y(): self.far_pair = mark(jnp.stack([far, far2]).astype(jnp.float32))  4.21 us
    convert_element_type x2, other arithmetic, gather_x(): self.pair = mark(jnp.stack([self.own, near]).astype(jnp.float32))  4.18 us
  transfers between devices with their start and end apart: 40, of which 12 were waited for; matrix products, arithmetic and copies ran while one was open for 11% of the time, Pallas kernels for 41%

profile of v6, /device:TPU:0, one launch (start us, length us, event | category | flops | bytes accessed | tf_op | source)
XLA Modules:
  0.0 163.3 jit_solution(6607218541046631173)
XLA Ops:
  0.7 1.8 %dynamic-slice_bitcast_fusion = f32[2,192,1536]{2,1,0:T(8,128)S(1)} fusion(f32[2,2,192,1536]{3,2,1,0:T(8,128)} %bitcast.72, s32[]{:T(128)S(6)} %select_n.243), kind=kLoop, calls=%fused_computation | loop fusion | bytes 4718596 | tf_op jit(solution)/shard_map/jit(dynamic_index_in_dim)/squeeze | solution.py:308
  3.1 3.7 %pick.1 = f32[2,192,2048]{2,1,0:T(8,128)} custom-call(s32[3]{0:T(128)S(1)} %pad_add_fusion.4.here, f32[192,8192]{1,0:T(8,128)} %bitcast.97), custom_call_target="tpu_custom_call" | custom-call | flops 20000000000 | bytes 1000000 | tf_op jit(solution)/shard_map/pick/pallas_call | solution.py:76
  7.3 3.7 %add_split.2 = (f32[2,192,384]{2,1,0:T(8,128)S(1)}, f32[2,192,384]{2,1,0:T(8,128)S(1)}, f32[2,192,384]{2,1,0:T(8,128)S(1)}, f32[2,192,384]{2,1,0:T(8,128)}) custom-call(s32[3]{0:T(128)S(1)} %pad_add_fusion.5.here, f32[2,2,192,1536]{3,2,1,0:T(8,128)} %bitcast.73, f32[2,2,192,1536]{3,2,1,0:T(8,128)} %bitcast.74, ...), custom_call_target="tpu_custom_call" | custom-call | flops 20000000000 | bytes 1000000 | tf_op jit(solution)/shard_map/add_split/pallas_call | solution.py:76
  11.1 2.9 %collective-permute-start.3 = (f16[2,192,384]{2,1,0:T(8,128)(2,1)S(1)}, f16[2,192,384]{2,1,0:T(8,128)(2,1)S(1)}, u32[]{:S(2)}, u32[]{:S(2)}) collective-permute-start(f16[2,192,384]{2,1,0:T(8,128)(2,1)S(1)} %multiply_convert_fusion.3), channel_id=1, source_target_pairs={{0,16},{1,17},{2,18},{3,19},{4,20},{5,21},{6,22},{7,23},{8,24},{9,... | collective-permute-start | bytes 884744 | tf_op jit(solution)/shard_map/expert_far_x/ppermute | solution.py:292
  14.2 4.4 %add_split.3 = (f32[2,192,512]{2,1,0:T(8,128)S(1)}, f32[2,192,512]{2,1,0:T(8,128)S(1)}, f32[2,192,512]{2,1,0:T(8,128)}, f32[2,192,512]{2,1,0:T(8,128)}) custom-call(s32[3]{0:T(128)S(1)} %pad_add_fusion.5.here, f32[192,8192]{1,0:T(8,128)} %bitcast.98, f32[192,8192]{1,0:T(8,128)} %bitcast.99, f32[2,192,2048]{2,1,0:T(8,128)} %collective-permute-done.2.got_sent.got_kept, ...), custom_call_target="tpu_custom_call" | custom-call | flops 20000000000 | bytes 1000000 | tf_op jit(solution)/shard_map/add_split/pallas_call | solution.py:76
  18.7 2.1 %collective-permute-start.8 = (f16[2,192,512]{2,1,0:T(8,128)(2,1)S(1)}, f16[2,192,512]{2,1,0:T(8,128)(2,1)S(1)}, u32[]{:S(2)}, u32[]{:S(2)}) collective-permute-start(f16[2,192,512]{2,1,0:T(8,128)(2,1)S(1)} %multiply_convert_fusion.1), channel_id=1, source_target_pairs={{0,16},{1,17},{2,18},{3,19},{4,20},{5,21},{6,22},{7,23},{8,24},{9,... | collective-permute-start | bytes 1179656 | tf_op jit(solution)/shard_map/table_far_x/ppermute | solution.py:292
  21.9 2.1 %collective-permute-start.4 = (f16[2,192,384]{2,1,0:T(8,128)(2,1)S(1)}, f16[2,192,384]{2,1,0:T(8,128)(2,1)S(1)}, u32[]{:S(2)}, u32[]{:S(2)}) collective-permute-start(f16[2,192,384]{2,1,0:T(8,128)(2,1)S(1)} %add_convert_fusion.3), channel_id=1, source_target_pairs={{0,1},{1,0},{2,3},{3,2},{4,5},{5,4},{6,7},{7,6},{8,9},{9,8},{10,11... | collective-permute-start | bytes 884744 | tf_op jit(solution)/shard_map/expert_y/ppermute | solution.py:292
  26.3 2.5 %transposed_base.2 = f32[768,384]{1,0:T(8,128)S(1)} custom-call(s32[3]{0:T(128)S(1)} %pad_add_fusion.5.here, f32[2,2,2,384,768]{4,3,2,1,0:T(8,128)} %bitcast.87, f32[2,2,2,384,768]{4,3,2,1,0:T(8,128)} %bitcast.92), custom_call_target="tpu_custom_call" | custom-call | flops 20000000000 | bytes 1000000 | tf_op jit(solution)/shard_map/transposed_base/pallas_call | solution.py:76
  31.8 2.6 %collective-permute-start.6 = (f16[192,384]{1,0:T(8,128)(2,1)S(1)}, f16[192,384]{1,0:T(8,128)(2,1)S(1)}, u32[]{:S(2)}, u32[]{:S(2)}) collective-permute-start(f16[192,384]{1,0:T(8,128)(2,1)S(1)} %get-tuple-element.251), channel_id=1, source_target_pairs={{0,4},{1,5},{2,6},{3,7},{4,0},{5,1},{6,2},{7,3},{8,12},{9,13},{10,... | collective-permute-start | bytes 442376 | tf_op jit(solution)/shard_map/expert_z2/ppermute | solution.py:292
  34.7 1.9 %collective-permute-done.8 = f16[2,192,512]{2,1,0:T(8,128)(2,1)S(1)} collective-permute-done((f16[2,192,512]{2,1,0:T(8,128)(2,1)S(1)}, f16[2,192,512]{2,1,0:T(8,128)(2,1)S(1)}, u32[]{:S(2)}, u32[]{:S(2)}) %collective-permute-start.8) | collective-permute-done | bytes 393248 | tf_op jit(solution)/shard_map/table_far_x/ppermute | solution.py:292
  37.4 2.1 %collective-permute-start.12 = (f16[2,192,512]{2,1,0:T(8,128)(2,1)}, f16[2,192,512]{2,1,0:T(8,128)(2,1)}, u32[]{:S(2)}, u32[]{:S(2)}) collective-permute-start(f16[2,192,512]{2,1,0:T(8,128)(2,1)} %add_convert_fusion.1), channel_id=1, source_target_pairs={{0,1},{1,0},{2,3},{3,2},{4,5},{5,4},{6,7},{7,6},{8,9},{9,8},{10,11... | collective-permute-start | bytes 1179656 | tf_op jit(solution)/shard_map/table_y/ppermute | solution.py:292
  39.5 2.7 %transposed_base.3 = f32[768,512]{1,0:T(8,128)S(1)} custom-call(s32[3]{0:T(128)S(1)} %pad_add_fusion.5.here, f32[2,2,2,512,768]{4,3,2,1,0:T(8,128)} %bitcast.77, f32[2,2,2,512,768]{4,3,2,1,0:T(8,128)} %bitcast.82), custom_call_target="tpu_custom_call" | custom-call | flops 20000000000 | bytes 1000000 | tf_op jit(solution)/shard_map/transposed_base/pallas_call | solution.py:76
  49.6 2.4 %select_bitcast_fusion.4 = (f16[192,512]{1,0:T(8,128)(2,1)}, f16[192,512]{1,0:T(8,128)(2,1)}, f16[192,512]{1,0:T(8,128)(2,1)S(1)}, f16[192,512]{1,0:T(8,128)(2,1)}) fusion(f16[2,192,512]{2,1,0:T(8,128)(2,1)} %collective-permute-done.12, s32[]{:T(128)S(6)} %select_n.257, f16[2,192,512]{2,1,0:T(8,128)(2,1)S(1)} %add_convert_fusion, pred[]{:T(512)S(6)} %eq.28, ...), kind=kLoop, calls=%fused_computation.21 | loop fusion | flops 393216 | bytes 2359316 | tf_op jit(solution)/shard_map/jit(_where)/select_n | solution.py:379
  52.0 3.4 %collective-permute-start.18 = (f16[192,512]{1,0:T(8,128)(2,1)}, f16[192,512]{1,0:T(8,128)(2,1)}, u32[]{:S(2)}, u32[]{:S(2)}) collective-permute-start(f16[192,512]{1,0:T(8,128)(2,1)} %get-tuple-element.243), channel_id=1, source_target_pairs={{0,6},{1,7},{2,4},{3,5},{4,2},{5,3},{6,0},{7,1},{8,14},{9,15},{10,... | collective-permute-start | bytes 589832 | tf_op jit(solution)/shard_map/table_z3/ppermute | solution.py:292
  57.4 4.6 %all-to-all-start = ((bf16[4,192,384]{2,1,0:T(8,128)(2,1)}), bf16[4,192,384]{2,1,0:T(8,128)(2,1)}, u32[]{:S(2)}, u32[]{:S(2)}) async-start(bf16[4,192,384]{2,1,0:T(8,128)(2,1)} %subtract_convert_fusion.1), calls=%async_computation | async-start | bytes 1179648 | tf_op jit(solution)/shard_map/expert_back_z/all_to_all | solution.py:305
  62.0 2.5 %collective-permute-start.13 = (f16[384,768]{1,0:T(8,128)(2,1)}, f16[384,768]{1,0:T(8,128)(2,1)S(1)}, u32[]{:S(2)}, u32[]{:S(2)}) collective-permute-start(f16[384,768]{1,0:T(8,128)(2,1)} %collective-permute-done.10), channel_id=1, source_target_pairs={{0,1},{1,0},{2,3},{3,2},{4,5},{5,4},{6,7},{7,6},{8,9},{9,8},{10,11... | collective-permute-start | bytes 1769480 | tf_op jit(solution)/shard_map/expert_gather2_y/ppermute | solution.py:292
  64.6 2.8 %maximum_convert_fusion.2.refs_0_ = f32[2,384,768]{2,1,0:T(8,128)} fusion(f16[1,384,768]{2,1,0:T(8,128)(2,1)} %bitcast.25, f16[1,384,768]{2,1,0:T(8,128)(2,1)} %bitcast.71), kind=kLoop, calls=%fused_computation.4 | loop fusion | flops 1179648 | bytes 3538944 | tf_op jit(solution)/shard_map/convert_element_type | solution.py:407
  67.4 5.3 %update.8 = (f32[2,2,2,384,768]{4,3,2,1,0:T(8,128)}, f32[2,2,2,384,768]{4,3,2,1,0:T(8,128)}) custom-call(s32[3]{0:T(128)S(1)} %pad_add_fusion.5.here, f32[2,384,768]{2,1,0:T(8,128)} %maximum_convert_fusion.2.refs_0_, f32[2,2,2,384,768]{4,3,2,1,0:T(8,128)} %bitcast.88, f32[2,2,2,384,768]{4,3,2,1,0:T(8,128)} %bitcast.93), custom_call_target="tpu_custom_call" | custom-call | flops 20000000000 | bytes 1000000 | tf_op jit(solution)/shard_map/update/pallas_call | solution.py:76
  73.7 2.6 %maximum_convert_fusion.3.refs_0_ = f32[2,384,768]{2,1,0:T(8,128)} fusion(f16[1,384,768]{2,1,0:T(8,128)(2,1)S(1)} %bitcast.76, f16[1,384,768]{2,1,0:T(8,128)(2,1)} %bitcast.26), kind=kLoop, calls=%fused_computation.5 | loop fusion | flops 1179648 | bytes 3538944 | tf_op jit(solution)/shard_map/convert_element_type | solution.py:412
  85.5 3.8 %all-to-all-start.1 = ((bf16[4,192,512]{2,1,0:T(8,128)(2,1)}), bf16[4,192,512]{2,1,0:T(8,128)(2,1)S(1)}, u32[]{:S(2)}, u32[]{:S(2)}) async-start(bf16[4,192,512]{2,1,0:T(8,128)(2,1)} %subtract_convert_fusion), calls=%async_computation.1 | async-start | bytes 1572864 | tf_op jit(solution)/shard_map/table_back_z/all_to_all | solution.py:305
  90.8 5.3 %update.9 = (f32[2,2,2,384,768]{4,3,2,1,0:T(8,128)}, f32[2,2,2,384,768]{4,3,2,1,0:T(8,128)}) custom-call(s32[3]{0:T(128)S(1)} %pad_add_fusion.4.here, f32[2,384,768]{2,1,0:T(8,128)} %collective-permute-done.15.refs_0_, f32[2,2,2,384,768]{4,3,2,1,0:T(8,128)} %bitcast.89, ...), custom_call_target="tpu_custom_call", output_to_operand_aliasing={{0}: (4, {}), {1}: (5, {})} | custom-call | flops 20000000000 | bytes 1000000 | tf_op jit(solution)/shard_map/update/pallas_call | solution.py:76
  96.1 5.3 %update.10 = (f32[2,2,2,384,768]{4,3,2,1,0:T(8,128)}, f32[2,2,2,384,768]{4,3,2,1,0:T(8,128)}) custom-call(s32[3]{0:T(128)S(1)} %get-tuple-element.254.here, f32[2,384,768]{2,1,0:T(8,128)} %maximum_convert_fusion.3.refs_0_, f32[2,2,2,384,768]{4,3,2,1,0:T(8,128)} %bitcast.90, ...), custom_call_target="tpu_custom_call", output_to_operand_aliasing={{0}: (4, {}), {1}: (5, {})} | custom-call | flops 20000000000 | bytes 1000000 | tf_op jit(solution)/shard_map/update/pallas_call | solution.py:76
  101.5 5.3 %update.11 = (f32[2,2,2,384,768]{4,3,2,1,0:T(8,128)}, f32[2,2,2,384,768]{4,3,2,1,0:T(8,128)}) custom-call(s32[3]{0:T(128)S(1)} %get-tuple-element.255.here, f32[2,384,768]{2,1,0:T(8,128)} %collective-permute-done.14.refs_0_, f32[2,2,2,384,768]{4,3,2,1,0:T(8,128)} %bitcast.91, ...), custom_call_target="tpu_custom_call", output_to_operand_aliasing={{0}: (4, {}), {1}: (5, {})} | custom-call | flops 20000000000 | bytes 1000000 | tf_op jit(solution)/shard_map/update/pallas_call | solution.py:76
  106.8 2.2 %all-to-all-done.1 = bf16[4,192,512]{2,1,0:T(8,128)(2,1)S(1)} async-done(((bf16[4,192,512]{2,1,0:T(8,128)(2,1)}), bf16[4,192,512]{2,1,0:T(8,128)(2,1)S(1)}, u32[]{:S(2)}, u32[]{:S(2)}) %all-to-all-start.1) | async-done | bytes 786464 | tf_op jit(solution)/shard_map/table_back_z/all_to_all | solution.py:305
  113.0 6.4 %update.12 = (f32[2,2,2,512,768]{4,3,2,1,0:T(8,128)}, f32[2,2,2,512,768]{4,3,2,1,0:T(8,128)}) custom-call(s32[3]{0:T(128)S(1)} %pad_add_fusion.5.here, f32[2,512,768]{2,1,0:T(8,128)} %copy-done.1, f32[2,2,2,512,768]{4,3,2,1,0:T(8,128)} %bitcast.78, f32[2,2,2,512,768]{4,3,2,1,0:T(8,128)} %bitcast.83), custom_call_target="tpu_custom_call" | custom-call | flops 20000000000 | bytes 1000000 | tf_op jit(solution)/shard_map/update/pallas_call | solution.py:76
  119.7 6.4 %update.13 = (f32[2,2,2,512,768]{4,3,2,1,0:T(8,128)}, f32[2,2,2,512,768]{4,3,2,1,0:T(8,128)}) custom-call(s32[3]{0:T(128)S(1)} %pad_add_fusion.4.here, f32[2,512,768]{2,1,0:T(8,128)} %collective-permute-done.28.refs_0_, f32[2,2,2,512,768]{4,3,2,1,0:T(8,128)} %bitcast.79, ...), custom_call_target="tpu_custom_call", output_to_operand_aliasing={{0}: (4, {}), {1}: (5, {})} | custom-call | flops 20000000000 | bytes 1000000 | tf_op jit(solution)/shard_map/update/pallas_call | solution.py:76
  126.2 4.5 %collective-permute-done.27 = f16[512,768]{1,0:T(8,128)(2,1)S(1)} collective-permute-done((f16[512,768]{1,0:T(8,128)(2,1)}, f16[512,768]{1,0:T(8,128)(2,1)S(1)}, u32[]{:S(2)}, u32[]{:S(2)}) %collective-permute-start.27) | collective-permute-done | bytes 786464 | tf_op jit(solution)/shard_map/table_gather2_y/ppermute | solution.py:292
  134.8 6.4 %update.14 = (f32[2,2,2,512,768]{4,3,2,1,0:T(8,128)}, f32[2,2,2,512,768]{4,3,2,1,0:T(8,128)}) custom-call(s32[3]{0:T(128)S(1)} %get-tuple-element.254.here, f32[2,512,768]{2,1,0:T(8,128)} %copy-done, f32[2,2,2,512,768]{4,3,2,1,0:T(8,128)} %bitcast.80, f32[2,2,2,512,768]{4,3,2,1,0:T(8,128)} %bitcast.85, ...), custom_call_target="tpu_custom_call", output_to_operand_aliasing={{0}: (4, {}), {1}: (5, {})} | custom-call | flops 20000000000 | bytes 1000000 | tf_op jit(solution)/shard_map/update/pallas_call | solution.py:76
  141.3 4.3 %collective-permute-done.32.refs_2_ = bf16[2,192,512]{2,1,0:T(8,128)(2,1)S(1)} collective-permute-done((bf16[2,192,512]{2,1,0:T(8,128)(2,1)S(1)}, bf16[2,192,512]{2,1,0:T(8,128)(2,1)S(1)}, u32[]{:S(2)}, u32[]{:S(2)}) %collective-permute-start.32) | collective-permute-done | bytes 393248 | tf_op jit(solution)/shard_map/table_back_x/ppermute | solution.py:292
  146.3 6.4 %update.15 = (f32[2,2,2,512,768]{4,3,2,1,0:T(8,128)}, f32[2,2,2,512,768]{4,3,2,1,0:T(8,128)}) custom-call(s32[3]{0:T(128)S(1)} %get-tuple-element.255.here, f32[2,512,768]{2,1,0:T(8,128)} %collective-permute-done.30.refs_0_, f32[2,2,2,512,768]{4,3,2,1,0:T(8,128)} %bitcast.81, ...), custom_call_target="tpu_custom_call", output_to_operand_aliasing={{0}: (4, {}), {1}: (5, {})} | custom-call | flops 20000000000 | bytes 1000000 | tf_op jit(solution)/shard_map/update/pallas_call | solution.py:76
  153.5 3.2 %place.2 = bf16[2,2,192,1536]{3,2,1,0:T(8,128)(2,1)} custom-call(s32[3]{0:T(128)S(1)} %pad_add_fusion.5.here, bf16[2,192,384]{2,1,0:T(8,128)(2,1)S(1)} %get-tuple-element.212.refs_0_, bf16[2,192,384]{2,1,0:T(8,128)(2,1)S(1)} %collective-permute-done.19.refs_1_, bf16[2,192,384]{2,1,0:T(8,128)(2,1)S(1)} %collective-permute-done.22.refs_2_, ...), custom_call_target="tpu_custom_call" | custom-call | flops 20000000000 | bytes 1000000 | tf_op jit(solution)/shard_map/place/pallas_call | solution.py:76
  159.6 3.7 %place.3 = bf16[192,8192]{1,0:T(8,128)(2,1)} custom-call(s32[3]{0:T(128)S(1)} %pad_add_fusion.5.here, bf16[2,192,512]{2,1,0:T(8,128)(2,1)S(1)} %get-tuple-element.226.refs_0_, bf16[2,192,512]{2,1,0:T(8,128)(2,1)S(1)} %collective-permute-done.31.refs_1_, bf16[2,192,512]{2,1,0:T(8,128)(2,1)S(1)} %collective-permute-done.32.refs_2_, ...), custom_call_target="tpu_custom_call" | custom-call | flops 20000000000 | bytes 1000000 | tf_op jit(solution)/shard_map/place/pallas_call | solution.py:76
  (109 shorter events, 42.5 us)
Async XLA Ops:
  14.1 14.8 %collective-permute-start.1 = (f16[2,192,384]{2,1,0:T(8,128)(2,1)S(1)}, f16[2,192,384]{2,1,0:T(8,128)(2,1)S(1)}, u32[]{:S(2)}, u32[]{:S(2)}) collective-permute-start(f16[2,192,384]{2,1,0:T(8,128)(2,1)S(1)} %multiply_convert_fusion.2), channel_id=1, source_target_pairs={{0,16},{1,17},{2,18},{3,19},{4,20},{5,21},{6,22},{7,23},{8,24},{9,... | collective-permute-start | bytes 884744 | tf_op jit(solution)/shard_map/expert_near_x/ppermute | solution.py:292
  18.7 17.9 %collective-permute-start.8 = (f16[2,192,512]{2,1,0:T(8,128)(2,1)S(1)}, f16[2,192,512]{2,1,0:T(8,128)(2,1)S(1)}, u32[]{:S(2)}, u32[]{:S(2)}) collective-permute-start(f16[2,192,512]{2,1,0:T(8,128)(2,1)S(1)} %multiply_convert_fusion.1), channel_id=1, source_target_pairs={{0,16},{1,17},{2,18},{3,19},{4,20},{5,21},{6,22},{7,23},{8,24},{9,... | collective-permute-start | bytes 1179656 | tf_op jit(solution)/shard_map/table_far_x/ppermute | solution.py:292
  24.9 23.4 %collective-permute-start.11 = (f16[2,192,512]{2,1,0:T(8,128)(2,1)}, f16[2,192,512]{2,1,0:T(8,128)(2,1)}, u32[]{:S(2)}, u32[]{:S(2)}) collective-permute-start(f16[2,192,512]{2,1,0:T(8,128)(2,1)} %multiply_convert_fusion), channel_id=1, source_target_pairs={{0,16},{1,17},{2,18},{3,19},{4,20},{5,21},{6,22},{7,23},{8,24},{9,... | collective-permute-start | bytes 1179656 | tf_op jit(solution)/shard_map/table_near_x/ppermute | solution.py:292
  30.2 12.1 %collective-permute-start.5 = (f16[192,384]{1,0:T(8,128)(2,1)S(1)}, f16[192,384]{1,0:T(8,128)(2,1)S(1)}, u32[]{:S(2)}, u32[]{:S(2)}) collective-permute-start(f16[192,384]{1,0:T(8,128)(2,1)S(1)} %get-tuple-element.252), channel_id=1, source_target_pairs={{0,2},{1,3},{2,0},{3,1},{4,6},{5,7},{6,4},{7,5},{8,10},{9,11},{10,... | collective-permute-start | bytes 442376 | tf_op jit(solution)/shard_map/expert_z1/ppermute | solution.py:292
  31.8 11.9 %collective-permute-start.6 = (f16[192,384]{1,0:T(8,128)(2,1)S(1)}, f16[192,384]{1,0:T(8,128)(2,1)S(1)}, u32[]{:S(2)}, u32[]{:S(2)}) collective-permute-start(f16[192,384]{1,0:T(8,128)(2,1)S(1)} %get-tuple-element.251), channel_id=1, source_target_pairs={{0,4},{1,5},{2,6},{3,7},{4,0},{5,1},{6,2},{7,3},{8,12},{9,13},{10,... | collective-permute-start | bytes 442376 | tf_op jit(solution)/shard_map/expert_z2/ppermute | solution.py:292
  37.4 12.2 %collective-permute-start.12 = (f16[2,192,512]{2,1,0:T(8,128)(2,1)}, f16[2,192,512]{2,1,0:T(8,128)(2,1)}, u32[]{:S(2)}, u32[]{:S(2)}) collective-permute-start(f16[2,192,512]{2,1,0:T(8,128)(2,1)} %add_convert_fusion.1), channel_id=1, source_target_pairs={{0,1},{1,0},{2,3},{3,2},{4,5},{5,4},{6,7},{7,6},{8,9},{9,8},{10,11... | collective-permute-start | bytes 1179656 | tf_op jit(solution)/shard_map/table_y/ppermute | solution.py:292
  45.2 16.8 %collective-permute-start.10 = (f16[384,768]{1,0:T(8,128)(2,1)}, f16[384,768]{1,0:T(8,128)(2,1)}, u32[]{:S(2)}, u32[]{:S(2)}) collective-permute-start(f16[384,768]{1,0:T(8,128)(2,1)} %copy.24), channel_id=1, source_target_pairs={{0,16},{1,17},{2,18},{3,19},{4,20},{5,21},{6,22},{7,23},{8,24},{9,... | collective-permute-start | bytes 1769480 | tf_op jit(solution)/shard_map/expert_gather_x/ppermute | solution.py:292
  46.7 15.3 %collective-permute-start.9 = (f16[384,768]{1,0:T(8,128)(2,1)}, f16[384,768]{1,0:T(8,128)(2,1)}, u32[]{:S(2)}, u32[]{:S(2)}) collective-permute-start(f16[384,768]{1,0:T(8,128)(2,1)} %copy.24), channel_id=1, source_target_pairs={{0,1},{1,0},{2,3},{3,2},{4,5},{5,4},{6,7},{7,6},{8,9},{9,8},{10,11... | collective-permute-start | bytes 1769480 | tf_op jit(solution)/shard_map/expert_gather_y/ppermute | solution.py:292
  52.0 26.1 %collective-permute-start.18 = (f16[192,512]{1,0:T(8,128)(2,1)}, f16[192,512]{1,0:T(8,128)(2,1)}, u32[]{:S(2)}, u32[]{:S(2)}) collective-permute-start(f16[192,512]{1,0:T(8,128)(2,1)} %get-tuple-element.243), channel_id=1, source_target_pairs={{0,6},{1,7},{2,4},{3,5},{4,2},{5,3},{6,0},{7,1},{8,14},{9,15},{10,... | collective-permute-start | bytes 589832 | tf_op jit(solution)/shard_map/table_z3/ppermute | solution.py:292
  56.4 20.0 %collective-permute-start.16 = (f16[192,512]{1,0:T(8,128)(2,1)}, f16[192,512]{1,0:T(8,128)(2,1)S(1)}, u32[]{:S(2)}, u32[]{:S(2)}) collective-permute-start(f16[192,512]{1,0:T(8,128)(2,1)} %get-tuple-element.241), channel_id=1, source_target_pairs={{0,2},{1,3},{2,0},{3,1},{4,6},{5,7},{6,4},{7,5},{8,10},{9,11},{10,... | collective-permute-start | bytes 589832 | tf_op jit(solution)/shard_map/table_z1/ppermute | solution.py:292
  56.7 21.3 %collective-permute-start.17 = (f16[192,512]{1,0:T(8,128)(2,1)}, f16[192,512]{1,0:T(8,128)(2,1)S(1)}, u32[]{:S(2)}, u32[]{:S(2)}) collective-permute-start(f16[192,512]{1,0:T(8,128)(2,1)} %get-tuple-element.240), channel_id=1, source_target_pairs={{0,4},{1,5},{2,6},{3,7},{4,0},{5,1},{6,2},{7,3},{8,12},{9,13},{10,... | collective-permute-start | bytes 589832 | tf_op jit(solution)/shard_map/table_z2/ppermute | solution.py:292
  57.4 25.6 %all-to-all-start = ((bf16[4,192,384]{2,1,0:T(8,128)(2,1)}), bf16[4,192,384]{2,1,0:T(8,128)(2,1)}, u32[]{:S(2)}, u32[]{:S(2)}) async-start(bf16[4,192,384]{2,1,0:T(8,128)(2,1)} %subtract_convert_fusion.1), calls=%async_computation | async-start | bytes 1179648 | tf_op jit(solution)/shard_map/expert_back_z/all_to_all | solution.py:305
  62.0 11.7 %collective-permute-start.13 = (f16[384,768]{1,0:T(8,128)(2,1)}, f16[384,768]{1,0:T(8,128)(2,1)S(1)}, u32[]{:S(2)}, u32[]{:S(2)}) collective-permute-start(f16[384,768]{1,0:T(8,128)(2,1)} %collective-permute-done.10), channel_id=1, source_target_pairs={{0,1},{1,0},{2,3},{3,2},{4,5},{5,4},{6,7},{7,6},{8,9},{9,8},{10,11... | collective-permute-start | bytes 1769480 | tf_op jit(solution)/shard_map/expert_gather2_y/ppermute | solution.py:292
  67.4 21.9 %collective-permute-start.15 = (f32[2,384,768]{2,1,0:T(8,128)}, f32[2,384,768]{2,1,0:T(8,128)}, u32[]{:S(2)}, u32[]{:S(2)}) collective-permute-start(f32[2,384,768]{2,1,0:T(8,128)} %maximum_convert_fusion.2.refs_0_), channel_id=1, source_target_pairs={{0,8},{1,9},{2,10},{3,11},{4,12},{5,13},{6,14},{7,15},{8,0},{9,1},... | collective-permute-start | bytes 7077896 | tf_op jit(solution)/shard_map/expert_gather_core/ppermute | solution.py:292
  76.3 25.1 %collective-permute-start.14 = (f32[2,384,768]{2,1,0:T(8,128)}, f32[2,384,768]{2,1,0:T(8,128)}, u32[]{:S(2)}, u32[]{:S(2)}) collective-permute-start(f32[2,384,768]{2,1,0:T(8,128)} %maximum_convert_fusion.3.refs_0_), channel_id=1, source_target_pairs={{0,8},{1,9},{2,10},{3,11},{4,12},{5,13},{6,14},{7,15},{8,0},{9,1},... | collective-permute-start | bytes 7077896 | tf_op jit(solution)/shard_map/expert_gather2_core/ppermute | solution.py:292
  80.2 26.6 %collective-permute-start.21 = (f16[512,768]{1,0:T(8,128)(2,1)S(1)}, f16[512,768]{1,0:T(8,128)(2,1)}, u32[]{:S(2)}, u32[]{:S(2)}) collective-permute-start(f16[512,768]{1,0:T(8,128)(2,1)S(1)} %copy.25), channel_id=1, source_target_pairs={{0,16},{1,17},{2,18},{3,19},{4,20},{5,21},{6,22},{7,23},{8,24},{9,... | collective-permute-start | bytes 2359304 | tf_op jit(solution)/shard_map/table_gather_x/ppermute | solution.py:292
  81.1 25.6 %collective-permute-start.20 = (f16[512,768]{1,0:T(8,128)(2,1)S(1)}, f16[512,768]{1,0:T(8,128)(2,1)}, u32[]{:S(2)}, u32[]{:S(2)}) collective-permute-start(f16[512,768]{1,0:T(8,128)(2,1)S(1)} %copy.25), channel_id=1, source_target_pairs={{0,1},{1,0},{2,3},{3,2},{4,5},{5,4},{6,7},{7,6},{8,9},{9,8},{10,11... | collective-permute-start | bytes 2359304 | tf_op jit(solution)/shard_map/table_gather_y/ppermute | solution.py:292
  84.1 22.7 %collective-permute-start.19 = (bf16[2,192,384]{2,1,0:T(8,128)(2,1)S(1)}, bf16[2,192,384]{2,1,0:T(8,128)(2,1)S(1)}, u32[]{:S(2)}, u32[]{:S(2)}) collective-permute-start(bf16[2,192,384]{2,1,0:T(8,128)(2,1)S(1)} %get-tuple-element.245), channel_id=1, source_target_pairs={{0,1},{1,0},{2,3},{3,2},{4,5},{5,4},{6,7},{7,6},{8,9},{9,8},{10,11... | collective-permute-start | bytes 884744 | tf_op jit(solution)/shard_map/expert_back_y/ppermute | solution.py:292
  85.5 23.5 %all-to-all-start.1 = ((bf16[4,192,512]{2,1,0:T(8,128)(2,1)}), bf16[4,192,512]{2,1,0:T(8,128)(2,1)S(1)}, u32[]{:S(2)}, u32[]{:S(2)}) async-start(bf16[4,192,512]{2,1,0:T(8,128)(2,1)} %subtract_convert_fusion), calls=%async_computation.1 | async-start | bytes 1572864 | tf_op jit(solution)/shard_map/table_back_z/all_to_all | solution.py:305
  89.3 17.5 %collective-permute-start.22 = (bf16[2,192,384]{2,1,0:T(8,128)(2,1)S(1)}, bf16[2,192,384]{2,1,0:T(8,128)(2,1)S(1)}, u32[]{:S(2)}, u32[]{:S(2)}) collective-permute-start(bf16[2,192,384]{2,1,0:T(8,128)(2,1)S(1)} %get-tuple-element.212.refs_0_), channel_id=1, source_target_pairs={{0,16},{1,17},{2,18},{3,19},{4,20},{5,21},{6,22},{7,23},{8,24},{9,... | collective-permute-start | bytes 884744 | tf_op jit(solution)/shard_map/expert_back_x/ppermute | solution.py:292
  110.5 20.2 %collective-permute-start.24 = (bf16[2,192,384]{2,1,0:T(8,128)(2,1)S(1)}, bf16[2,192,384]{2,1,0:T(8,128)(2,1)S(1)}, u32[]{:S(2)}, u32[]{:S(2)}) collective-permute-start(bf16[2,192,384]{2,1,0:T(8,128)(2,1)S(1)} %get-tuple-element.212.refs_0_), channel_id=1, source_target_pairs={{0,8},{1,9},{2,10},{3,11},{4,12},{5,13},{6,14},{7,15},{8,0},{9,1},... | collective-permute-start | bytes 884744 | tf_op jit(solution)/shard_map/expert_back_core/ppermute | solution.py:292
  111.0 19.7 %collective-permute-start.27 = (f16[512,768]{1,0:T(8,128)(2,1)}, f16[512,768]{1,0:T(8,128)(2,1)S(1)}, u32[]{:S(2)}, u32[]{:S(2)}) collective-permute-start(f16[512,768]{1,0:T(8,128)(2,1)} %collective-permute-done.21), channel_id=1, source_target_pairs={{0,1},{1,0},{2,3},{3,2},{4,5},{5,4},{6,7},{7,6},{8,9},{9,8},{10,11... | collective-permute-start | bytes 2359304 | tf_op jit(solution)/shard_map/table_gather2_y/ppermute | solution.py:292
  112.5 18.2 %collective-permute-start.25 = (bf16[2,192,384]{2,1,0:T(8,128)(2,1)S(1)}, bf16[2,192,384]{2,1,0:T(8,128)(2,1)S(1)}, u32[]{:S(2)}, u32[]{:S(2)}) collective-permute-start(bf16[2,192,384]{2,1,0:T(8,128)(2,1)S(1)} %collective-permute-done.19.refs_1_), channel_id=1, source_target_pairs={{0,8},{1,9},{2,10},{3,11},{4,12},{5,13},{6,14},{7,15},{8,0},{9,1},... | collective-permute-start | bytes 884744 | tf_op jit(solution)/shard_map/expert_back_core/ppermute | solution.py:292
  112.5 18.2 %collective-permute-start.23 = (bf16[2,192,384]{2,1,0:T(8,128)(2,1)S(1)}, bf16[2,192,384]{2,1,0:T(8,128)(2,1)S(1)}, u32[]{:S(2)}, u32[]{:S(2)}) collective-permute-start(bf16[2,192,384]{2,1,0:T(8,128)(2,1)S(1)} %collective-permute-done.19.refs_1_), channel_id=1, source_target_pairs={{0,16},{1,17},{2,18},{3,19},{4,20},{5,21},{6,22},{7,23},{8,24},{9,... | collective-permute-start | bytes 884744 | tf_op jit(solution)/shard_map/expert_back2_x/ppermute | solution.py:292
  119.5 11.2 %collective-permute-start.26 = (bf16[2,192,384]{2,1,0:T(8,128)(2,1)S(1)}, bf16[2,192,384]{2,1,0:T(8,128)(2,1)S(1)}, u32[]{:S(2)}, u32[]{:S(2)}) collective-permute-start(bf16[2,192,384]{2,1,0:T(8,128)(2,1)S(1)} %collective-permute-done.22.refs_2_), channel_id=1, source_target_pairs={{0,8},{1,9},{2,10},{3,11},{4,12},{5,13},{6,14},{7,15},{8,0},{9,1},... | collective-permute-start | bytes 884744 | tf_op jit(solution)/shard_map/expert_back_core/ppermute | solution.py:292
  132.4 13.7 %collective-permute-start.30 = (f32[2,512,768]{2,1,0:T(8,128)S(1)}, f32[2,512,768]{2,1,0:T(8,128)}, u32[]{:S(2)}, u32[]{:S(2)}) collective-permute-start(f32[2,512,768]{2,1,0:T(8,128)S(1)} %maximum_convert_fusion.1.refs_0_), channel_id=1, source_target_pairs={{0,8},{1,9},{2,10},{3,11},{4,12},{5,13},{6,14},{7,15},{8,0},{9,1},... | collective-permute-start | bytes 9437192 | tf_op jit(solution)/shard_map/table_gather2_core/ppermute | solution.py:292
  132.5 13.1 %collective-permute-start.31 = (bf16[2,192,512]{2,1,0:T(8,128)(2,1)S(1)}, bf16[2,192,512]{2,1,0:T(8,128)(2,1)S(1)}, u32[]{:S(2)}, u32[]{:S(2)}) collective-permute-start(bf16[2,192,512]{2,1,0:T(8,128)(2,1)S(1)} %get-tuple-element.235), channel_id=1, source_target_pairs={{0,1},{1,0},{2,3},{3,2},{4,5},{5,4},{6,7},{7,6},{8,9},{9,8},{10,11... | collective-permute-start | bytes 1179656 | tf_op jit(solution)/shard_map/table_back_y/ppermute | solution.py:292
  134.0 18.8 %collective-permute-start.29 = (bf16[2,192,384]{2,1,0:T(8,128)(2,1)S(1)}, bf16[2,192,384]{2,1,0:T(8,128)(2,1)S(1)}, u32[]{:S(2)}, u32[]{:S(2)}) collective-permute-start(bf16[2,192,384]{2,1,0:T(8,128)(2,1)S(1)} %collective-permute-done.23.refs_3_), channel_id=1, source_target_pairs={{0,8},{1,9},{2,10},{3,11},{4,12},{5,13},{6,14},{7,15},{8,0},{9,1},... | collective-permute-start | bytes 884744 | tf_op jit(solution)/shard_map/expert_back2_core/ppermute | solution.py:292
  134.2 11.4 %collective-permute-start.32 = (bf16[2,192,512]{2,1,0:T(8,128)(2,1)S(1)}, bf16[2,192,512]{2,1,0:T(8,128)(2,1)S(1)}, u32[]{:S(2)}, u32[]{:S(2)}) collective-permute-start(bf16[2,192,512]{2,1,0:T(8,128)(2,1)S(1)} %get-tuple-element.226.refs_0_), channel_id=1, source_target_pairs={{0,16},{1,17},{2,18},{3,19},{4,20},{5,21},{6,22},{7,23},{8,24},{9,... | collective-permute-start | bytes 1179656 | tf_op jit(solution)/shard_map/table_back_x/ppermute | solution.py:292
  134.7 22.0 %collective-permute-start.34 = (bf16[2,192,512]{2,1,0:T(8,128)(2,1)S(1)}, bf16[2,192,512]{2,1,0:T(8,128)(2,1)S(1)}, u32[]{:S(2)}, u32[]{:S(2)}) collective-permute-start(bf16[2,192,512]{2,1,0:T(8,128)(2,1)S(1)} %get-tuple-element.226.refs_0_), channel_id=1, source_target_pairs={{0,8},{1,9},{2,10},{3,11},{4,12},{5,13},{6,14},{7,15},{8,0},{9,1},... | collective-permute-start | bytes 1179656 | tf_op jit(solution)/shard_map/table_back_core/ppermute | solution.py:292
  145.6 11.1 %collective-permute-start.35 = (bf16[2,192,512]{2,1,0:T(8,128)(2,1)S(1)}, bf16[2,192,512]{2,1,0:T(8,128)(2,1)S(1)}, u32[]{:S(2)}, u32[]{:S(2)}) collective-permute-start(bf16[2,192,512]{2,1,0:T(8,128)(2,1)S(1)} %collective-permute-done.31.refs_1_), channel_id=1, source_target_pairs={{0,8},{1,9},{2,10},{3,11},{4,12},{5,13},{6,14},{7,15},{8,0},{9,1},... | collective-permute-start | bytes 1179656 | tf_op jit(solution)/shard_map/table_back_core/ppermute | solution.py:292
  145.6 11.5 %collective-permute-start.33 = (bf16[2,192,512]{2,1,0:T(8,128)(2,1)S(1)}, bf16[2,192,512]{2,1,0:T(8,128)(2,1)S(1)}, u32[]{:S(2)}, u32[]{:S(2)}) collective-permute-start(bf16[2,192,512]{2,1,0:T(8,128)(2,1)S(1)} %collective-permute-done.31.refs_1_), channel_id=1, source_target_pairs={{0,16},{1,17},{2,18},{3,19},{4,20},{5,21},{6,22},{7,23},{8,24},{9,... | collective-permute-start | bytes 1179656 | tf_op jit(solution)/shard_map/table_back2_x/ppermute | solution.py:292
  (17 other events, 84.4 us)
